TPU v7x, 32 devices: a whole 2x2x4 slice. The times are simulated.
32 devices in a mesh: row: 4 (over z), col: 2 (over x), layer: 4 (over y, core).
Axes of the slice: x: 2, y: 2, z: 4, core: 2. Of those that a mesh axis runs over, the one named last changes fastest.
Arguments:
- p_slabs: bfloat16 [4, 1024, 256], P('layer', 'row', 'col'), may hold values from -0.1875 to 0.1875
- p_mask: int32 [4, 32, 8], P('layer', 'row', 'col'), may hold values 0 or 1
- h_slabs: bfloat16 [4, 256, 1024], P('layer', 'row', 'col'), may hold values from -12 to 12
- h_mask: int32 [4, 8, 32], P('layer', 'row', 'col'), may hold values from 0 to 1, as said below
- gauss_row: int32 [32768], P(('row', 'col', 'layer')), may hold values from 0 to 255
- gauss_col: int32 [32768], P(('row', 'col', 'layer')), may hold values from 0 to 1023
- gauss_cell: int32 [32768], P(('row', 'col', 'layer')), may hold values from 0 to 32767
- gauss_expo: float32 [32768], P(('row', 'col', 'layer')), may hold values from 0.05 to 0.6
- gauss_pref: float32 [32768], P(('row', 'col', 'layer')), may hold values from -96 to 96
Outputs:
- product: bfloat16 [1024, 1024], P('row', ('col', 'layer'))
- density: float32 [64, 32, 512], P('row', 'col', 'layer')
Inputs may be any that keep to these rules, and one draw needn't show every extreme that they name: Each device's tile of h_mask (block rows l, r * 2 to r * 2 + 1, block columns c * 16 to c * 16 + 15) has at most 16 ones; some tile has exactly 16.
All inputs are finite; a program needn't handle non-finite values. No bound on the sum of `p_mask` on one device may be relied on, other than what follows from the above.
Results may differ from a plain program's by a relative error of at most 0.001.
Values may be sent and summed in bfloat16 or wider, within the bound.
No kernel may reach another device: no remote copies, remote signals or barrier semaphores. Data moves between devices by JAX's collectives and lax.ppermute only.
A program may use at most 64 MiB of HBM per device.

v0:
```python
import functools

import jax
import jax.numpy as jnp
from jax import lax
from jax.experimental import pallas as pl
from jax.experimental.pallas import tpu as pltpu
from jax.sharding import PartitionSpec as P

BS = 32
GX = 16
GY = 16
GZ = 128
R = 4
LANES = 128
F32 = jnp.float32
BF16 = jnp.bfloat16
HALO = R * GY
CORE = GX * GY
FULL = CORE + 2 * HALO
UNIT = 2 * LANES
PAIRS = 4
META = (PAIRS + 1) * 16
BASE = LANES + META
FLAG = 12
VMEM = pl.BlockSpec(memory_space=pltpu.VMEM)
SMEM = pl.BlockSpec(memory_space=pltpu.SMEM)
PARAMS = pltpu.CompilerParams(vmem_limit_bytes=40 * 1024 * 1024)
NT = (((1,), (1,)), ((), ()))
TN = (((0,), (0,)), ((), ()))


def iota(shape, axis):
    return lax.broadcasted_iota(jnp.int32, shape, axis).astype(F32)


def split3(value):
    first = value.astype(BF16).astype(F32)
    rest = value - first
    second = rest.astype(BF16).astype(F32)
    return first, second, rest - second


def masked(values, bits):
    lane = lax.broadcasted_iota(jnp.int32, values.shape, 1) // BS
    keep = jnp.zeros(values.shape, jnp.int32)
    for piece, bit in enumerate(bits):
        keep = jnp.where(lane == piece, bit, keep)
    return jnp.where(keep > 0, values.astype(F32), 0.0)


def ranks(flags):
    up = (iota((LANES, LANES), 0) <= iota((LANES, LANES), 1)).astype(F32).astype(BF16)
    ones = jnp.ones((LANES, LANES), BF16)
    within = jnp.dot(flags.astype(BF16), up, preferred_element_type=F32)
    totals = jnp.dot(flags.astype(BF16), ones, preferred_element_type=F32)
    row, other = iota((16, 16), 0), iota((16, 16), 1)
    same = (row < 8) == (other < 8)
    before = jnp.where(same & (other < row), 1.0, 0.0).astype(BF16)
    every = jnp.where(same, 1.0, 0.0).astype(BF16)
    earlier = jnp.dot(before, totals.astype(BF16), preferred_element_type=F32)
    count = jnp.dot(every, totals.astype(BF16), preferred_element_type=F32)
    return jnp.where(flags > 0, within + earlier - 1.0, -1.0), count


def prepare_kernel(paired, p_ref, pm_ref, h_ref, hm_ref, row_ref, col_ref, cell_ref, expo_ref, pref_ref, *refs):
    outs, (tmp, fields, matrix, onehot) = refs[:-4], refs[-4:]
    layer = lax.axis_index("layer")
    count = lax.axis_size("layer")
    band = p_ref.shape[0]
    for block in range(band // BS):
        rows = pl.ds(block * BS, BS)
        tmp[rows, :] = masked(p_ref[rows, :], [pm_ref[piece, block] for piece in range(LANES // BS)])
    turned = tmp[...].T.astype(BF16)
    col = col_ref[...]
    cell = cell_ref[...]
    cell_z = (cell % GZ).astype(F32)
    values = [
        row_ref[...].astype(F32),
        (col // LANES).astype(F32),
        (col % LANES).astype(F32),
        (cell // (GY * GZ)).astype(F32),
        (cell // GZ % GY).astype(F32),
        cell_z,
        *split3(expo_ref[...]),
        *split3(pref_ref[...]),
    ]
    for index in range(16):
        fields[8 * index : 8 * index + 8, :] = values[index] if index < len(values) else jnp.zeros((8, LANES), F32)
    tiles = [fields[pl.ds(part, 16, stride=8), :].astype(BF16) for part in range(2 * PAIRS)]
    for part in range(2 * PAIRS):
        matrix[:, part * LANES : part * LANES + LANES] = tiles[part]
    faces = jnp.concatenate([jnp.where(cell_z < R, 1.0, 0.0), jnp.where(cell_z >= GZ - R, 1.0, 0.0)], axis=0)
    place, many = ranks(faces)
    slot = iota((LANES, LANES), 0)
    for part in range(2 * PAIRS):
        lanes = pl.ds(part * LANES, LANES)
        for face in range(2):
            hit = slot == place[face * 8 + part : face * 8 + part + 1, :]
            onehot[face * LANES : face * LANES + LANES, lanes] = jnp.where(hit, 1.0, 0.0).astype(BF16)
    listed = lax.dot_general(matrix[...], onehot[...], NT, preferred_element_type=F32)
    over = jnp.where(jnp.max(many, axis=0, keepdims=True) > LANES, 1.0, 0.0)
    over = jnp.concatenate([over, over], axis=1)
    listed = jnp.where(iota(listed.shape, 0) == FLAG, over, listed).astype(BF16)
    copies = outs[:3] if paired else outs[:1]
    for out in copies:
        out[0:LANES, :] = turned
        for pair in range(PAIRS):
            out[LANES + 16 * pair : LANES + 16 * pair + 16, :] = matrix[:, pair * UNIT : pair * UNIT + UNIT]
        out[LANES + 16 * PAIRS : BASE, :] = listed

    def piece(chunk):
        pieces = LANES // BS
        out = []
        for block in range(h_ref.shape[0] // BS):
            rows = pl.ds(block * BS, BS)
            bits = [hm_ref[block, chunk * pieces + at] for at in range(pieces)]
            value = h_ref[rows, pl.ds(pl.multiple_of(chunk * LANES, LANES), LANES)]
            out.append(masked(value, bits).astype(BF16))
        return jnp.concatenate(out, axis=0)

    if paired:
        outs[1][BASE:, 0:LANES] = piece(layer ^ 2)
        outs[1][BASE:, LANES:UNIT] = piece(layer ^ 3)
        outs[2][BASE:, 0:LANES] = piece(layer ^ 1)
        outs[2][BASE:, LANES:UNIT] = jnp.zeros((h_ref.shape[0], LANES), BF16)
        outs[3][...] = piece(layer)
    else:
        for back in range(h_ref.shape[1] // LANES):
            outs[1][back] = piece(lax.rem(layer + back, count))


def prepare(paired, p, p_mask, h, h_mask, *gauss):
    band = p.shape[0]
    base = jax.ShapeDtypeStruct((BASE, band), BF16)
    tall = jax.ShapeDtypeStruct((BASE + h.shape[0], band), BF16)
    if paired:
        outs = (base, tall, tall, jax.ShapeDtypeStruct((h.shape[0], LANES), BF16))
    else:
        outs = (base, jax.ShapeDtypeStruct((h.shape[1] // LANES, h.shape[0], LANES), BF16))
    return pl.pallas_call(
        functools.partial(prepare_kernel, paired),
        out_shape=outs,
        in_specs=[VMEM, SMEM, VMEM, SMEM] + [VMEM] * 5,
        out_specs=(VMEM,) * len(outs),
        scratch_shapes=[
            pltpu.VMEM(p.shape, F32),
            pltpu.VMEM((16 * 8, LANES), F32),
            pltpu.VMEM((16, 2 * PAIRS * LANES), BF16),
            pltpu.VMEM((UNIT, 2 * PAIRS * LANES), BF16),
        ],
        compiler_params=PARAMS,
        name="prepare",
    )(p, p_mask, h, h_mask, *gauss)


class Blocks:
    def __init__(self, refs, num_col, num_layer):
        self.refs = refs
        self.num_col, self.num_layer = num_col, num_layer
        self.paired = len(refs) > 1
        self.col, self.layer = lax.axis_index("col"), lax.axis_index("layer")
        self.total = num_col * num_layer
        self.col_shifts = [0, 1] if num_col == 2 else [0, -1, 1]

    def ident(self, index):
        if not self.paired:
            return index
        return (self.layer ^ (index % 4)) * 2 + (self.col ^ (index // 4))

    def matrix(self, index):
        return self.refs[index][0:LANES, :] if self.paired else self.refs[0][index, 0:LANES, :]

    def slab(self, layer, piece):
        index = layer * self.num_col + piece
        return self.refs[0][index, 0:LANES, :]

    def tile(self, which, side, pair):
        rows = pl.ds(LANES + 16 * pair, 16)
        if self.paired:
            return self.refs[which * 4 + side][rows, :].astype(F32)
        shift_l = 0 if side == 0 else (1 if side == 1 else -1)
        index = lax.rem(self.layer + shift_l + self.num_layer, self.num_layer) * self.num_col
        index += lax.rem(self.col + self.col_shifts[which] + self.num_col, self.num_col)
        return self.refs[0][index, rows, :].astype(F32)

    def side_shift(self, side):
        if self.paired:
            even = (self.layer % 2) == 0
            return jnp.where(even, 1.0, -1.0) if side == 1 else jnp.where(even, -1.0, 1.0)
        return 1.0 if side == 1 else -1.0

    def sides(self):
        return (1, 3) if self.paired else (1, 2)

    def units(self):
        return [(which, pair) for which in range(len(self.col_shifts)) for pair in range(PAIRS + 1)]

    def listed(self, which):
        halves = []
        for side in self.sides():
            both = self.tile(which, side, PAIRS)
            upward = self.side_shift(side) > 0
            halves.append(jnp.where(upward, both[:, 0:LANES], both[:, LANES:UNIT]))
        return jnp.concatenate(halves, axis=1)

    def unit(self, which, pair):
        return self.tile(which, 0, pair) if pair < PAIRS else self.listed(which)

    def lifts(self, pair):
        if pair < PAIRS:
            return 0.0
        lane = iota((1, UNIT), 1)
        first, second = self.sides()
        return jnp.where(lane < LANES, self.side_shift(first), self.side_shift(second)) * float(GZ)

    def over(self):
        flags = [
            self.tile(which, side, PAIRS)[FLAG : FLAG + 1, :]
            for which in range(len(self.col_shifts))
            for side in self.sides()
        ]
        return functools.reduce(jnp.maximum, flags)

    def long_steps(self):
        return [(which, side) for which in range(len(self.col_shifts)) for side in self.sides()]


def weigh(blocks, whole, tile):
    band = whole.shape[1]
    onehot = jnp.where(iota((band, UNIT), 0) == tile[0:1, :], 1.0, 0.0).astype(BF16)
    found = jnp.dot(whole[...], onehot, preferred_element_type=F32)
    picked = jnp.zeros((LANES, UNIT), F32)
    for index in range(blocks.total):
        mine = tile[1:2, :] == jnp.asarray(blocks.ident(index)).astype(F32)
        picked = jnp.where(mine, found[index * LANES : index * LANES + LANES, :], picked)
    value = jnp.sum(jnp.where(iota((LANES, UNIT), 0) == tile[2:3, :], picked, 0.0), axis=0, keepdims=True)
    return (tile[9:10, :] + tile[10:11, :] + tile[11:12, :]) * value


def weigh_kernel(num_col, num_layer, refs_in, *refs):
    blocks = Blocks(refs[:refs_in], num_col, num_layer)
    coef_ref, long_ref, whole = refs[refs_in:]
    for index in range(blocks.total):
        whole[index * LANES : index * LANES + LANES, :] = blocks.matrix(index)
    over = blocks.over()
    for at, (which, pair) in enumerate(blocks.units()):
        coef = weigh(blocks, whole, blocks.unit(which, pair))
        if pair == PAIRS:
            coef = jnp.where(over > 0, 0.0, coef)
        coef_ref[at : at + 1, :] = coef

    @pl.when(jnp.max(over) > 0)
    def _():
        for at, (which, side) in enumerate(blocks.long_steps()):

            def step(pair, carry):
                long_ref[at, pl.ds(pair, 1), :] = weigh(blocks, whole, blocks.tile(which, side, pair))
                return carry

            lax.fori_loop(0, PAIRS, step, 0)


def weigh_all(arrays, num_col, num_layer):
    ways = 2 if num_col == 2 else 3
    band = arrays[0].shape[-1]
    return pl.pallas_call(
        functools.partial(weigh_kernel, num_col, num_layer, len(arrays)),
        out_shape=(
            jax.ShapeDtypeStruct((ways * (PAIRS + 1), UNIT), F32),
            jax.ShapeDtypeStruct((ways * 2, PAIRS, UNIT), F32),
        ),
        in_specs=[VMEM] * len(arrays),
        out_specs=(VMEM, VMEM),
        scratch_shapes=[pltpu.VMEM((num_col * num_layer * LANES, band), BF16)],
        compiler_params=PARAMS,
        cost_estimate=pl.CostEstimate(flops=2_000_000_000, bytes_accessed=1_000_000, transcendentals=0),
        name="weigh",
    )(*arrays)


def bell(dist, expo):
    square = dist * dist
    return jnp.where(square < (R + 0.5) ** 2, jnp.exp(-expo * square), 0.0)


def spread(blocks, tile, which, lift, coef, at, planeh, planel, depth):
    expo = tile[6:7, :] + tile[7:8, :] + tile[8:9, :]
    ex = bell(iota((GX + 2 * R, UNIT), 0) - float(R) - tile[3:4, :], expo)
    dy = iota((GY, UNIT), 0) - tile[4:5, :] - float(blocks.col_shifts[which] * GY)
    if blocks.num_col == 2 and which == 1:
        dy = jnp.where(dy < -float(GY), dy + 2.0 * GY, dy)
    ey = bell(dy, expo)
    ez = bell(iota((GZ, UNIT), 0) - tile[5:6, :] - lift, expo) * coef
    lanes = pl.ds(at * UNIT, UNIT)
    ez_hi = ez.astype(BF16)
    depth[0:GZ, lanes] = ez_hi
    depth[GZ : 2 * GZ, lanes] = (ez - ez_hi.astype(F32)).astype(BF16)
    for x in range(GX + 2 * R):
        plane = ex[x : x + 1, :] * ey
        plane_hi = plane.astype(BF16)
        planeh[x * GY : x * GY + GY, lanes] = plane_hi
        planel[x * GY : x * GY + GY, lanes] = (plane - plane_hi.astype(F32)).astype(BF16)


def summed(planeh, planel, depth):
    first = lax.dot_general(planeh, depth, NT, preferred_element_type=F32)
    second = lax.dot_general(planel, depth[0:GZ, :], NT, preferred_element_type=F32)
    return first[:, 0:GZ] + first[:, GZ : 2 * GZ] + second


def collocate_kernel(num_col, num_layer, refs_in, *refs):
    blocks = Blocks(refs[:refs_in], num_col, num_layer)
    coef_ref, long_ref, core_ref, low_ref, high_ref, planeh, planel, depth, acc = refs[refs_in:]
    for at, (which, pair) in enumerate(blocks.units()):
        spread(
            blocks, blocks.unit(which, pair), which, blocks.lifts(pair), coef_ref[at : at + 1, :], at,
            planeh, planel, depth,
        )
    total = summed(planeh[...], planel[...], depth[...])
    low_ref[...] = total[0:HALO, :]
    core_ref[...] = total[HALO : HALO + CORE, :]
    high_ref[...] = total[HALO + CORE : FULL, :]

    @pl.when(jnp.max(blocks.over()) > 0)
    def _():
        acc[...] = jnp.zeros_like(acc)
        for at, (which, side) in enumerate(blocks.long_steps()):

            def step(pair, carry):
                lift = blocks.side_shift(side) * float(GZ)
                coef = long_ref[at, pl.ds(pair, 1), :]
                spread(blocks, blocks.tile(which, side, pair), which, lift, coef, 0, planeh, planel, depth)
                acc[...] += summed(planeh[:, 0:UNIT], planel[:, 0:UNIT], depth[:, 0:UNIT])
                return carry

            lax.fori_loop(0, PAIRS, step, 0)
        low_ref[...] += acc[0:HALO, :]
        core_ref[...] += acc[HALO : HALO + CORE, :]
        high_ref[...] += acc[HALO + CORE : FULL, :]


def collocate(arrays, coef, long, num_col, num_layer):
    gaussians = coef.shape[0] * UNIT
    return pl.pallas_call(
        functools.partial(collocate_kernel, num_col, num_layer, len(arrays)),
        out_shape=(
            jax.ShapeDtypeStruct((CORE, GZ), F32),
            jax.ShapeDtypeStruct((HALO, GZ), F32),
            jax.ShapeDtypeStruct((HALO, GZ), F32),
        ),
        in_specs=[VMEM] * (len(arrays) + 2),
        out_specs=(VMEM, VMEM, VMEM),
        scratch_shapes=[
            pltpu.VMEM((FULL, gaussians), BF16),
            pltpu.VMEM((FULL, gaussians), BF16),
            pltpu.VMEM((2 * GZ, gaussians), BF16),
            pltpu.VMEM((FULL, GZ), F32),
        ],
        compiler_params=PARAMS,
        cost_estimate=pl.CostEstimate(flops=3_000_000_000, bytes_accessed=1_000_000, transcendentals=0),
        name="collocate",
    )(*arrays, coef, long)


def product_kernel(num_row, num_col, num_layer, refs_in, *refs):
    blocks = Blocks(refs[:refs_in], num_col, num_layer)
    h_refs = refs[refs_in : refs_in + num_row]
    out_ref, slab = refs[refs_in + num_row :]
    row = lax.axis_index("row")
    rows = h_refs[0].shape[1]
    for back in range(num_layer):
        for step in range(num_row):
            start = pl.multiple_of(lax.rem(row - step + num_row, num_row) * rows, rows)
            slab[back, pl.ds(start, rows), :] = h_refs[step][back]
    total = jnp.zeros(out_ref.shape, F32)
    for back in range(num_layer):
        for piece in range(num_col):
            if blocks.paired:
                left = blocks.matrix(piece * 4 + back)
                start = pl.multiple_of((blocks.col ^ piece) * LANES, LANES)
            else:
                source = lax.rem(blocks.layer - back + num_layer, num_layer)
                left = blocks.slab(source, piece)
                start = piece * LANES
            right = slab[back, pl.ds(start, LANES), :]
            total += lax.dot_general(left, right, TN, preferred_element_type=F32)
    out_ref[...] = total.astype(BF16)


def multiply(arrays, parts, num_row, num_col, num_layer):
    return pl.pallas_call(
        functools.partial(product_kernel, num_row, num_col, num_layer, len(arrays)),
        out_shape=jax.ShapeDtypeStruct((arrays[0].shape[-1], LANES), BF16),
        in_specs=[VMEM] * (num_row + len(arrays)),
        out_specs=VMEM,
        scratch_shapes=[pltpu.VMEM((num_layer, num_col * LANES, LANES), BF16)],
        compiler_params=PARAMS,
        cost_estimate=pl.CostEstimate(flops=500_000_000, bytes_accessed=1_000_000, transcendentals=0),
        name="multiply",
    )(*arrays, *parts)


def stack_kernel(rows, own_ref, near_ref, far_ref, both_ref, out_ref):
    out_ref[0] = own_ref[...]
    out_ref[1] = near_ref[BASE:, 0:LANES]
    out_ref[2] = far_ref[BASE:, 0:LANES]
    out_ref[3] = both_ref[BASE:, LANES:UNIT]


def stack(own, near, far, both):
    rows = own.shape[0]
    return pl.pallas_call(
        functools.partial(stack_kernel, rows),
        out_shape=jax.ShapeDtypeStruct((4, rows, LANES), BF16),
        in_specs=[VMEM] * 4,
        out_specs=VMEM,
        compiler_params=PARAMS,
        name="stack",
    )(own, near, far, both)


def fold_kernel(core_ref, below_ref, above_ref, out_ref):
    out_ref[0:HALO, :] = core_ref[0:HALO, :] + below_ref[...]
    out_ref[HALO : CORE - HALO, :] = core_ref[HALO : CORE - HALO, :]
    out_ref[CORE - HALO : CORE, :] = core_ref[CORE - HALO : CORE, :] + above_ref[...]


def fold(core, below, above):
    return pl.pallas_call(
        fold_kernel,
        out_shape=jax.ShapeDtypeStruct((CORE, GZ), F32),
        in_specs=[VMEM, VMEM, VMEM],
        out_specs=VMEM,
        name="fold",
    )(core, below, above)


def shifted(value, axis, count, step):
    return lax.ppermute(value, axis, [(i, (i + step) % count) for i in range(count)])


def crossed(value, col_bit, layer_bits):
    pairs = [(c * 4 + l, (c ^ col_bit) * 4 + (l ^ layer_bits)) for c in range(2) for l in range(4)]
    return lax.ppermute(value, ("col", "layer"), pairs)


def gather_paired(base, tall_y, tall_core):
    got_x = crossed(base, 1, 0)
    got_y = crossed(tall_y, 0, 2)
    got_xy = crossed(base, 1, 2)
    near = crossed(tall_core, 0, 1)
    near_x = crossed(got_x, 0, 1)
    near_y = crossed(got_y, 0, 1)
    near_xy = crossed(got_xy, 0, 1)
    return [base, near, got_y, near_y, got_x, near_x, got_xy, near_xy]


def on_device(p_slabs, p_mask, h_slabs, h_mask, gauss_row, gauss_col, gauss_cell, gauss_expo, gauss_pref):
    num_row, num_col, num_layer = (lax.axis_size(axis) for axis in ("row", "col", "layer"))
    paired = num_col == 2 and num_layer == 4
    flat = [x.reshape(8, LANES) for x in (gauss_row, gauss_col, gauss_cell, gauss_expo, gauss_pref)]
    made = prepare(paired, p_slabs[0], p_mask[0].T, h_slabs[0], h_mask[0], *flat)
    if paired:
        base, tall_y, tall_core, own = made
        arrays = gather_paired(base, tall_y, tall_core)
        mine = stack(own, arrays[1], arrays[2], arrays[3])
    else:
        base, pieces = made
        arrays = [lax.all_gather(base, ("layer", "col"), axis=0)]
        mine = [pieces[0]] + [shifted(pieces[step], "layer", num_layer, step) for step in range(1, num_layer)]
        mine = jnp.stack(mine)
    parts = [mine] + [shifted(mine, "row", num_row, step) for step in range(1, num_row)]
    coef, long = weigh_all(arrays, num_col, num_layer)
    core, low, high = collocate(arrays, coef, long, num_col, num_layer)
    below = shifted(high, "row", num_row, 1)
    above = shifted(low, "row", num_row, num_row - 1)
    product = multiply(arrays, parts, num_row, num_col, num_layer)
    density = fold(core, below, above).reshape(GX, GY, GZ)
    return (product, density)


def solution(mesh):
    placed = (P("layer", "row", "col"),) * 4 + (P(("row", "col", "layer")),) * 5
    return jax.shard_map(
        on_device,
        mesh=mesh,
        in_specs=placed,
        out_specs=(P("row", ("col", "layer")), P("row", "col", "layer")),
        check_vma=False,
    )
```

profile of v0, /device:TPU:0, one launch (start us, length us, event | category | flops | bytes accessed | tf_op | source)
XLA Modules:
  0.0 34.2 jit_solution(12705493528596943609)
XLA Ops:
  0.7 0.6 %copy-done.6 = f32[1024]{0:T(1024)S(1)} copy-done((f32[1024]{0:T(1024)S(1)}, f32[1024]{0:T(1024)}, u32[]{:S(2)}) %copy-start.6) | copy-done | bytes 4120
  1.4 0.8 %copy-done.1 = bf16[1,256,128]{2,1,0:T(8,128)(2,1)S(1)} copy-done((bf16[1,256,128]{2,1,0:T(8,128)(2,1)S(1)}, bf16[1,256,128]{2,1,0:T(8,128)(2,1)}, u32[]{:S(2)}) %copy-start.1) | copy-done | bytes 65560
  2.2 0.8 %copy-done.2 = bf16[1,64,512]{2,1,0:T(8,128)(2,1)S(1)} copy-done((bf16[1,64,512]{2,1,0:T(8,128)(2,1)S(1)}, bf16[1,64,512]{2,1,0:T(8,128)(2,1)}, u32[]{:S(2)}) %copy-start.2) | copy-done | bytes 65560
  3.1 0.7 %copy-done.7 = f32[1024]{0:T(1024)S(1)} copy-done((f32[1024]{0:T(1024)S(1)}, f32[1024]{0:T(1024)}, u32[]{:S(2)}) %copy-start.7) | copy-done | bytes 4120
  3.7 0.7 %copy-done.8 = s32[1,8,4]{1,2,0:T(4,128)S(1)} copy-done((s32[1,8,4]{1,2,0:T(4,128)S(1)}, s32[1,8,4]{1,2,0:T(4,128)}, u32[]{:S(2)}) %copy-start.8) | copy-done | bytes 152
  4.4 1.2 %prepare.1 = (bf16[208,256]{1,0:T(8,128)(2,1)S(1)}, bf16[272,256]{1,0:T(8,128)(2,1)S(1)}, bf16[272,256]{1,0:T(8,128)(2,1)S(1)}, bf16[64,128]{1,0:T(8,128)(2,1)S(1)}) custom-call(bf16[256,128]{1,0:T(8,128)(2,1)S(1)} %bitcast.12, s32[4,8]{1,0:T(4,128)S(1)} %bitcast.19, bf16[64,512]{1,0:T(8,128)(2,1)S(1)} %bitcast.13, s32[2,16]{1,0:T(2,128)S(1)} %bitcast.20, ...), custom_call_target="tpu_custom_call" | custom-call | tf_op jit(solution)/shard_map/prepare/pallas_call | solution.py:141
  5.6 3.0 %collective-permute-start.1 = (bf16[272,256]{1,0:T(8,128)(2,1)S(1)}, bf16[272,256]{1,0:T(8,128)(2,1)S(1)}, u32[]{:S(2)}, u32[]{:S(2)}) collective-permute-start(bf16[272,256]{1,0:T(8,128)(2,1)S(1)} %get-tuple-element.13), channel_id=1, source_target_pairs={{0,2},{1,3},{2,0},{3,1},{4,6},{5,7},{6,4},{7,5},{8,10},{9,11},{10,... | collective-permute-start | bytes 417800 | tf_op jit(solution)/shard_map/ppermute | solution.py:445
  8.6 1.5 %collective-permute-start.3 = (bf16[208,256]{1,0:T(8,128)(2,1)S(1)}, bf16[208,256]{1,0:T(8,128)(2,1)S(1)}, u32[]{:S(2)}, u32[]{:S(2)}) collective-permute-start(bf16[208,256]{1,0:T(8,128)(2,1)S(1)} %get-tuple-element.11.refs_0_), channel_id=1, source_target_pairs={{0,4},{1,5},{2,6},{3,7},{4,0},{5,1},{6,2},{7,3},{8,12},{9,13},{10,... | collective-permute-start | bytes 319496 | tf_op jit(solution)/shard_map/ppermute | solution.py:445
  10.1 0.0 collective-permute-start.5
  10.2 2.1 %collective-permute-done.1.far_ref.refs_2_ = bf16[272,256]{1,0:T(8,128)(2,1)S(1)} collective-permute-done((bf16[272,256]{1,0:T(8,128)(2,1)S(1)}, bf16[272,256]{1,0:T(8,128)(2,1)S(1)}, u32[]{:S(2)}, u32[]{:S(2)}) %collective-permute-start.1) | collective-permute-done | bytes 139296 | tf_op jit(solution)/shard_map/ppermute | solution.py:445
  12.3 1.9 %collective-permute-done.3.refs_4_ = bf16[208,256]{1,0:T(8,128)(2,1)S(1)} collective-permute-done((bf16[208,256]{1,0:T(8,128)(2,1)S(1)}, bf16[208,256]{1,0:T(8,128)(2,1)S(1)}, u32[]{:S(2)}, u32[]{:S(2)}) %collective-permute-start.3) | collective-permute-done | bytes 106528 | tf_op jit(solution)/shard_map/ppermute | solution.py:445
  14.2 1.5 %collective-permute-done.5.refs_6_ = bf16[208,256]{1,0:T(8,128)(2,1)S(1)} collective-permute-done((bf16[208,256]{1,0:T(8,128)(2,1)S(1)}, bf16[208,256]{1,0:T(8,128)(2,1)S(1)}, u32[]{:S(2)}, u32[]{:S(2)}) %collective-permute-start.5) | collective-permute-done | bytes 106528 | tf_op jit(solution)/shard_map/ppermute | solution.py:445
  15.8 1.6 %collective-permute-start.7 = (bf16[4,64,128]{2,1,0:T(8,128)(2,1)S(1)}, bf16[4,64,128]{2,1,0:T(8,128)(2,1)S(1)}, u32[]{:S(2)}, u32[]{:S(2)}) collective-permute-start(bf16[4,64,128]{2,1,0:T(8,128)(2,1)S(1)} %stack.1.refs_8_), channel_id=1, source_target_pairs={{0,8},{8,16},{16,24},{24,0},{1,9},{9,17},{17,25},{25,1},{2,10},{10... | collective-permute-start | bytes 196616 | tf_op jit(solution)/shard_map/ppermute | solution.py:440
  17.4 2.6 %collective-permute-start.8 = (bf16[4,64,128]{2,1,0:T(8,128)(2,1)S(1)}, bf16[4,64,128]{2,1,0:T(8,128)(2,1)S(1)}, u32[]{:S(2)}, u32[]{:S(2)}) collective-permute-start(bf16[4,64,128]{2,1,0:T(8,128)(2,1)S(1)} %stack.1.refs_8_), channel_id=1, source_target_pairs={{0,16},{8,24},{16,0},{24,8},{1,17},{9,25},{17,1},{25,9},{2,18},{10... | collective-permute-start | bytes 196616 | tf_op jit(solution)/shard_map/ppermute | solution.py:440
  20.0 1.3 %collective-permute-start.9 = (bf16[4,64,128]{2,1,0:T(8,128)(2,1)S(1)}, bf16[4,64,128]{2,1,0:T(8,128)(2,1)S(1)}, u32[]{:S(2)}, u32[]{:S(2)}) collective-permute-start(bf16[4,64,128]{2,1,0:T(8,128)(2,1)S(1)} %stack.1.refs_8_), channel_id=1, source_target_pairs={{0,24},{8,0},{16,8},{24,16},{1,25},{9,1},{17,9},{25,17},{2,26},{10... | collective-permute-start | bytes 196616 | tf_op jit(solution)/shard_map/ppermute | solution.py:440
  21.3 1.6 %weigh.1 = (f32[10,256]{1,0:T(8,128)S(1)}, f32[4,4,256]{2,1,0:T(4,128)S(1)}) custom-call(bf16[208,256]{1,0:T(8,128)(2,1)S(1)} %get-tuple-element.11.refs_0_, bf16[272,256]{1,0:T(8,128)(2,1)S(1)} %collective-permute-done.near_ref.refs_1_, bf16[272,256]{1,0:T(8,128)(2,1)S(1)} %collective-permute-done.1.far_ref.refs_2_, ...), custom_call_target="tpu_custom_call" | custom-call | flops 2000000000 | bytes 1000000 | tf_op jit(solution)/shard_map/weigh/pallas_call | solution.py:267
  22.9 1.7 %collocate.1 = (f32[256,128]{1,0:T(8,128)S(1)}, f32[64,128]{1,0:T(8,128)S(1)}, f32[64,128]{1,0:T(8,128)S(1)}) custom-call(bf16[208,256]{1,0:T(8,128)(2,1)S(1)} %get-tuple-element.11.refs_0_, bf16[272,256]{1,0:T(8,128)(2,1)S(1)} %collective-permute-done.near_ref.refs_1_, bf16[272,256]{1,0:T(8,128)(2,1)S(1)} %collective-permute-done.1.far_ref.refs_2_, ...), custom_call_target="tpu_custom_call" | custom-call | flops 3000000000 | bytes 1000000 | tf_op jit(solution)/shard_map/collocate/pallas_call | solution.py:345
  24.6 0.6 %copy-done = f32[256,128]{1,0:T(8,128)} copy-done((f32[256,128]{1,0:T(8,128)}, f32[256,128]{1,0:T(8,128)S(1)}, u32[]{:S(2)}) %copy-start) | copy-done | bytes 131096
  25.3 0.7 %collective-permute-start.10 = (f32[64,128]{1,0:T(8,128)S(1)}, f32[64,128]{1,0:T(8,128)S(1)}, u32[]{:S(2)}, u32[]{:S(2)}) collective-permute-start(f32[64,128]{1,0:T(8,128)S(1)} %get-tuple-element.18), channel_id=1, source_target_pairs={{0,8},{8,16},{16,24},{24,0},{1,9},{9,17},{17,25},{25,1},{2,10},{10... | collective-permute-start | bytes 98312 | tf_op jit(solution)/shard_map/ppermute | solution.py:440
  26.0 3.1 %collective-permute-start.11 = (f32[64,128]{1,0:T(8,128)S(1)}, f32[64,128]{1,0:T(8,128)S(1)}, u32[]{:S(2)}, u32[]{:S(2)}) collective-permute-start(f32[64,128]{1,0:T(8,128)S(1)} %get-tuple-element.19), channel_id=1, source_target_pairs={{0,24},{8,0},{16,8},{24,16},{1,25},{9,1},{17,9},{25,17},{2,26},{10... | collective-permute-start | bytes 98312 | tf_op jit(solution)/shard_map/ppermute | solution.py:440
  29.1 1.9 %collective-permute-done.10.below_ref = f32[64,128]{1,0:T(8,128)S(1)} collective-permute-done((f32[64,128]{1,0:T(8,128)S(1)}, f32[64,128]{1,0:T(8,128)S(1)}, u32[]{:S(2)}, u32[]{:S(2)}) %collective-permute-start.10) | collective-permute-done | bytes 32800 | tf_op jit(solution)/shard_map/ppermute | solution.py:440
  31.0 0.6 %copy-done.10 = f32[64,128]{1,0:T(8,128)} copy-done((f32[64,128]{1,0:T(8,128)}, f32[64,128]{1,0:T(8,128)S(1)}, u32[]{:S(2)}) %copy-start.10) | copy-done | bytes 32792
  31.6 1.6 %fold.1 = f32[256,128]{1,0:T(8,128)} custom-call(f32[256,128]{1,0:T(8,128)} %copy-done, f32[64,128]{1,0:T(8,128)} %copy-done.10, f32[64,128]{1,0:T(8,128)} %copy-done.11), custom_call_target="tpu_custom_call" | custom-call | tf_op jit(solution)/shard_map/fold/pallas_call | solution.py:430
  33.2 1.0 %multiply.1 = bf16[256,128]{1,0:T(8,128)(2,1)} custom-call(bf16[208,256]{1,0:T(8,128)(2,1)S(1)} %get-tuple-element.11.refs_0_, bf16[272,256]{1,0:T(8,128)(2,1)S(1)} %collective-permute-done.near_ref.refs_1_, bf16[272,256]{1,0:T(8,128)(2,1)S(1)} %collective-permute-done.1.far_ref.refs_2_, bf16[272,256]{1,0:T(8,128)(2,1)S(1)} %collective-permute-done.2.both_ref.refs_3_, ...), custom_call_target="tpu_custom_call" | custom-call | flops 500000000 | bytes 1000000 | tf_op jit(solution)/shard_map/multiply/pallas_call | solution.py:392
  (30 shorter events, 0.1 us)
Async XLA Ops:
  0.6 0.7 %copy-start.6 = (f32[1024]{0:T(1024)S(1)}, f32[1024]{0:T(1024)}, u32[]{:S(2)}) copy-start(f32[1024]{0:T(1024)} %param.16) | copy-start | bytes 12292
  0.6 0.7 %copy-start.5 = (s32[1024]{0:T(1024)S(1)}, s32[1024]{0:T(1024)}, u32[]{:S(2)}) copy-start(s32[1024]{0:T(1024)} %param.15) | copy-start | bytes 12292
  0.7 0.7 %copy-start.4 = (s32[1024]{0:T(1024)S(1)}, s32[1024]{0:T(1024)}, u32[]{:S(2)}) copy-start(s32[1024]{0:T(1024)} %param.14) | copy-start | bytes 12292
  0.7 0.7 %copy-start.3 = (s32[1024]{0:T(1024)S(1)}, s32[1024]{0:T(1024)}, u32[]{:S(2)}) copy-start(s32[1024]{0:T(1024)} %param.13) | copy-start | bytes 12292
  0.7 0.7 %copy-start.9 = (s32[1,2,16]{2,1,0:T(2,128)S(1)}, s32[1,2,16]{2,1,0:T(2,128)}, u32[]{:S(2)}) copy-start(s32[1,2,16]{2,1,0:T(2,128)} %param.12) | copy-start | bytes 388
  1.4 0.8 %copy-start.1 = (bf16[1,256,128]{2,1,0:T(8,128)(2,1)S(1)}, bf16[1,256,128]{2,1,0:T(8,128)(2,1)}, u32[]{:S(2)}) copy-start(bf16[1,256,128]{2,1,0:T(8,128)(2,1)} %param.9) | copy-start | bytes 196612
  2.2 0.8 %copy-start.2 = (bf16[1,64,512]{2,1,0:T(8,128)(2,1)S(1)}, bf16[1,64,512]{2,1,0:T(8,128)(2,1)}, u32[]{:S(2)}) copy-start(bf16[1,64,512]{2,1,0:T(8,128)(2,1)} %param.11) | copy-start | bytes 196612
  3.1 0.7 %copy-start.7 = (f32[1024]{0:T(1024)S(1)}, f32[1024]{0:T(1024)}, u32[]{:S(2)}) copy-start(f32[1024]{0:T(1024)} %param.17) | copy-start | bytes 12292
  3.7 0.7 %copy-start.8 = (s32[1,8,4]{1,2,0:T(4,128)S(1)}, s32[1,8,4]{1,2,0:T(4,128)}, u32[]{:S(2)}) copy-start(s32[1,8,4]{1,2,0:T(4,128)} %param.10) | copy-start | bytes 388
  5.6 6.7 %collective-permute-start.1 = (bf16[272,256]{1,0:T(8,128)(2,1)S(1)}, bf16[272,256]{1,0:T(8,128)(2,1)S(1)}, u32[]{:S(2)}, u32[]{:S(2)}) collective-permute-start(bf16[272,256]{1,0:T(8,128)(2,1)S(1)} %get-tuple-element.13), channel_id=1, source_target_pairs={{0,2},{1,3},{2,0},{3,1},{4,6},{5,7},{6,4},{7,5},{8,10},{9,11},{10,... | collective-permute-start | bytes 417800 | tf_op jit(solution)/shard_map/ppermute | solution.py:445
  8.6 5.6 %collective-permute-start.3 = (bf16[208,256]{1,0:T(8,128)(2,1)S(1)}, bf16[208,256]{1,0:T(8,128)(2,1)S(1)}, u32[]{:S(2)}, u32[]{:S(2)}) collective-permute-start(bf16[208,256]{1,0:T(8,128)(2,1)S(1)} %get-tuple-element.11.refs_0_), channel_id=1, source_target_pairs={{0,4},{1,5},{2,6},{3,7},{4,0},{5,1},{6,2},{7,3},{8,12},{9,13},{10,... | collective-permute-start | bytes 319496 | tf_op jit(solution)/shard_map/ppermute | solution.py:445
  10.1 5.6 %collective-permute-start.5 = (bf16[208,256]{1,0:T(8,128)(2,1)S(1)}, bf16[208,256]{1,0:T(8,128)(2,1)S(1)}, u32[]{:S(2)}, u32[]{:S(2)}) collective-permute-start(bf16[208,256]{1,0:T(8,128)(2,1)S(1)} %get-tuple-element.11.refs_0_), channel_id=1, source_target_pairs={{0,6},{1,7},{2,4},{3,5},{4,2},{5,3},{6,0},{7,1},{8,14},{9,15},{10,... | collective-permute-start | bytes 319496 | tf_op jit(solution)/shard_map/ppermute | solution.py:445
  10.2 5.6 %collective-permute-start = (bf16[272,256]{1,0:T(8,128)(2,1)S(1)}, bf16[272,256]{1,0:T(8,128)(2,1)S(1)}, u32[]{:S(2)}, u32[]{:S(2)}) collective-permute-start(bf16[272,256]{1,0:T(8,128)(2,1)S(1)} %get-tuple-element.12), channel_id=1, source_target_pairs={{0,1},{1,0},{2,3},{3,2},{4,5},{5,4},{6,7},{7,6},{8,9},{9,8},{10,11... | collective-permute-start | bytes 417800 | tf_op jit(solution)/shard_map/ppermute | solution.py:445
  12.3 3.4 %collective-permute-start.2 = (bf16[272,256]{1,0:T(8,128)(2,1)S(1)}, bf16[272,256]{1,0:T(8,128)(2,1)S(1)}, u32[]{:S(2)}, u32[]{:S(2)}) collective-permute-start(bf16[272,256]{1,0:T(8,128)(2,1)S(1)} %collective-permute-done.1.far_ref.refs_2_), channel_id=1, source_target_pairs={{0,1},{1,0},{2,3},{3,2},{4,5},{5,4},{6,7},{7,6},{8,9},{9,8},{10,11... | collective-permute-start | bytes 417800 | tf_op jit(solution)/shard_map/ppermute | solution.py:445
  14.2 7.1 %collective-permute-start.4 = (bf16[208,256]{1,0:T(8,128)(2,1)S(1)}, bf16[208,256]{1,0:T(8,128)(2,1)S(1)}, u32[]{:S(2)}, u32[]{:S(2)}) collective-permute-start(bf16[208,256]{1,0:T(8,128)(2,1)S(1)} %collective-permute-done.3.refs_4_), channel_id=1, source_target_pairs={{0,1},{1,0},{2,3},{3,2},{4,5},{5,4},{6,7},{7,6},{8,9},{9,8},{10,11... | collective-permute-start | bytes 319496 | tf_op jit(solution)/shard_map/ppermute | solution.py:445
  15.7 5.6 %collective-permute-start.6 = (bf16[208,256]{1,0:T(8,128)(2,1)S(1)}, bf16[208,256]{1,0:T(8,128)(2,1)S(1)}, u32[]{:S(2)}, u32[]{:S(2)}) collective-permute-start(bf16[208,256]{1,0:T(8,128)(2,1)S(1)} %collective-permute-done.5.refs_6_), channel_id=1, source_target_pairs={{0,1},{1,0},{2,3},{3,2},{4,5},{5,4},{6,7},{7,6},{8,9},{9,8},{10,11... | collective-permute-start | bytes 319496 | tf_op jit(solution)/shard_map/ppermute | solution.py:445
  15.8 17.5 %collective-permute-start.7 = (bf16[4,64,128]{2,1,0:T(8,128)(2,1)S(1)}, bf16[4,64,128]{2,1,0:T(8,128)(2,1)S(1)}, u32[]{:S(2)}, u32[]{:S(2)}) collective-permute-start(bf16[4,64,128]{2,1,0:T(8,128)(2,1)S(1)} %stack.1.refs_8_), channel_id=1, source_target_pairs={{0,8},{8,16},{16,24},{24,0},{1,9},{9,17},{17,25},{25,1},{2,10},{10... | collective-permute-start | bytes 196616 | tf_op jit(solution)/shard_map/ppermute | solution.py:440
  17.4 15.8 %collective-permute-start.8 = (bf16[4,64,128]{2,1,0:T(8,128)(2,1)S(1)}, bf16[4,64,128]{2,1,0:T(8,128)(2,1)S(1)}, u32[]{:S(2)}, u32[]{:S(2)}) collective-permute-start(bf16[4,64,128]{2,1,0:T(8,128)(2,1)S(1)} %stack.1.refs_8_), channel_id=1, source_target_pairs={{0,16},{8,24},{16,0},{24,8},{1,17},{9,25},{17,1},{25,9},{2,18},{10... | collective-permute-start | bytes 196616 | tf_op jit(solution)/shard_map/ppermute | solution.py:440
  20.0 13.2 %collective-permute-start.9 = (bf16[4,64,128]{2,1,0:T(8,128)(2,1)S(1)}, bf16[4,64,128]{2,1,0:T(8,128)(2,1)S(1)}, u32[]{:S(2)}, u32[]{:S(2)}) collective-permute-start(bf16[4,64,128]{2,1,0:T(8,128)(2,1)S(1)} %stack.1.refs_8_), channel_id=1, source_target_pairs={{0,24},{8,0},{16,8},{24,16},{1,25},{9,1},{17,9},{25,17},{2,26},{10... | collective-permute-start | bytes 196616 | tf_op jit(solution)/shard_map/ppermute | solution.py:440
  24.6 0.7 %copy-start = (f32[256,128]{1,0:T(8,128)}, f32[256,128]{1,0:T(8,128)S(1)}, u32[]{:S(2)}) copy-start(f32[256,128]{1,0:T(8,128)S(1)} %get-tuple-element.17.core_ref) | copy-start | bytes 393220
  25.3 5.7 %collective-permute-start.10 = (f32[64,128]{1,0:T(8,128)S(1)}, f32[64,128]{1,0:T(8,128)S(1)}, u32[]{:S(2)}, u32[]{:S(2)}) collective-permute-start(f32[64,128]{1,0:T(8,128)S(1)} %get-tuple-element.18), channel_id=1, source_target_pairs={{0,8},{8,16},{16,24},{24,0},{1,9},{9,17},{17,25},{25,1},{2,10},{10... | collective-permute-start | bytes 98312 | tf_op jit(solution)/shard_map/ppermute | solution.py:440
  26.0 5.0 %collective-permute-start.11 = (f32[64,128]{1,0:T(8,128)S(1)}, f32[64,128]{1,0:T(8,128)S(1)}, u32[]{:S(2)}, u32[]{:S(2)}) collective-permute-start(f32[64,128]{1,0:T(8,128)S(1)} %get-tuple-element.19), channel_id=1, source_target_pairs={{0,24},{8,0},{16,8},{24,16},{1,25},{9,1},{17,9},{25,17},{2,26},{10... | collective-permute-start | bytes 98312 | tf_op jit(solution)/shard_map/ppermute | solution.py:440
  31.0 0.6 %copy-start.10 = (f32[64,128]{1,0:T(8,128)}, f32[64,128]{1,0:T(8,128)S(1)}, u32[]{:S(2)}) copy-start(f32[64,128]{1,0:T(8,128)S(1)} %collective-permute-done.10.below_ref) | copy-start | bytes 98308
  31.0 0.6 %copy-start.11 = (f32[64,128]{1,0:T(8,128)}, f32[64,128]{1,0:T(8,128)S(1)}, u32[]{:S(2)}) copy-start(f32[64,128]{1,0:T(8,128)S(1)} %collective-permute-done.11.above_ref) | copy-start | bytes 98308
where the time goes:
time: 34.5 us; the launch traced here: 34.2 us
  starting transfers between devices  14 us (41%)
  waiting for transfers between devices  7.45 us (22%)
  Pallas kernels  7.03 us (20%)
  local copies, waits for them, and re-layouts  5.01 us (15%)
  between operations  0.73 us (2%)
    ppermute x5, starting transfers between devices, shifted(): lax.ppermute(value, axis, [(i, (i + step) % count) for i in range(count)])  9.39 us
    ppermute x7, waiting for transfers between devices, crossed(): return lax.ppermute(value, ('col', 'layer'), pairs)  5.55 us
    unnamed x24, local copies, waits for them, and re-layouts  5.01 us
    ppermute x7, starting transfers between devices, crossed(): return lax.ppermute(value, ('col', 'layer'), pairs)  4.58 us
    ppermute x5, waiting for transfers between devices, shifted(): lax.ppermute(value, axis, [(i, (i + step) % count) for i in range(count)])  1.9 us
    pallas_call x1, Pallas kernels, collocate(): pl.pallas_call(functools.partial(collocate_kernel, num_col, num_layer, le...  1.67 us
    pallas_call x1, Pallas kernels, weigh_all(): pl.pallas_call(functools.partial(weigh_kernel, num_col, num_layer, len(ar...  1.62 us
    pallas_call x1, Pallas kernels, fold(): pl.pallas_call(fold_kernel, out_shape=jax.ShapeDtypeStruct((CORE, GZ), F3...  1.59 us
  transfers between devices with their start and end apart: 12, of which 4 were waited for; matrix products, arithmetic and copies ran while one was open for 0% of the time, Pallas kernels for 14%

commit v1 on v0

--- a/solution.py
+++ b/solution.py
@@ -24,7 +24,7 @@
 BASE = LANES + META
 FLAG = 12
 VMEM = pl.BlockSpec(memory_space=pltpu.VMEM)
-SMEM = pl.BlockSpec(memory_space=pltpu.SMEM)
+HBM = pl.BlockSpec(memory_space=pltpu.HBM)
 PARAMS = pltpu.CompilerParams(vmem_limit_bytes=40 * 1024 * 1024)
 NT = (((1,), (1,)), ((), ()))
 TN = (((0,), (0,)), ((), ()))
@@ -63,8 +63,15 @@
     return jnp.where(flags > 0, within + earlier - 1.0, -1.0), count
 
 
-def prepare_kernel(paired, p_ref, pm_ref, h_ref, hm_ref, row_ref, col_ref, cell_ref, expo_ref, pref_ref, *refs):
-    outs, (tmp, fields, matrix, onehot) = refs[:-4], refs[-4:]
+def prepare_kernel(paired, *refs):
+    sources, outs, refs = refs[:9], refs[9:-14], refs[-14:]
+    landed, (tmp, fields, matrix, onehot, sems) = refs[:9], refs[9:]
+    copies = [pltpu.make_async_copy(src, dst, sems.at[at]) for at, (src, dst) in enumerate(zip(sources, landed))]
+    for copy in copies:
+        copy.start()
+    for copy in copies:
+        copy.wait()
+    p_ref, pm_ref, h_ref, hm_ref, row_ref, col_ref, cell_ref, expo_ref, pref_ref = landed
     layer = lax.axis_index("layer")
     count = lax.axis_size("layer")
     band = p_ref.shape[0]
@@ -141,15 +148,21 @@
     return pl.pallas_call(
         functools.partial(prepare_kernel, paired),
         out_shape=outs,
-        in_specs=[VMEM, SMEM, VMEM, SMEM] + [VMEM] * 5,
+        in_specs=[HBM] * 9,
         out_specs=(VMEM,) * len(outs),
         scratch_shapes=[
+            pltpu.VMEM(p.shape, p.dtype),
+            pltpu.SMEM(p_mask.shape, p_mask.dtype),
+            pltpu.VMEM(h.shape, h.dtype),
+            pltpu.SMEM(h_mask.shape, h_mask.dtype),
+            *[pltpu.VMEM(x.shape, x.dtype) for x in gauss],
             pltpu.VMEM(p.shape, F32),
             pltpu.VMEM((16 * 8, LANES), F32),
             pltpu.VMEM((16, 2 * PAIRS * LANES), BF16),
             pltpu.VMEM((UNIT, 2 * PAIRS * LANES), BF16),
+            pltpu.SemaphoreType.DMA((9,)),
         ],
-        compiler_params=PARAMS,
+        compiler_params=pltpu.CompilerParams(vmem_limit_bytes=62 * 1024 * 1024),
         name="prepare",
     )(p, p_mask, h, h_mask, *gauss)
 
@@ -366,12 +379,13 @@
 def product_kernel(num_row, num_col, num_layer, refs_in, *refs):
     blocks = Blocks(refs[:refs_in], num_col, num_layer)
     h_refs = refs[refs_in : refs_in + num_row]
-    out_ref, slab = refs[refs_in + num_row :]
+    out_ref, token_ref, slab = refs[refs_in + num_row :]
+    token_ref[...] = jnp.zeros_like(token_ref)
     row = lax.axis_index("row")
     rows = h_refs[0].shape[1]
     for back in range(num_layer):
         for step in range(num_row):
-            start = pl.multiple_of(lax.rem(row - step + num_row, num_row) * rows, rows)
+            start = pl.multiple_of((row ^ step) * rows, rows)
             slab[back, pl.ds(start, rows), :] = h_refs[step][back]
     total = jnp.zeros(out_ref.shape, F32)
     for back in range(num_layer):
@@ -391,9 +405,12 @@
 def multiply(arrays, parts, num_row, num_col, num_layer):
     return pl.pallas_call(
         functools.partial(product_kernel, num_row, num_col, num_layer, len(arrays)),
-        out_shape=jax.ShapeDtypeStruct((arrays[0].shape[-1], LANES), BF16),
+        out_shape=(
+            jax.ShapeDtypeStruct((arrays[0].shape[-1], LANES), BF16),
+            jax.ShapeDtypeStruct((8, LANES), F32),
+        ),
         in_specs=[VMEM] * (num_row + len(arrays)),
-        out_specs=VMEM,
+        out_specs=(VMEM, VMEM),
         scratch_shapes=[pltpu.VMEM((num_layer, num_col * LANES, LANES), BF16)],
         compiler_params=PARAMS,
         cost_estimate=pl.CostEstimate(flops=500_000_000, bytes_accessed=1_000_000, transcendentals=0),
@@ -420,20 +437,22 @@
     )(own, near, far, both)
 
 
-def fold_kernel(core_ref, below_ref, above_ref, out_ref):
+def fold_kernel(core_ref, below_ref, above_ref, after_ref, out_ref):
     out_ref[0:HALO, :] = core_ref[0:HALO, :] + below_ref[...]
     out_ref[HALO : CORE - HALO, :] = core_ref[HALO : CORE - HALO, :]
     out_ref[CORE - HALO : CORE, :] = core_ref[CORE - HALO : CORE, :] + above_ref[...]
 
 
-def fold(core, below, above):
+def fold(core, below, above, after):
     return pl.pallas_call(
         fold_kernel,
         out_shape=jax.ShapeDtypeStruct((CORE, GZ), F32),
-        in_specs=[VMEM, VMEM, VMEM],
+        in_specs=[VMEM] * 4,
         out_specs=VMEM,
+        compiler_params=PARAMS,
+        cost_estimate=pl.CostEstimate(flops=1_000_000, bytes_accessed=400_000, transcendentals=0),
         name="fold",
-    )(core, below, above)
+    )(core, below, above, after)
 
 
 def shifted(value, axis, count, step):
@@ -470,13 +489,15 @@
         arrays = [lax.all_gather(base, ("layer", "col"), axis=0)]
         mine = [pieces[0]] + [shifted(pieces[step], "layer", num_layer, step) for step in range(1, num_layer)]
         mine = jnp.stack(mine)
-    parts = [mine] + [shifted(mine, "row", num_row, step) for step in range(1, num_row)]
+    parts = [mine] + [
+        lax.ppermute(mine, "row", [(i, i ^ step) for i in range(num_row)]) for step in range(1, num_row)
+    ]
     coef, long = weigh_all(arrays, num_col, num_layer)
     core, low, high = collocate(arrays, coef, long, num_col, num_layer)
     below = shifted(high, "row", num_row, 1)
     above = shifted(low, "row", num_row, num_row - 1)
-    product = multiply(arrays, parts, num_row, num_col, num_layer)
-    density = fold(core, below, above).reshape(GX, GY, GZ)
+    product, token = multiply(arrays, parts, num_row, num_col, num_layer)
+    density = fold(core, below, above, token).reshape(GX, GY, GZ)
     return (product, density)
 
 

time: 34.5 us -> 28.6 us (0.83)
  local copies, waits for them, and re-layouts: 5.01 us -> 0.72 us
  starting transfers between devices: 14 us -> 12.9 us
  waiting for transfers between devices: 7.45 us -> 6.79 us
    ppermute x5 -> x2, starting transfers between devices: 9.39 us -> 3.88 us  [shifted(): lax.ppermute(value, axis, [(i, (i + step) % count) for i in range(count)])]
    ppermute x0 -> x3, starting transfers between devices: none -> 4.45 us  [on_device(): lax.ppermute(mine, 'row', [(i, i ^ step) for i in range(num_row)])]
    unnamed x24 -> x4, local copies, waits for them, and re-layouts: 5.01 us -> 0.72 us
    pallas_call x1, Pallas kernels: 1.16 us -> 2.29 us  [prepare(): pl.pallas_call(functools.partial(prepare_kernel, paired), out_shape=outs,...]
    pallas_call x1, Pallas kernels: 1.59 us -> 0.67 us  [fold(): pl.pallas_call(fold_kernel, out_shape=jax.ShapeDtypeStruct((CORE, GZ), F3...]
    ppermute x5 -> x2, waiting for transfers between devices: 1.9 us -> 1.02 us  [shifted(): lax.ppermute(value, axis, [(i, (i + step) % count) for i in range(count)])]
  transfers between devices with their start and end apart: 12 -> 12, of which waited for: 4 -> 4; matrix products, arithmetic and copies ran while one was open for 0% -> 0% of each run, Pallas kernels for 14% -> 15%
where the time goes in v1:
time: 28.6 us; the launch traced here: 28.4 us
  starting transfers between devices  12.9 us (45%)
  Pallas kernels  7.24 us (25%)
  waiting for transfers between devices  6.79 us (24%)
  local copies, waits for them, and re-layouts  0.72 us (3%)
  between operations  0.69 us (2%)
    ppermute x7, waiting for transfers between devices, crossed(): return lax.ppermute(value, ('col', 'layer'), pairs)  5.76 us
    ppermute x7, starting transfers between devices, crossed(): return lax.ppermute(value, ('col', 'layer'), pairs)  4.58 us
    ppermute x3, starting transfers between devices, on_device(): lax.ppermute(mine, 'row', [(i, i ^ step) for i in range(num_row)])  4.45 us
    ppermute x2, starting transfers between devices, shifted(): lax.ppermute(value, axis, [(i, (i + step) % count) for i in range(count)])  3.88 us
    pallas_call x1, Pallas kernels, prepare(): pl.pallas_call(functools.partial(prepare_kernel, paired), out_shape=outs,...  2.29 us
    pallas_call x1, Pallas kernels, collocate(): pl.pallas_call(functools.partial(collocate_kernel, num_col, num_layer, le...  1.67 us
    pallas_call x1, Pallas kernels, weigh_all(): pl.pallas_call(functools.partial(weigh_kernel, num_col, num_layer, len(ar...  1.62 us
    ppermute x2, waiting for transfers between devices, shifted(): lax.ppermute(value, axis, [(i, (i + step) % count) for i in range(count)])  1.02 us
  transfers between devices with their start and end apart: 12, of which 4 were waited for; matrix products, arithmetic and copies ran while one was open for 0% of the time, Pallas kernels for 15%

profile of v1, /device:TPU:0, one launch (start us, length us, event | category | flops | bytes accessed | tf_op | source)
XLA Modules:
  0.0 28.4 jit_solution(2044212968955922175)
XLA Ops:
  0.6 2.3 %prepare.1 = (bf16[208,256]{1,0:T(8,128)(2,1)}, bf16[272,256]{1,0:T(8,128)(2,1)}, bf16[272,256]{1,0:T(8,128)(2,1)}, bf16[64,128]{1,0:T(8,128)(2,1)}) custom-call(bf16[256,128]{1,0:T(8,128)(2,1)} %bitcast.13, s32[4,8]{1,0:T(4,128)} %bitcast.20, bf16[64,512]{1,0:T(8,128)(2,1)} %bitcast.14, s32[2,16]{1,0:T(2,128)} %bitcast.21, s32[8,128]{1,0:T(8,128)} %bitcast.15, ...), custom_call_target="tpu_custom_call" | custom-call | tf_op jit(solution)/shard_map/prepare/pallas_call | solution.py:148
  2.9 3.0 %collective-permute-start.1 = (bf16[272,256]{1,0:T(8,128)(2,1)}, bf16[272,256]{1,0:T(8,128)(2,1)S(1)}, u32[]{:S(2)}, u32[]{:S(2)}) collective-permute-start(bf16[272,256]{1,0:T(8,128)(2,1)} %get-tuple-element.15), channel_id=1, source_target_pairs={{0,2},{1,3},{2,0},{3,1},{4,6},{5,7},{6,4},{7,5},{8,10},{9,11},{10,... | collective-permute-start | bytes 417800 | tf_op jit(solution)/shard_map/ppermute | solution.py:464
  6.0 1.5 %collective-permute-start.3 = (bf16[208,256]{1,0:T(8,128)(2,1)}, bf16[208,256]{1,0:T(8,128)(2,1)S(1)}, u32[]{:S(2)}, u32[]{:S(2)}) collective-permute-start(bf16[208,256]{1,0:T(8,128)(2,1)} %get-tuple-element.13.refs_0_), channel_id=1, source_target_pairs={{0,4},{1,5},{2,6},{3,7},{4,0},{5,1},{6,2},{7,3},{8,12},{9,13},{10,... | collective-permute-start | bytes 319496 | tf_op jit(solution)/shard_map/ppermute | solution.py:464
  7.5 0.0 collective-permute-start.5
  7.5 0.0 collective-permute-start
  7.5 2.5 %collective-permute-done.1.far_ref.refs_2_ = bf16[272,256]{1,0:T(8,128)(2,1)S(1)} collective-permute-done((bf16[272,256]{1,0:T(8,128)(2,1)}, bf16[272,256]{1,0:T(8,128)(2,1)S(1)}, u32[]{:S(2)}, u32[]{:S(2)}) %collective-permute-start.1) | collective-permute-done | bytes 139296 | tf_op jit(solution)/shard_map/ppermute | solution.py:464
  10.0 1.8 %collective-permute-done.3.refs_4_ = bf16[208,256]{1,0:T(8,128)(2,1)S(1)} collective-permute-done((bf16[208,256]{1,0:T(8,128)(2,1)}, bf16[208,256]{1,0:T(8,128)(2,1)S(1)}, u32[]{:S(2)}, u32[]{:S(2)}) %collective-permute-start.3) | collective-permute-done | bytes 106528 | tf_op jit(solution)/shard_map/ppermute | solution.py:464
  11.8 0.0 collective-permute-start.4
  11.8 1.5 %collective-permute-done.5.refs_6_ = bf16[208,256]{1,0:T(8,128)(2,1)S(1)} collective-permute-done((bf16[208,256]{1,0:T(8,128)(2,1)}, bf16[208,256]{1,0:T(8,128)(2,1)S(1)}, u32[]{:S(2)}, u32[]{:S(2)}) %collective-permute-start.5) | collective-permute-done | bytes 106528 | tf_op jit(solution)/shard_map/ppermute | solution.py:464
  13.3 0.0 collective-permute-start.6
  13.3 0.0 copy-start
  13.3 0.7 %copy-done = bf16[64,128]{1,0:T(8,128)(2,1)S(1)} copy-done((bf16[64,128]{1,0:T(8,128)(2,1)S(1)}, bf16[64,128]{1,0:T(8,128)(2,1)}, u32[]{:S(2)}) %copy-start) | copy-done | bytes 16408
  14.0 1.6 %collective-permute-start.7 = (bf16[4,64,128]{2,1,0:T(8,128)(2,1)S(1)}, bf16[4,64,128]{2,1,0:T(8,128)(2,1)S(1)}, u32[]{:S(2)}, u32[]{:S(2)}) collective-permute-start(bf16[4,64,128]{2,1,0:T(8,128)(2,1)S(1)} %stack.1.refs_8_), channel_id=1, source_target_pairs={{0,8},{8,0},{16,24},{24,16},{1,9},{9,1},{17,25},{25,17},{2,10},{10... | collective-permute-start | bytes 196616 | tf_op jit(solution)/shard_map/ppermute | solution.py:493
  15.7 2.6 %collective-permute-start.8 = (bf16[4,64,128]{2,1,0:T(8,128)(2,1)S(1)}, bf16[4,64,128]{2,1,0:T(8,128)(2,1)S(1)}, u32[]{:S(2)}, u32[]{:S(2)}) collective-permute-start(bf16[4,64,128]{2,1,0:T(8,128)(2,1)S(1)} %stack.1.refs_8_), channel_id=1, source_target_pairs={{0,16},{8,24},{16,0},{24,8},{1,17},{9,25},{17,1},{25,9},{2,18},{10... | collective-permute-start | bytes 196616 | tf_op jit(solution)/shard_map/ppermute | solution.py:493
  18.2 0.2 collective-permute-start.9
  18.5 1.6 %weigh.1 = (f32[10,256]{1,0:T(8,128)S(1)}, f32[4,4,256]{2,1,0:T(4,128)S(1)}) custom-call(bf16[208,256]{1,0:T(8,128)(2,1)S(1)} %copy-done.1, bf16[272,256]{1,0:T(8,128)(2,1)S(1)} %collective-permute-done.near_ref.refs_1_, bf16[272,256]{1,0:T(8,128)(2,1)S(1)} %collective-permute-done.1.far_ref.refs_2_, ...), custom_call_target="tpu_custom_call" | custom-call | flops 2000000000 | bytes 1000000 | tf_op jit(solution)/shard_map/weigh/pallas_call | solution.py:280
  20.1 1.7 %collocate.1 = (f32[256,128]{1,0:T(8,128)S(1)}, f32[64,128]{1,0:T(8,128)S(1)}, f32[64,128]{1,0:T(8,128)S(1)}) custom-call(bf16[208,256]{1,0:T(8,128)(2,1)S(1)} %copy-done.1, bf16[272,256]{1,0:T(8,128)(2,1)S(1)} %collective-permute-done.near_ref.refs_1_, bf16[272,256]{1,0:T(8,128)(2,1)S(1)} %collective-permute-done.1.far_ref.refs_2_, ...), custom_call_target="tpu_custom_call" | custom-call | flops 3000000000 | bytes 1000000 | tf_op jit(solution)/shard_map/collocate/pallas_call | solution.py:358
  21.8 0.7 %collective-permute-start.10 = (f32[64,128]{1,0:T(8,128)S(1)}, f32[64,128]{1,0:T(8,128)S(1)}, u32[]{:S(2)}, u32[]{:S(2)}) collective-permute-start(f32[64,128]{1,0:T(8,128)S(1)} %get-tuple-element.21), channel_id=1, source_target_pairs={{0,8},{8,16},{16,24},{24,0},{1,9},{9,17},{17,25},{25,1},{2,10},{10... | collective-permute-start | bytes 98312 | tf_op jit(solution)/shard_map/ppermute | solution.py:459
  22.5 3.1 %collective-permute-start.11 = (f32[64,128]{1,0:T(8,128)S(1)}, f32[64,128]{1,0:T(8,128)S(1)}, u32[]{:S(2)}, u32[]{:S(2)}) collective-permute-start(f32[64,128]{1,0:T(8,128)S(1)} %get-tuple-element.22), channel_id=1, source_target_pairs={{0,24},{8,0},{16,8},{24,16},{1,25},{9,1},{17,9},{25,17},{2,26},{10... | collective-permute-start | bytes 98312 | tf_op jit(solution)/shard_map/ppermute | solution.py:459
  25.7 0.0 collective-permute-done.8.refs_10_
  25.7 0.0 collective-permute-done.9.refs_11_
  25.7 1.0 %multiply.1 = (bf16[256,128]{1,0:T(8,128)(2,1)}, f32[8,128]{1,0:T(8,128)S(1)}) custom-call(bf16[208,256]{1,0:T(8,128)(2,1)S(1)} %copy-done.1, bf16[272,256]{1,0:T(8,128)(2,1)S(1)} %collective-permute-done.near_ref.refs_1_, bf16[272,256]{1,0:T(8,128)(2,1)S(1)} %collective-permute-done.1.far_ref.refs_2_, ...), custom_call_target="tpu_custom_call" | custom-call | flops 500000000 | bytes 1000000 | tf_op jit(solution)/shard_map/multiply/pallas_call | solution.py:406
  26.7 1.0 %collective-permute-done.10.below_ref = f32[64,128]{1,0:T(8,128)S(1)} collective-permute-done((f32[64,128]{1,0:T(8,128)S(1)}, f32[64,128]{1,0:T(8,128)S(1)}, u32[]{:S(2)}, u32[]{:S(2)}) %collective-permute-start.10) | collective-permute-done | bytes 32800 | tf_op jit(solution)/shard_map/ppermute | solution.py:459
  27.7 0.7 %fold.1 = f32[256,128]{1,0:T(8,128)} custom-call(f32[256,128]{1,0:T(8,128)S(1)} %get-tuple-element.20.core_ref, f32[64,128]{1,0:T(8,128)S(1)} %collective-permute-done.10.below_ref, f32[64,128]{1,0:T(8,128)S(1)} %collective-permute-done.11.above_ref, f32[8,128]{1,0:T(8,128)S(1)} %get-tuple-element.23.after_ref), custom_call_target="tpu_custom_call" | custom-call | flops 1000000 | bytes 400000 | tf_op jit(solution)/shard_map/fold/pallas_call | solution.py:447
  (10 shorter events, 0.0 us)
Async XLA Ops:
  2.9 7.0 %collective-permute-start.1 = (bf16[272,256]{1,0:T(8,128)(2,1)}, bf16[272,256]{1,0:T(8,128)(2,1)S(1)}, u32[]{:S(2)}, u32[]{:S(2)}) collective-permute-start(bf16[272,256]{1,0:T(8,128)(2,1)} %get-tuple-element.15), channel_id=1, source_target_pairs={{0,2},{1,3},{2,0},{3,1},{4,6},{5,7},{6,4},{7,5},{8,10},{9,11},{10,... | collective-permute-start | bytes 417800 | tf_op jit(solution)/shard_map/ppermute | solution.py:464
  6.0 5.8 %collective-permute-start.3 = (bf16[208,256]{1,0:T(8,128)(2,1)}, bf16[208,256]{1,0:T(8,128)(2,1)S(1)}, u32[]{:S(2)}, u32[]{:S(2)}) collective-permute-start(bf16[208,256]{1,0:T(8,128)(2,1)} %get-tuple-element.13.refs_0_), channel_id=1, source_target_pairs={{0,4},{1,5},{2,6},{3,7},{4,0},{5,1},{6,2},{7,3},{8,12},{9,13},{10,... | collective-permute-start | bytes 319496 | tf_op jit(solution)/shard_map/ppermute | solution.py:464
  7.5 5.8 %collective-permute-start.5 = (bf16[208,256]{1,0:T(8,128)(2,1)}, bf16[208,256]{1,0:T(8,128)(2,1)S(1)}, u32[]{:S(2)}, u32[]{:S(2)}) collective-permute-start(bf16[208,256]{1,0:T(8,128)(2,1)} %get-tuple-element.13.refs_0_), channel_id=1, source_target_pairs={{0,6},{1,7},{2,4},{3,5},{4,2},{5,3},{6,0},{7,1},{8,14},{9,15},{10,... | collective-permute-start | bytes 319496 | tf_op jit(solution)/shard_map/ppermute | solution.py:464
  7.5 5.8 %collective-permute-start = (bf16[272,256]{1,0:T(8,128)(2,1)}, bf16[272,256]{1,0:T(8,128)(2,1)S(1)}, u32[]{:S(2)}, u32[]{:S(2)}) collective-permute-start(bf16[272,256]{1,0:T(8,128)(2,1)} %get-tuple-element.14), channel_id=1, source_target_pairs={{0,1},{1,0},{2,3},{3,2},{4,5},{5,4},{6,7},{7,6},{8,9},{9,8},{10,11... | collective-permute-start | bytes 417800 | tf_op jit(solution)/shard_map/ppermute | solution.py:464
  10.0 3.3 %collective-permute-start.2 = (bf16[272,256]{1,0:T(8,128)(2,1)S(1)}, bf16[272,256]{1,0:T(8,128)(2,1)S(1)}, u32[]{:S(2)}, u32[]{:S(2)}) collective-permute-start(bf16[272,256]{1,0:T(8,128)(2,1)S(1)} %collective-permute-done.1.far_ref.refs_2_), channel_id=1, source_target_pairs={{0,1},{1,0},{2,3},{3,2},{4,5},{5,4},{6,7},{7,6},{8,9},{9,8},{10,11... | collective-permute-start | bytes 417800 | tf_op jit(solution)/shard_map/ppermute | solution.py:464
  11.8 6.7 %collective-permute-start.4 = (bf16[208,256]{1,0:T(8,128)(2,1)S(1)}, bf16[208,256]{1,0:T(8,128)(2,1)S(1)}, u32[]{:S(2)}, u32[]{:S(2)}) collective-permute-start(bf16[208,256]{1,0:T(8,128)(2,1)S(1)} %collective-permute-done.3.refs_4_), channel_id=1, source_target_pairs={{0,1},{1,0},{2,3},{3,2},{4,5},{5,4},{6,7},{7,6},{8,9},{9,8},{10,11... | collective-permute-start | bytes 319496 | tf_op jit(solution)/shard_map/ppermute | solution.py:464
  13.3 5.2 %collective-permute-start.6 = (bf16[208,256]{1,0:T(8,128)(2,1)S(1)}, bf16[208,256]{1,0:T(8,128)(2,1)S(1)}, u32[]{:S(2)}, u32[]{:S(2)}) collective-permute-start(bf16[208,256]{1,0:T(8,128)(2,1)S(1)} %collective-permute-done.5.refs_6_), channel_id=1, source_target_pairs={{0,1},{1,0},{2,3},{3,2},{4,5},{5,4},{6,7},{7,6},{8,9},{9,8},{10,11... | collective-permute-start | bytes 319496 | tf_op jit(solution)/shard_map/ppermute | solution.py:464
  13.3 0.7 %copy-start = (bf16[64,128]{1,0:T(8,128)(2,1)S(1)}, bf16[64,128]{1,0:T(8,128)(2,1)}, u32[]{:S(2)}) copy-start(bf16[64,128]{1,0:T(8,128)(2,1)} %get-tuple-element.16.own_ref) | copy-start | bytes 49156
  14.0 4.5 %copy-start.1 = (bf16[208,256]{1,0:T(8,128)(2,1)S(1)}, bf16[208,256]{1,0:T(8,128)(2,1)}, u32[]{:S(2)}) copy-start(bf16[208,256]{1,0:T(8,128)(2,1)} %get-tuple-element.13.refs_0_) | copy-start | bytes 319492
  14.0 11.6 %collective-permute-start.7 = (bf16[4,64,128]{2,1,0:T(8,128)(2,1)S(1)}, bf16[4,64,128]{2,1,0:T(8,128)(2,1)S(1)}, u32[]{:S(2)}, u32[]{:S(2)}) collective-permute-start(bf16[4,64,128]{2,1,0:T(8,128)(2,1)S(1)} %stack.1.refs_8_), channel_id=1, source_target_pairs={{0,8},{8,0},{16,24},{24,16},{1,9},{9,1},{17,25},{25,17},{2,10},{10... | collective-permute-start | bytes 196616 | tf_op jit(solution)/shard_map/ppermute | solution.py:493
  15.7 10.0 %collective-permute-start.8 = (bf16[4,64,128]{2,1,0:T(8,128)(2,1)S(1)}, bf16[4,64,128]{2,1,0:T(8,128)(2,1)S(1)}, u32[]{:S(2)}, u32[]{:S(2)}) collective-permute-start(bf16[4,64,128]{2,1,0:T(8,128)(2,1)S(1)} %stack.1.refs_8_), channel_id=1, source_target_pairs={{0,16},{8,24},{16,0},{24,8},{1,17},{9,25},{17,1},{25,9},{2,18},{10... | collective-permute-start | bytes 196616 | tf_op jit(solution)/shard_map/ppermute | solution.py:493
  18.2 7.4 %collective-permute-start.9 = (bf16[4,64,128]{2,1,0:T(8,128)(2,1)S(1)}, bf16[4,64,128]{2,1,0:T(8,128)(2,1)S(1)}, u32[]{:S(2)}, u32[]{:S(2)}) collective-permute-start(bf16[4,64,128]{2,1,0:T(8,128)(2,1)S(1)} %stack.1.refs_8_), channel_id=1, source_target_pairs={{0,24},{8,16},{16,8},{24,0},{1,25},{9,17},{17,9},{25,1},{2,26},{10... | collective-permute-start | bytes 196616 | tf_op jit(solution)/shard_map/ppermute | solution.py:493
  21.8 5.9 %collective-permute-start.10 = (f32[64,128]{1,0:T(8,128)S(1)}, f32[64,128]{1,0:T(8,128)S(1)}, u32[]{:S(2)}, u32[]{:S(2)}) collective-permute-start(f32[64,128]{1,0:T(8,128)S(1)} %get-tuple-element.21), channel_id=1, source_target_pairs={{0,8},{8,16},{16,24},{24,0},{1,9},{9,17},{17,25},{25,1},{2,10},{10... | collective-permute-start | bytes 98312 | tf_op jit(solution)/shard_map/ppermute | solution.py:459
  22.5 5.2 %collective-permute-start.11 = (f32[64,128]{1,0:T(8,128)S(1)}, f32[64,128]{1,0:T(8,128)S(1)}, u32[]{:S(2)}, u32[]{:S(2)}) collective-permute-start(f32[64,128]{1,0:T(8,128)S(1)} %get-tuple-element.22), channel_id=1, source_target_pairs={{0,24},{8,0},{16,8},{24,16},{1,25},{9,1},{17,9},{25,17},{2,26},{10... | collective-permute-start | bytes 98312 | tf_op jit(solution)/shard_map/ppermute | solution.py:459

commit v2 on v1

--- a/solution.py
+++ b/solution.py
@@ -63,7 +63,7 @@
     return jnp.where(flags > 0, within + earlier - 1.0, -1.0), count
 
 
-def prepare_kernel(paired, *refs):
+def prepare_kernel(*refs):
     sources, outs, refs = refs[:9], refs[9:-14], refs[-14:]
     landed, (tmp, fields, matrix, onehot, sems) = refs[:9], refs[9:]
     copies = [pltpu.make_async_copy(src, dst, sems.at[at]) for at, (src, dst) in enumerate(zip(sources, landed))]
@@ -72,8 +72,6 @@
     for copy in copies:
         copy.wait()
     p_ref, pm_ref, h_ref, hm_ref, row_ref, col_ref, cell_ref, expo_ref, pref_ref = landed
-    layer = lax.axis_index("layer")
-    count = lax.axis_size("layer")
     band = p_ref.shape[0]
     for block in range(band // BS):
         rows = pl.ds(block * BS, BS)
@@ -109,44 +107,24 @@
     over = jnp.where(jnp.max(many, axis=0, keepdims=True) > LANES, 1.0, 0.0)
     over = jnp.concatenate([over, over], axis=1)
     listed = jnp.where(iota(listed.shape, 0) == FLAG, over, listed).astype(BF16)
-    copies = outs[:3] if paired else outs[:1]
-    for out in copies:
-        out[0:LANES, :] = turned
-        for pair in range(PAIRS):
-            out[LANES + 16 * pair : LANES + 16 * pair + 16, :] = matrix[:, pair * UNIT : pair * UNIT + UNIT]
-        out[LANES + 16 * PAIRS : BASE, :] = listed
-
-    def piece(chunk):
-        pieces = LANES // BS
-        out = []
+    out, tile_ref = outs
+    out[0:LANES, :] = turned
+    for pair in range(PAIRS):
+        out[LANES + 16 * pair : LANES + 16 * pair + 16, :] = matrix[:, pair * UNIT : pair * UNIT + UNIT]
+    out[LANES + 16 * PAIRS : BASE, :] = listed
+    pieces = LANES // BS
+    for chunk in range(h_ref.shape[1] // LANES):
+        cols = pl.ds(chunk * LANES, LANES)
         for block in range(h_ref.shape[0] // BS):
             rows = pl.ds(block * BS, BS)
             bits = [hm_ref[block, chunk * pieces + at] for at in range(pieces)]
-            value = h_ref[rows, pl.ds(pl.multiple_of(chunk * LANES, LANES), LANES)]
-            out.append(masked(value, bits).astype(BF16))
-        return jnp.concatenate(out, axis=0)
-
-    if paired:
-        outs[1][BASE:, 0:LANES] = piece(layer ^ 2)
-        outs[1][BASE:, LANES:UNIT] = piece(layer ^ 3)
-        outs[2][BASE:, 0:LANES] = piece(layer ^ 1)
-        outs[2][BASE:, LANES:UNIT] = jnp.zeros((h_ref.shape[0], LANES), BF16)
-        outs[3][...] = piece(layer)
-    else:
-        for back in range(h_ref.shape[1] // LANES):
-            outs[1][back] = piece(lax.rem(layer + back, count))
-
-
-def prepare(paired, p, p_mask, h, h_mask, *gauss):
-    band = p.shape[0]
-    base = jax.ShapeDtypeStruct((BASE, band), BF16)
-    tall = jax.ShapeDtypeStruct((BASE + h.shape[0], band), BF16)
-    if paired:
-        outs = (base, tall, tall, jax.ShapeDtypeStruct((h.shape[0], LANES), BF16))
-    else:
-        outs = (base, jax.ShapeDtypeStruct((h.shape[1] // LANES, h.shape[0], LANES), BF16))
+            tile_ref[rows, cols] = masked(h_ref[rows, cols], bits).astype(BF16)
+
+
+def prepare(p, p_mask, h, h_mask, *gauss):
+    outs = (jax.ShapeDtypeStruct((BASE, p.shape[0]), BF16), jax.ShapeDtypeStruct(h.shape, BF16))
     return pl.pallas_call(
-        functools.partial(prepare_kernel, paired),
+        prepare_kernel,
         out_shape=outs,
         in_specs=[HBM] * 9,
         out_specs=(VMEM,) * len(outs),
@@ -251,69 +229,41 @@
     return (tile[9:10, :] + tile[10:11, :] + tile[11:12, :]) * value
 
 
-def weigh_kernel(num_col, num_layer, refs_in, *refs):
-    blocks = Blocks(refs[:refs_in], num_col, num_layer)
-    coef_ref, long_ref, whole = refs[refs_in:]
-    for index in range(blocks.total):
-        whole[index * LANES : index * LANES + LANES, :] = blocks.matrix(index)
-    over = blocks.over()
-    for at, (which, pair) in enumerate(blocks.units()):
-        coef = weigh(blocks, whole, blocks.unit(which, pair))
-        if pair == PAIRS:
-            coef = jnp.where(over > 0, 0.0, coef)
-        coef_ref[at : at + 1, :] = coef
-
-    @pl.when(jnp.max(over) > 0)
-    def _():
-        for at, (which, side) in enumerate(blocks.long_steps()):
-
-            def step(pair, carry):
-                long_ref[at, pl.ds(pair, 1), :] = weigh(blocks, whole, blocks.tile(which, side, pair))
-                return carry
-
-            lax.fori_loop(0, PAIRS, step, 0)
-
-
-def weigh_all(arrays, num_col, num_layer):
-    ways = 2 if num_col == 2 else 3
-    band = arrays[0].shape[-1]
-    return pl.pallas_call(
-        functools.partial(weigh_kernel, num_col, num_layer, len(arrays)),
-        out_shape=(
-            jax.ShapeDtypeStruct((ways * (PAIRS + 1), UNIT), F32),
-            jax.ShapeDtypeStruct((ways * 2, PAIRS, UNIT), F32),
-        ),
-        in_specs=[VMEM] * len(arrays),
-        out_specs=(VMEM, VMEM),
-        scratch_shapes=[pltpu.VMEM((num_col * num_layer * LANES, band), BF16)],
-        compiler_params=PARAMS,
-        cost_estimate=pl.CostEstimate(flops=2_000_000_000, bytes_accessed=1_000_000, transcendentals=0),
-        name="weigh",
-    )(*arrays)
-
-
 def bell(dist, expo):
     square = dist * dist
     return jnp.where(square < (R + 0.5) ** 2, jnp.exp(-expo * square), 0.0)
 
 
-def spread(blocks, tile, which, lift, coef, at, planeh, planel, depth):
-    expo = tile[6:7, :] + tile[7:8, :] + tile[8:9, :]
+RIM_X = tuple(range(R)) + tuple(range(GX + R, GX + 2 * R))
+CORE_X = tuple(range(R, GX + R))
+ALL_X = tuple(range(GX + 2 * R))
+
+
+def decay(tile):
+    return tile[6:7, :] + tile[7:8, :] + tile[8:9, :]
+
+
+def set_planes(blocks, tile, which, places, at, planeh, planel):
+    expo = decay(tile)
     ex = bell(iota((GX + 2 * R, UNIT), 0) - float(R) - tile[3:4, :], expo)
     dy = iota((GY, UNIT), 0) - tile[4:5, :] - float(blocks.col_shifts[which] * GY)
     if blocks.num_col == 2 and which == 1:
         dy = jnp.where(dy < -float(GY), dy + 2.0 * GY, dy)
     ey = bell(dy, expo)
-    ez = bell(iota((GZ, UNIT), 0) - tile[5:6, :] - lift, expo) * coef
+    lanes = pl.ds(at * UNIT, UNIT)
+    for spot, x in enumerate(places):
+        plane = ex[x : x + 1, :] * ey
+        plane_hi = plane.astype(BF16)
+        planeh[spot * GY : spot * GY + GY, lanes] = plane_hi
+        planel[spot * GY : spot * GY + GY, lanes] = (plane - plane_hi.astype(F32)).astype(BF16)
+
+
+def set_depth(tile, lift, coef, at, depth):
+    ez = bell(iota((GZ, UNIT), 0) - tile[5:6, :] - lift, decay(tile)) * coef
     lanes = pl.ds(at * UNIT, UNIT)
     ez_hi = ez.astype(BF16)
     depth[0:GZ, lanes] = ez_hi
     depth[GZ : 2 * GZ, lanes] = (ez - ez_hi.astype(F32)).astype(BF16)
-    for x in range(GX + 2 * R):
-        plane = ex[x : x + 1, :] * ey
-        plane_hi = plane.astype(BF16)
-        planeh[x * GY : x * GY + GY, lanes] = plane_hi
-        planel[x * GY : x * GY + GY, lanes] = (plane - plane_hi.astype(F32)).astype(BF16)
 
 
 def summed(planeh, planel, depth):
@@ -322,119 +272,169 @@
     return first[:, 0:GZ] + first[:, GZ : 2 * GZ] + second
 
 
-def collocate_kernel(num_col, num_layer, refs_in, *refs):
+def rims_kernel(num_col, num_layer, refs_in, *refs):
     blocks = Blocks(refs[:refs_in], num_col, num_layer)
-    coef_ref, long_ref, core_ref, low_ref, high_ref, planeh, planel, depth, acc = refs[refs_in:]
+    low_ref, high_ref, depth, extra, whole, planeh, planel, longh, longl, long_depth, acc = refs[refs_in:]
+    for index in range(blocks.total):
+        whole[index * LANES : index * LANES + LANES, :] = blocks.matrix(index)
+    over = blocks.over()
     for at, (which, pair) in enumerate(blocks.units()):
-        spread(
-            blocks, blocks.unit(which, pair), which, blocks.lifts(pair), coef_ref[at : at + 1, :], at,
-            planeh, planel, depth,
-        )
+        tile = blocks.unit(which, pair)
+        set_planes(blocks, tile, which, RIM_X, at, planeh, planel)
+        coef = weigh(blocks, whole, tile)
+        if pair == PAIRS:
+            coef = jnp.where(over > 0, 0.0, coef)
+        set_depth(tile, blocks.lifts(pair), coef, at, depth)
     total = summed(planeh[...], planel[...], depth[...])
     low_ref[...] = total[0:HALO, :]
-    core_ref[...] = total[HALO : HALO + CORE, :]
-    high_ref[...] = total[HALO + CORE : FULL, :]
-
-    @pl.when(jnp.max(blocks.over()) > 0)
+    high_ref[...] = total[HALO:, :]
+
+    @pl.when(jnp.max(over) > 0)
     def _():
         acc[...] = jnp.zeros_like(acc)
-        for at, (which, side) in enumerate(blocks.long_steps()):
+        for which, side in blocks.long_steps():
 
             def step(pair, carry):
+                tile = blocks.tile(which, side, pair)
                 lift = blocks.side_shift(side) * float(GZ)
-                coef = long_ref[at, pl.ds(pair, 1), :]
-                spread(blocks, blocks.tile(which, side, pair), which, lift, coef, 0, planeh, planel, depth)
-                acc[...] += summed(planeh[:, 0:UNIT], planel[:, 0:UNIT], depth[:, 0:UNIT])
+                set_planes(blocks, tile, which, ALL_X, 0, longh, longl)
+                set_depth(tile, lift, weigh(blocks, whole, tile), 0, long_depth)
+                acc[...] += summed(longh[...], longl[...], long_depth[...])
                 return carry
 
             lax.fori_loop(0, PAIRS, step, 0)
         low_ref[...] += acc[0:HALO, :]
-        core_ref[...] += acc[HALO : HALO + CORE, :]
+        extra[...] = acc[HALO : HALO + CORE, :]
         high_ref[...] += acc[HALO + CORE : FULL, :]
 
 
-def collocate(arrays, coef, long, num_col, num_layer):
-    gaussians = coef.shape[0] * UNIT
+def rims(arrays, num_col, num_layer):
+    gaussians = (2 if num_col == 2 else 3) * (PAIRS + 1) * UNIT
     return pl.pallas_call(
-        functools.partial(collocate_kernel, num_col, num_layer, len(arrays)),
+        functools.partial(rims_kernel, num_col, num_layer, len(arrays)),
         out_shape=(
-            jax.ShapeDtypeStruct((CORE, GZ), F32),
             jax.ShapeDtypeStruct((HALO, GZ), F32),
             jax.ShapeDtypeStruct((HALO, GZ), F32),
+            jax.ShapeDtypeStruct((2 * GZ, gaussians), BF16),
+            jax.ShapeDtypeStruct((CORE, GZ), F32),
         ),
-        in_specs=[VMEM] * (len(arrays) + 2),
-        out_specs=(VMEM, VMEM, VMEM),
+        in_specs=[VMEM] * len(arrays),
+        out_specs=(VMEM,) * 4,
         scratch_shapes=[
-            pltpu.VMEM((FULL, gaussians), BF16),
-            pltpu.VMEM((FULL, gaussians), BF16),
-            pltpu.VMEM((2 * GZ, gaussians), BF16),
+            pltpu.VMEM((num_col * num_layer * LANES, arrays[0].shape[-1]), BF16),
+            pltpu.VMEM((2 * HALO, gaussians), BF16),
+            pltpu.VMEM((2 * HALO, gaussians), BF16),
+            pltpu.VMEM((FULL, UNIT), BF16),
+            pltpu.VMEM((FULL, UNIT), BF16),
+            pltpu.VMEM((2 * GZ, UNIT), BF16),
             pltpu.VMEM((FULL, GZ), F32),
         ],
         compiler_params=PARAMS,
         cost_estimate=pl.CostEstimate(flops=3_000_000_000, bytes_accessed=1_000_000, transcendentals=0),
-        name="collocate",
-    )(*arrays, coef, long)
-
-
-def product_kernel(num_row, num_col, num_layer, refs_in, *refs):
+        name="rims",
+    )(*arrays)
+
+
+def core_kernel(num_col, num_layer, refs_in, *refs):
     blocks = Blocks(refs[:refs_in], num_col, num_layer)
-    h_refs = refs[refs_in : refs_in + num_row]
-    out_ref, token_ref, slab = refs[refs_in + num_row :]
+    depth, extra, core_ref, planeh, planel = refs[refs_in:]
+    for at, (which, pair) in enumerate(blocks.units()):
+        set_planes(blocks, blocks.unit(which, pair), which, CORE_X, at, planeh, planel)
+    core_ref[...] = summed(planeh[...], planel[...], depth[...])
+
+    @pl.when(jnp.max(blocks.over()) > 0)
+    def _():
+        core_ref[...] += extra[...]
+
+
+def core_part(arrays, depth, extra, num_col, num_layer):
+    gaussians = depth.shape[1]
+    return pl.pallas_call(
+        functools.partial(core_kernel, num_col, num_layer, len(arrays)),
+        out_shape=jax.ShapeDtypeStruct((CORE, GZ), F32),
+        in_specs=[VMEM] * (len(arrays) + 2),
+        out_specs=VMEM,
+        scratch_shapes=[pltpu.VMEM((CORE, gaussians), BF16), pltpu.VMEM((CORE, gaussians), BF16)],
+        compiler_params=PARAMS,
+        cost_estimate=pl.CostEstimate(flops=1_500_000_000, bytes_accessed=1_000_000, transcendentals=0),
+        name="core",
+    )(*arrays, depth, extra)
+
+
+def cut_kernel(paired, num_row, own_hbm, *refs):
+    tiles, outs, (own, sem) = refs[: num_row - 1], refs[num_row:-2], refs[-2:]
+    copy = pltpu.make_async_copy(own_hbm, own, sem)
+    copy.start()
+    row, layer = lax.axis_index("row"), lax.axis_index("layer")
+    count = lax.axis_size("layer")
+    rows = own.shape[0]
+
+    def place(tile, step):
+        start = pl.multiple_of((row ^ step) * rows, rows)
+        for back in range(count):
+            chunk = (layer ^ back) if paired else lax.rem(layer + back, count)
+            value = tile[:, pl.ds(pl.multiple_of(chunk * LANES, LANES), LANES)]
+            if paired and back >= 2:
+                outs[2][back - 2, pl.ds(start, rows), :] = value
+            else:
+                outs[back][pl.ds(start, rows), :] = value
+
+    for step in range(1, num_row):
+        place(tiles[step - 1], step)
+    copy.wait()
+    place(own, 0)
+
+
+def cut(paired, own, tiles, after, num_layer):
+    num_row = len(tiles) + 1
+    piece = jax.ShapeDtypeStruct((num_row * own.shape[0], LANES), BF16)
+    both = jax.ShapeDtypeStruct((2, num_row * own.shape[0], LANES), BF16)
+    outs = (piece, piece, both) if paired else (piece,) * num_layer
+    return pl.pallas_call(
+        functools.partial(cut_kernel, paired, num_row),
+        out_shape=outs,
+        in_specs=[HBM] + [VMEM] * num_row,
+        out_specs=(VMEM,) * len(outs),
+        scratch_shapes=[pltpu.VMEM(own.shape, BF16), pltpu.SemaphoreType.DMA(())],
+        compiler_params=PARAMS,
+        cost_estimate=pl.CostEstimate(flops=100_000_000, bytes_accessed=500_000, transcendentals=0),
+        name="cut",
+    )(own, *tiles, after)
+
+
+def product_kernel(num_col, num_layer, refs_in, *refs):
+    blocks = Blocks(refs[:refs_in], num_col, num_layer)
+    slabs = refs[refs_in:-2]
+    out_ref, token_ref = refs[-2:]
     token_ref[...] = jnp.zeros_like(token_ref)
-    row = lax.axis_index("row")
-    rows = h_refs[0].shape[1]
-    for back in range(num_layer):
-        for step in range(num_row):
-            start = pl.multiple_of((row ^ step) * rows, rows)
-            slab[back, pl.ds(start, rows), :] = h_refs[step][back]
     total = jnp.zeros(out_ref.shape, F32)
     for back in range(num_layer):
         for piece in range(num_col):
             if blocks.paired:
                 left = blocks.matrix(piece * 4 + back)
                 start = pl.multiple_of((blocks.col ^ piece) * LANES, LANES)
+                right = slabs[back][pl.ds(start, LANES), :] if back < 2 else slabs[back][back - 2, pl.ds(start, LANES), :]
             else:
                 source = lax.rem(blocks.layer - back + num_layer, num_layer)
                 left = blocks.slab(source, piece)
-                start = piece * LANES
-            right = slab[back, pl.ds(start, LANES), :]
+                right = slabs[back][piece * LANES : piece * LANES + LANES, :]
             total += lax.dot_general(left, right, TN, preferred_element_type=F32)
     out_ref[...] = total.astype(BF16)
 
 
-def multiply(arrays, parts, num_row, num_col, num_layer):
+def multiply(arrays, slabs, num_col, num_layer):
     return pl.pallas_call(
-        functools.partial(product_kernel, num_row, num_col, num_layer, len(arrays)),
+        functools.partial(product_kernel, num_col, num_layer, len(arrays)),
         out_shape=(
             jax.ShapeDtypeStruct((arrays[0].shape[-1], LANES), BF16),
             jax.ShapeDtypeStruct((8, LANES), F32),
         ),
-        in_specs=[VMEM] * (num_row + len(arrays)),
+        in_specs=[VMEM] * (num_layer + len(arrays)),
         out_specs=(VMEM, VMEM),
-        scratch_shapes=[pltpu.VMEM((num_layer, num_col * LANES, LANES), BF16)],
         compiler_params=PARAMS,
         cost_estimate=pl.CostEstimate(flops=500_000_000, bytes_accessed=1_000_000, transcendentals=0),
         name="multiply",
-    )(*arrays, *parts)
-
-
-def stack_kernel(rows, own_ref, near_ref, far_ref, both_ref, out_ref):
-    out_ref[0] = own_ref[...]
-    out_ref[1] = near_ref[BASE:, 0:LANES]
-    out_ref[2] = far_ref[BASE:, 0:LANES]
-    out_ref[3] = both_ref[BASE:, LANES:UNIT]
-
-
-def stack(own, near, far, both):
-    rows = own.shape[0]
-    return pl.pallas_call(
-        functools.partial(stack_kernel, rows),
-        out_shape=jax.ShapeDtypeStruct((4, rows, LANES), BF16),
-        in_specs=[VMEM] * 4,
-        out_specs=VMEM,
-        compiler_params=PARAMS,
-        name="stack",
-    )(own, near, far, both)
+    )(*arrays, *slabs)
 
 
 def fold_kernel(core_ref, below_ref, above_ref, after_ref, out_ref):
@@ -464,11 +464,11 @@
     return lax.ppermute(value, ("col", "layer"), pairs)
 
 
-def gather_paired(base, tall_y, tall_core):
+def gather_paired(base):
     got_x = crossed(base, 1, 0)
-    got_y = crossed(tall_y, 0, 2)
+    got_y = crossed(base, 0, 2)
     got_xy = crossed(base, 1, 2)
-    near = crossed(tall_core, 0, 1)
+    near = crossed(base, 0, 1)
     near_x = crossed(got_x, 0, 1)
     near_y = crossed(got_y, 0, 1)
     near_xy = crossed(got_xy, 0, 1)
@@ -479,24 +479,20 @@
     num_row, num_col, num_layer = (lax.axis_size(axis) for axis in ("row", "col", "layer"))
     paired = num_col == 2 and num_layer == 4
     flat = [x.reshape(8, LANES) for x in (gauss_row, gauss_col, gauss_cell, gauss_expo, gauss_pref)]
-    made = prepare(paired, p_slabs[0], p_mask[0].T, h_slabs[0], h_mask[0], *flat)
+    base, tile = prepare(p_slabs[0], p_mask[0].T, h_slabs[0], h_mask[0], *flat)
+    arrays = gather_paired(base) if paired else [lax.all_gather(base, ("layer", "col"), axis=0)]
+    tiles = [lax.ppermute(tile, "row", [(i, i ^ step) for i in range(num_row)]) for step in range(1, num_row)]
+    low, high, depth, extra = rims(arrays, num_col, num_layer)
+    parts = cut(paired, tile, tiles, low, num_layer)
     if paired:
-        base, tall_y, tall_core, own = made
-        arrays = gather_paired(base, tall_y, tall_core)
-        mine = stack(own, arrays[1], arrays[2], arrays[3])
+        far = crossed(parts[2], 0, 2)
+        slabs = [parts[0], crossed(parts[1], 0, 1), far, crossed(far, 0, 1)]
     else:
-        base, pieces = made
-        arrays = [lax.all_gather(base, ("layer", "col"), axis=0)]
-        mine = [pieces[0]] + [shifted(pieces[step], "layer", num_layer, step) for step in range(1, num_layer)]
-        mine = jnp.stack(mine)
-    parts = [mine] + [
-        lax.ppermute(mine, "row", [(i, i ^ step) for i in range(num_row)]) for step in range(1, num_row)
-    ]
-    coef, long = weigh_all(arrays, num_col, num_layer)
-    core, low, high = collocate(arrays, coef, long, num_col, num_layer)
+        slabs = [parts[0]] + [shifted(parts[step], "layer", num_layer, step) for step in range(1, num_layer)]
     below = shifted(high, "row", num_row, 1)
     above = shifted(low, "row", num_row, num_row - 1)
-    product, token = multiply(arrays, parts, num_row, num_col, num_layer)
+    core = core_part(arrays, depth, extra, num_col, num_layer)
+    product, token = multiply(arrays, slabs, num_col, num_layer)
     density = fold(core, below, above, token).reshape(GX, GY, GZ)
     return (product, density)
 

time: 28.6 us -> 34 us (1.19)
  waiting for transfers between devices: 6.79 us -> 12.4 us
  starting transfers between devices: 12.9 us -> 12.5 us
    ppermute x3, waiting for transfers between devices: 0.01 us -> 2.8 us  [on_device(): lax.ppermute(tile, 'row', [(i, i ^ step) for i in range(num_row)])]
    ppermute x7 -> x10, waiting for transfers between devices: 5.76 us -> 7.65 us  [crossed(): return lax.ppermute(value, ('col', 'layer'), pairs)]
    ppermute x2, starting transfers between devices: 3.88 us -> 2.41 us  [shifted(): lax.ppermute(value, axis, [(i, (i + step) % count) for i in range(count)])]
    ppermute x7 -> x10, starting transfers between devices: 4.58 us -> 5.75 us  [crossed(): return lax.ppermute(value, ('col', 'layer'), pairs)]
    ppermute x2, waiting for transfers between devices: 1.02 us -> 1.93 us  [shifted(): lax.ppermute(value, axis, [(i, (i + step) % count) for i in range(count)])]
    unnamed x4 -> x6, local copies, waits for them, and re-layouts: 0.72 us -> 0.9 us
  transfers between devices with their start and end apart: 12 -> 15, of which waited for: 4 -> 8; matrix products, arithmetic and copies ran while one was open for 0% -> 0% of each run, Pallas kernels for 15% -> 13%
where the time goes in v2:
time: 34 us; the launch traced here: 33.8 us
  starting transfers between devices  12.5 us (37%)
  waiting for transfers between devices  12.4 us (36%)
  Pallas kernels  7.26 us (21%)
  local copies, waits for them, and re-layouts  0.9 us (3%)
  between operations  0.69 us (2%)
    ppermute x10, waiting for transfers between devices, crossed(): return lax.ppermute(value, ('col', 'layer'), pairs)  7.65 us
    ppermute x10, starting transfers between devices, crossed(): return lax.ppermute(value, ('col', 'layer'), pairs)  5.75 us
    ppermute x3, starting transfers between devices, on_device(): lax.ppermute(tile, 'row', [(i, i ^ step) for i in range(num_row)])  4.39 us
    ppermute x3, waiting for transfers between devices, on_device(): lax.ppermute(tile, 'row', [(i, i ^ step) for i in range(num_row)])  2.8 us
    ppermute x2, starting transfers between devices, shifted(): lax.ppermute(value, axis, [(i, (i + step) % count) for i in range(count)])  2.41 us
    pallas_call x1, Pallas kernels, rims(): pl.pallas_call(functools.partial(rims_kernel, num_col, num_layer, len(arr...  2.39 us
    pallas_call x1, Pallas kernels, prepare(): pl.pallas_call(prepare_kernel, out_shape=outs, in_specs=[HBM] * 9, out_sp...  2.19 us
    ppermute x2, waiting for transfers between devices, shifted(): lax.ppermute(value, axis, [(i, (i + step) % count) for i in range(count)])  1.93 us
  transfers between devices with their start and end apart: 15, of which 8 were waited for; matrix products, arithmetic and copies ran while one was open for 0% of the time, Pallas kernels for 13%

profile of v2, /device:TPU:0, one launch (start us, length us, event | category | flops | bytes accessed | tf_op | source)
XLA Modules:
  0.0 33.8 jit_solution(7355887352952695710)
XLA Ops:
  0.6 2.2 %prepare.1 = (bf16[208,256]{1,0:T(8,128)(2,1)}, bf16[64,512]{1,0:T(8,128)(2,1)}) custom-call(bf16[256,128]{1,0:T(8,128)(2,1)} %bitcast.13, s32[4,8]{1,0:T(4,128)} %bitcast.20, bf16[64,512]{1,0:T(8,128)(2,1)} %bitcast.14, s32[2,16]{1,0:T(2,128)} %bitcast.21, s32[8,128]{1,0:T(8,128)} %bitcast.15, s32[8,128]{1,0:T(8,128)} %bitcast.16, s32[8,128]{1,0:T(8,128)} %bitcast.17, ...), custom_call_target="tpu_custom_call" | custom-call | tf_op jit(solution)/shard_map/prepare/pallas_call | solution.py:126
  2.8 3.0 %collective-permute-start.1 = (bf16[208,256]{1,0:T(8,128)(2,1)}, bf16[208,256]{1,0:T(8,128)(2,1)S(1)}, u32[]{:S(2)}, u32[]{:S(2)}) collective-permute-start(bf16[208,256]{1,0:T(8,128)(2,1)} %get-tuple-element.13.refs_0_), channel_id=1, source_target_pairs={{0,2},{1,3},{2,0},{3,1},{4,6},{5,7},{6,4},{7,5},{8,10},{9,11},{10,... | collective-permute-start | bytes 319496 | tf_op jit(solution)/shard_map/ppermute | solution.py:464
  5.9 1.5 %collective-permute-start.3 = (bf16[208,256]{1,0:T(8,128)(2,1)}, bf16[208,256]{1,0:T(8,128)(2,1)S(1)}, u32[]{:S(2)}, u32[]{:S(2)}) collective-permute-start(bf16[208,256]{1,0:T(8,128)(2,1)} %get-tuple-element.13.refs_0_), channel_id=1, source_target_pairs={{0,4},{1,5},{2,6},{3,7},{4,0},{5,1},{6,2},{7,3},{8,12},{9,13},{10,... | collective-permute-start | bytes 319496 | tf_op jit(solution)/shard_map/ppermute | solution.py:464
  7.4 0.0 collective-permute-start.5
  7.4 0.0 collective-permute-start
  7.4 1.6 %collective-permute-done.1.refs_2_ = bf16[208,256]{1,0:T(8,128)(2,1)S(1)} collective-permute-done((bf16[208,256]{1,0:T(8,128)(2,1)}, bf16[208,256]{1,0:T(8,128)(2,1)S(1)}, u32[]{:S(2)}, u32[]{:S(2)}) %collective-permute-start.1) | collective-permute-done | bytes 106528 | tf_op jit(solution)/shard_map/ppermute | solution.py:464
  9.1 2.6 %collective-permute-done.3.refs_4_ = bf16[208,256]{1,0:T(8,128)(2,1)S(1)} collective-permute-done((bf16[208,256]{1,0:T(8,128)(2,1)}, bf16[208,256]{1,0:T(8,128)(2,1)S(1)}, u32[]{:S(2)}, u32[]{:S(2)}) %collective-permute-start.3) | collective-permute-done | bytes 106528 | tf_op jit(solution)/shard_map/ppermute | solution.py:464
  11.7 1.5 %collective-permute-done.5.refs_6_ = bf16[208,256]{1,0:T(8,128)(2,1)S(1)} collective-permute-done((bf16[208,256]{1,0:T(8,128)(2,1)}, bf16[208,256]{1,0:T(8,128)(2,1)S(1)}, u32[]{:S(2)}, u32[]{:S(2)}) %collective-permute-start.5) | collective-permute-done | bytes 106528 | tf_op jit(solution)/shard_map/ppermute | solution.py:464
  13.2 1.6 %collective-permute-start.7 = (bf16[64,512]{1,0:T(8,128)(2,1)}, bf16[64,512]{1,0:T(8,128)(2,1)S(1)}, u32[]{:S(2)}, u32[]{:S(2)}) collective-permute-start(bf16[64,512]{1,0:T(8,128)(2,1)} %get-tuple-element.14.own_hbm), channel_id=1, source_target_pairs={{0,8},{8,0},{16,24},{24,16},{1,9},{9,1},{17,25},{25,17},{2,10},{10... | collective-permute-start | bytes 196616 | tf_op jit(solution)/shard_map/ppermute | solution.py:484
  14.8 2.6 %collective-permute-start.8 = (bf16[64,512]{1,0:T(8,128)(2,1)}, bf16[64,512]{1,0:T(8,128)(2,1)S(1)}, u32[]{:S(2)}, u32[]{:S(2)}) collective-permute-start(bf16[64,512]{1,0:T(8,128)(2,1)} %get-tuple-element.14.own_hbm), channel_id=1, source_target_pairs={{0,16},{8,24},{16,0},{24,8},{1,17},{9,25},{17,1},{25,9},{2,18},{10... | collective-permute-start | bytes 196616 | tf_op jit(solution)/shard_map/ppermute | solution.py:484
  17.3 0.2 collective-permute-start.9
  17.6 0.9 %copy-done = bf16[208,256]{1,0:T(8,128)(2,1)S(1)} copy-done((bf16[208,256]{1,0:T(8,128)(2,1)S(1)}, bf16[208,256]{1,0:T(8,128)(2,1)}, u32[]{:S(2)}) %copy-start) | copy-done | bytes 106520
  18.5 2.4 %rims.1 = (f32[64,128]{1,0:T(8,128)S(1)}, f32[64,128]{1,0:T(8,128)S(1)}, bf16[256,2560]{1,0:T(8,128)(2,1)S(1)}, f32[256,128]{1,0:T(8,128)S(1)}) custom-call(bf16[208,256]{1,0:T(8,128)(2,1)S(1)} %copy-done, bf16[208,256]{1,0:T(8,128)(2,1)S(1)} %collective-permute-done.refs_1_, bf16[208,256]{1,0:T(8,128)(2,1)S(1)} %collective-permute-done.1.refs_2_, ...), custom_call_target="tpu_custom_call" | custom-call | flops 3000000000 | bytes 1000000 | tf_op jit(solution)/shard_map/rims/pallas_call | solution.py:313
  20.9 1.0 %collective-permute-done.8.refs_1_ = bf16[64,512]{1,0:T(8,128)(2,1)S(1)} collective-permute-done((bf16[64,512]{1,0:T(8,128)(2,1)}, bf16[64,512]{1,0:T(8,128)(2,1)S(1)}, u32[]{:S(2)}, u32[]{:S(2)}) %collective-permute-start.8) | collective-permute-done | bytes 65568 | tf_op jit(solution)/shard_map/ppermute | solution.py:484
  21.9 1.8 %collective-permute-done.9.refs_2_ = bf16[64,512]{1,0:T(8,128)(2,1)S(1)} collective-permute-done((bf16[64,512]{1,0:T(8,128)(2,1)}, bf16[64,512]{1,0:T(8,128)(2,1)S(1)}, u32[]{:S(2)}, u32[]{:S(2)}) %collective-permute-start.9) | collective-permute-done | bytes 65568 | tf_op jit(solution)/shard_map/ppermute | solution.py:484
  23.7 0.1 cut.1
  23.8 1.2 %collective-permute-start.11 = (bf16[2,256,128]{2,1,0:T(8,128)(2,1)S(1)}, bf16[2,256,128]{2,1,0:T(8,128)(2,1)S(1)}, u32[]{:S(2)}, u32[]{:S(2)}) collective-permute-start(bf16[2,256,128]{2,1,0:T(8,128)(2,1)S(1)} %get-tuple-element.18), channel_id=1, source_target_pairs={{0,2},{1,3},{2,0},{3,1},{4,6},{5,7},{6,4},{7,5},{8,10},{9,11},{10,... | collective-permute-start | bytes 393224 | tf_op jit(solution)/shard_map/ppermute | solution.py:464
  25.0 2.4 %collective-permute-start.14 = (f32[64,128]{1,0:T(8,128)S(1)}, f32[64,128]{1,0:T(8,128)S(1)}, u32[]{:S(2)}, u32[]{:S(2)}) collective-permute-start(f32[64,128]{1,0:T(8,128)S(1)} %get-tuple-element.15.refs_3_), channel_id=1, source_target_pairs={{0,24},{8,0},{16,8},{24,16},{1,25},{9,1},{17,9},{25,17},{2,26},{10... | collective-permute-start | bytes 98312 | tf_op jit(solution)/shard_map/ppermute | solution.py:459
  27.4 1.5 %collective-permute-done.11.refs_10_ = bf16[2,256,128]{2,1,0:T(8,128)(2,1)S(1)} collective-permute-done((bf16[2,256,128]{2,1,0:T(8,128)(2,1)S(1)}, bf16[2,256,128]{2,1,0:T(8,128)(2,1)S(1)}, u32[]{:S(2)}, u32[]{:S(2)}) %collective-permute-start.11) | collective-permute-done | bytes 131104 | tf_op jit(solution)/shard_map/ppermute | solution.py:464
  28.9 0.9 %core.1.core_ref = f32[256,128]{1,0:T(8,128)S(1)} custom-call(bf16[208,256]{1,0:T(8,128)(2,1)S(1)} %copy-done.1, bf16[208,256]{1,0:T(8,128)(2,1)S(1)} %collective-permute-done.refs_1_, bf16[208,256]{1,0:T(8,128)(2,1)S(1)} %collective-permute-done.1.refs_2_, bf16[208,256]{1,0:T(8,128)(2,1)S(1)} %collective-permute-done.2.refs_3_, ...), custom_call_target="tpu_custom_call" | custom-call | flops 1500000000 | bytes 1000000 | tf_op jit(solution)/shard_map/core/pallas_call | solution.py:352
  29.8 0.4 %collective-permute-done.12.refs_11_ = bf16[2,256,128]{2,1,0:T(8,128)(2,1)S(1)} collective-permute-done((bf16[2,256,128]{2,1,0:T(8,128)(2,1)S(1)}, bf16[2,256,128]{2,1,0:T(8,128)(2,1)S(1)}, u32[]{:S(2)}, u32[]{:S(2)}) %collective-permute-start.12) | collective-permute-done | bytes 131104 | tf_op jit(solution)/shard_map/ppermute | solution.py:464
  30.2 1.0 %multiply.1 = (bf16[256,128]{1,0:T(8,128)(2,1)}, f32[8,128]{1,0:T(8,128)S(1)}) custom-call(bf16[208,256]{1,0:T(8,128)(2,1)S(1)} %copy-done.1, bf16[208,256]{1,0:T(8,128)(2,1)S(1)} %collective-permute-done.refs_1_, bf16[208,256]{1,0:T(8,128)(2,1)S(1)} %collective-permute-done.1.refs_2_, bf16[208,256]{1,0:T(8,128)(2,1)S(1)} %collective-permute-done.2.refs_3_, ...), custom_call_target="tpu_custom_call" | custom-call | flops 500000000 | bytes 1000000 | tf_op jit(solution)/shard_map/multiply/pallas_call | solution.py:426
  31.2 1.9 %collective-permute-done.13.below_ref = f32[64,128]{1,0:T(8,128)S(1)} collective-permute-done((f32[64,128]{1,0:T(8,128)S(1)}, f32[64,128]{1,0:T(8,128)S(1)}, u32[]{:S(2)}, u32[]{:S(2)}) %collective-permute-start.13) | collective-permute-done | bytes 32800 | tf_op jit(solution)/shard_map/ppermute | solution.py:459
  33.1 0.7 %fold.1 = f32[256,128]{1,0:T(8,128)} custom-call(f32[256,128]{1,0:T(8,128)S(1)} %core.1.core_ref, f32[64,128]{1,0:T(8,128)S(1)} %collective-permute-done.13.below_ref, f32[64,128]{1,0:T(8,128)S(1)} %collective-permute-done.14.above_ref, f32[8,128]{1,0:T(8,128)S(1)} %get-tuple-element.23.after_ref), custom_call_target="tpu_custom_call" | custom-call | flops 1000000 | bytes 400000 | tf_op jit(solution)/shard_map/fold/pallas_call | solution.py:447
  (18 shorter events, 0.0 us)
Async XLA Ops:
  2.8 6.2 %collective-permute-start.1 = (bf16[208,256]{1,0:T(8,128)(2,1)}, bf16[208,256]{1,0:T(8,128)(2,1)S(1)}, u32[]{:S(2)}, u32[]{:S(2)}) collective-permute-start(bf16[208,256]{1,0:T(8,128)(2,1)} %get-tuple-element.13.refs_0_), channel_id=1, source_target_pairs={{0,2},{1,3},{2,0},{3,1},{4,6},{5,7},{6,4},{7,5},{8,10},{9,11},{10,... | collective-permute-start | bytes 319496 | tf_op jit(solution)/shard_map/ppermute | solution.py:464
  5.9 5.8 %collective-permute-start.3 = (bf16[208,256]{1,0:T(8,128)(2,1)}, bf16[208,256]{1,0:T(8,128)(2,1)S(1)}, u32[]{:S(2)}, u32[]{:S(2)}) collective-permute-start(bf16[208,256]{1,0:T(8,128)(2,1)} %get-tuple-element.13.refs_0_), channel_id=1, source_target_pairs={{0,4},{1,5},{2,6},{3,7},{4,0},{5,1},{6,2},{7,3},{8,12},{9,13},{10,... | collective-permute-start | bytes 319496 | tf_op jit(solution)/shard_map/ppermute | solution.py:464
  7.4 5.8 %collective-permute-start.5 = (bf16[208,256]{1,0:T(8,128)(2,1)}, bf16[208,256]{1,0:T(8,128)(2,1)S(1)}, u32[]{:S(2)}, u32[]{:S(2)}) collective-permute-start(bf16[208,256]{1,0:T(8,128)(2,1)} %get-tuple-element.13.refs_0_), channel_id=1, source_target_pairs={{0,6},{1,7},{2,4},{3,5},{4,2},{5,3},{6,0},{7,1},{8,14},{9,15},{10,... | collective-permute-start | bytes 319496 | tf_op jit(solution)/shard_map/ppermute | solution.py:464
  7.4 7.3 %collective-permute-start = (bf16[208,256]{1,0:T(8,128)(2,1)}, bf16[208,256]{1,0:T(8,128)(2,1)S(1)}, u32[]{:S(2)}, u32[]{:S(2)}) collective-permute-start(bf16[208,256]{1,0:T(8,128)(2,1)} %get-tuple-element.13.refs_0_), channel_id=1, source_target_pairs={{0,1},{1,0},{2,3},{3,2},{4,5},{5,4},{6,7},{7,6},{8,9},{9,8},{10,11... | collective-permute-start | bytes 319496 | tf_op jit(solution)/shard_map/ppermute | solution.py:464
  9.0 8.3 %collective-permute-start.2 = (bf16[208,256]{1,0:T(8,128)(2,1)S(1)}, bf16[208,256]{1,0:T(8,128)(2,1)S(1)}, u32[]{:S(2)}, u32[]{:S(2)}) collective-permute-start(bf16[208,256]{1,0:T(8,128)(2,1)S(1)} %collective-permute-done.1.refs_2_), channel_id=1, source_target_pairs={{0,1},{1,0},{2,3},{3,2},{4,5},{5,4},{6,7},{7,6},{8,9},{9,8},{10,11... | collective-permute-start | bytes 319496 | tf_op jit(solution)/shard_map/ppermute | solution.py:464
  11.7 5.9 %collective-permute-start.4 = (bf16[208,256]{1,0:T(8,128)(2,1)S(1)}, bf16[208,256]{1,0:T(8,128)(2,1)S(1)}, u32[]{:S(2)}, u32[]{:S(2)}) collective-permute-start(bf16[208,256]{1,0:T(8,128)(2,1)S(1)} %collective-permute-done.3.refs_4_), channel_id=1, source_target_pairs={{0,1},{1,0},{2,3},{3,2},{4,5},{5,4},{6,7},{7,6},{8,9},{9,8},{10,11... | collective-permute-start | bytes 319496 | tf_op jit(solution)/shard_map/ppermute | solution.py:464
  13.2 4.4 %collective-permute-start.6 = (bf16[208,256]{1,0:T(8,128)(2,1)S(1)}, bf16[208,256]{1,0:T(8,128)(2,1)S(1)}, u32[]{:S(2)}, u32[]{:S(2)}) collective-permute-start(bf16[208,256]{1,0:T(8,128)(2,1)S(1)} %collective-permute-done.5.refs_6_), channel_id=1, source_target_pairs={{0,1},{1,0},{2,3},{3,2},{4,5},{5,4},{6,7},{7,6},{8,9},{9,8},{10,11... | collective-permute-start | bytes 319496 | tf_op jit(solution)/shard_map/ppermute | solution.py:464
  13.2 7.7 %collective-permute-start.7 = (bf16[64,512]{1,0:T(8,128)(2,1)}, bf16[64,512]{1,0:T(8,128)(2,1)S(1)}, u32[]{:S(2)}, u32[]{:S(2)}) collective-permute-start(bf16[64,512]{1,0:T(8,128)(2,1)} %get-tuple-element.14.own_hbm), channel_id=1, source_target_pairs={{0,8},{8,0},{16,24},{24,16},{1,9},{9,1},{17,25},{25,17},{2,10},{10... | collective-permute-start | bytes 196616 | tf_op jit(solution)/shard_map/ppermute | solution.py:484
  14.8 7.2 %collective-permute-start.8 = (bf16[64,512]{1,0:T(8,128)(2,1)}, bf16[64,512]{1,0:T(8,128)(2,1)S(1)}, u32[]{:S(2)}, u32[]{:S(2)}) collective-permute-start(bf16[64,512]{1,0:T(8,128)(2,1)} %get-tuple-element.14.own_hbm), channel_id=1, source_target_pairs={{0,16},{8,24},{16,0},{24,8},{1,17},{9,25},{17,1},{25,9},{2,18},{10... | collective-permute-start | bytes 196616 | tf_op jit(solution)/shard_map/ppermute | solution.py:484
  17.3 6.3 %collective-permute-start.9 = (bf16[64,512]{1,0:T(8,128)(2,1)}, bf16[64,512]{1,0:T(8,128)(2,1)S(1)}, u32[]{:S(2)}, u32[]{:S(2)}) collective-permute-start(bf16[64,512]{1,0:T(8,128)(2,1)} %get-tuple-element.14.own_hbm), channel_id=1, source_target_pairs={{0,24},{8,16},{16,8},{24,0},{1,25},{9,17},{17,9},{25,1},{2,26},{10... | collective-permute-start | bytes 196616 | tf_op jit(solution)/shard_map/ppermute | solution.py:484
  17.6 0.9 %copy-start = (bf16[208,256]{1,0:T(8,128)(2,1)S(1)}, bf16[208,256]{1,0:T(8,128)(2,1)}, u32[]{:S(2)}) copy-start(bf16[208,256]{1,0:T(8,128)(2,1)} %get-tuple-element.13.refs_0_) | copy-start | bytes 319492
  18.5 5.2 %copy-start.2 = (bf16[64,512]{1,0:T(8,128)(2,1)S(1)}, bf16[64,512]{1,0:T(8,128)(2,1)}, u32[]{:S(2)}) copy-start(bf16[64,512]{1,0:T(8,128)(2,1)} %get-tuple-element.14.own_hbm) | copy-start | bytes 196612
  18.5 10.4 %copy-start.1 = (bf16[208,256]{1,0:T(8,128)(2,1)S(1)}, bf16[208,256]{1,0:T(8,128)(2,1)}, u32[]{:S(2)}) copy-start(bf16[208,256]{1,0:T(8,128)(2,1)} %get-tuple-element.13.refs_0_) | copy-start | bytes 319492
  23.8 5.0 %collective-permute-start.11 = (bf16[2,256,128]{2,1,0:T(8,128)(2,1)S(1)}, bf16[2,256,128]{2,1,0:T(8,128)(2,1)S(1)}, u32[]{:S(2)}, u32[]{:S(2)}) collective-permute-start(bf16[2,256,128]{2,1,0:T(8,128)(2,1)S(1)} %get-tuple-element.18), channel_id=1, source_target_pairs={{0,2},{1,3},{2,0},{3,1},{4,6},{5,7},{6,4},{7,5},{8,10},{9,11},{10,... | collective-permute-start | bytes 393224 | tf_op jit(solution)/shard_map/ppermute | solution.py:464
  25.0 8.1 %collective-permute-start.14 = (f32[64,128]{1,0:T(8,128)S(1)}, f32[64,128]{1,0:T(8,128)S(1)}, u32[]{:S(2)}, u32[]{:S(2)}) collective-permute-start(f32[64,128]{1,0:T(8,128)S(1)} %get-tuple-element.15.refs_3_), channel_id=1, source_target_pairs={{0,24},{8,0},{16,8},{24,16},{1,25},{9,1},{17,9},{25,17},{2,26},{10... | collective-permute-start | bytes 98312 | tf_op jit(solution)/shard_map/ppermute | solution.py:459
  27.4 2.4 %collective-permute-start.10 = (bf16[256,128]{1,0:T(8,128)(2,1)S(1)}, bf16[256,128]{1,0:T(8,128)(2,1)S(1)}, u32[]{:S(2)}, u32[]{:S(2)}) collective-permute-start(bf16[256,128]{1,0:T(8,128)(2,1)S(1)} %get-tuple-element.17), channel_id=1, source_target_pairs={{0,1},{1,0},{2,3},{3,2},{4,5},{5,4},{6,7},{7,6},{8,9},{9,8},{10,11... | collective-permute-start | bytes 196616 | tf_op jit(solution)/shard_map/ppermute | solution.py:464
  27.4 5.7 %collective-permute-start.13 = (f32[64,128]{1,0:T(8,128)S(1)}, f32[64,128]{1,0:T(8,128)S(1)}, u32[]{:S(2)}, u32[]{:S(2)}) collective-permute-start(f32[64,128]{1,0:T(8,128)S(1)} %get-tuple-element.22), channel_id=1, source_target_pairs={{0,8},{8,16},{16,24},{24,0},{1,9},{9,17},{17,25},{25,1},{2,10},{10... | collective-permute-start | bytes 98312 | tf_op jit(solution)/shard_map/ppermute | solution.py:459
  28.9 1.3 %collective-permute-start.12 = (bf16[2,256,128]{2,1,0:T(8,128)(2,1)S(1)}, bf16[2,256,128]{2,1,0:T(8,128)(2,1)S(1)}, u32[]{:S(2)}, u32[]{:S(2)}) collective-permute-start(bf16[2,256,128]{2,1,0:T(8,128)(2,1)S(1)} %collective-permute-done.11.refs_10_), channel_id=1, source_target_pairs={{0,1},{1,0},{2,3},{3,2},{4,5},{5,4},{6,7},{7,6},{8,9},{9,8},{10,11... | collective-permute-start | bytes 393224 | tf_op jit(solution)/shard_map/ppermute | solution.py:464

commit v3 on v1

--- a/solution.py
+++ b/solution.py
@@ -61,6 +61,16 @@
     earlier = jnp.dot(before, totals.astype(BF16), preferred_element_type=F32)
     count = jnp.dot(every, totals.astype(BF16), preferred_element_type=F32)
     return jnp.where(flags > 0, within + earlier - 1.0, -1.0), count
+
+
+def h_piece(h_ref, hm_ref, chunk):
+    pieces = LANES // BS
+    out = []
+    for block in range(h_ref.shape[0] // BS):
+        bits = [hm_ref[block, chunk * pieces + at] for at in range(pieces)]
+        value = h_ref[pl.ds(block * BS, BS), pl.ds(pl.multiple_of(chunk * LANES, LANES), LANES)]
+        out.append(masked(value, bits).astype(BF16))
+    return jnp.concatenate(out, axis=0)
 
 
 def prepare_kernel(paired, *refs):
@@ -117,21 +127,13 @@
         out[LANES + 16 * PAIRS : BASE, :] = listed
 
     def piece(chunk):
-        pieces = LANES // BS
-        out = []
-        for block in range(h_ref.shape[0] // BS):
-            rows = pl.ds(block * BS, BS)
-            bits = [hm_ref[block, chunk * pieces + at] for at in range(pieces)]
-            value = h_ref[rows, pl.ds(pl.multiple_of(chunk * LANES, LANES), LANES)]
-            out.append(masked(value, bits).astype(BF16))
-        return jnp.concatenate(out, axis=0)
+        return h_piece(h_ref, hm_ref, chunk)
 
     if paired:
         outs[1][BASE:, 0:LANES] = piece(layer ^ 2)
         outs[1][BASE:, LANES:UNIT] = piece(layer ^ 3)
         outs[2][BASE:, 0:LANES] = piece(layer ^ 1)
-        outs[2][BASE:, LANES:UNIT] = jnp.zeros((h_ref.shape[0], LANES), BF16)
-        outs[3][...] = piece(layer)
+        outs[2][BASE:, LANES:UNIT] = piece(layer)
     else:
         for back in range(h_ref.shape[1] // LANES):
             outs[1][back] = piece(lax.rem(layer + back, count))
@@ -142,7 +144,7 @@
     base = jax.ShapeDtypeStruct((BASE, band), BF16)
     tall = jax.ShapeDtypeStruct((BASE + h.shape[0], band), BF16)
     if paired:
-        outs = (base, tall, tall, jax.ShapeDtypeStruct((h.shape[0], LANES), BF16))
+        outs = (base, tall, tall)
     else:
         outs = (base, jax.ShapeDtypeStruct((h.shape[1] // LANES, h.shape[0], LANES), BF16))
     return pl.pallas_call(
@@ -251,69 +253,81 @@
     return (tile[9:10, :] + tile[10:11, :] + tile[11:12, :]) * value
 
 
-def weigh_kernel(num_col, num_layer, refs_in, *refs):
-    blocks = Blocks(refs[:refs_in], num_col, num_layer)
-    coef_ref, long_ref, whole = refs[refs_in:]
-    for index in range(blocks.total):
-        whole[index * LANES : index * LANES + LANES, :] = blocks.matrix(index)
-    over = blocks.over()
-    for at, (which, pair) in enumerate(blocks.units()):
-        coef = weigh(blocks, whole, blocks.unit(which, pair))
-        if pair == PAIRS:
-            coef = jnp.where(over > 0, 0.0, coef)
-        coef_ref[at : at + 1, :] = coef
-
-    @pl.when(jnp.max(over) > 0)
-    def _():
-        for at, (which, side) in enumerate(blocks.long_steps()):
-
-            def step(pair, carry):
-                long_ref[at, pl.ds(pair, 1), :] = weigh(blocks, whole, blocks.tile(which, side, pair))
-                return carry
-
-            lax.fori_loop(0, PAIRS, step, 0)
-
-
-def weigh_all(arrays, num_col, num_layer):
-    ways = 2 if num_col == 2 else 3
-    band = arrays[0].shape[-1]
-    return pl.pallas_call(
-        functools.partial(weigh_kernel, num_col, num_layer, len(arrays)),
-        out_shape=(
-            jax.ShapeDtypeStruct((ways * (PAIRS + 1), UNIT), F32),
-            jax.ShapeDtypeStruct((ways * 2, PAIRS, UNIT), F32),
-        ),
-        in_specs=[VMEM] * len(arrays),
-        out_specs=(VMEM, VMEM),
-        scratch_shapes=[pltpu.VMEM((num_col * num_layer * LANES, band), BF16)],
-        compiler_params=PARAMS,
-        cost_estimate=pl.CostEstimate(flops=2_000_000_000, bytes_accessed=1_000_000, transcendentals=0),
-        name="weigh",
-    )(*arrays)
-
-
 def bell(dist, expo):
     square = dist * dist
     return jnp.where(square < (R + 0.5) ** 2, jnp.exp(-expo * square), 0.0)
 
 
-def spread(blocks, tile, which, lift, coef, at, planeh, planel, depth):
-    expo = tile[6:7, :] + tile[7:8, :] + tile[8:9, :]
-    ex = bell(iota((GX + 2 * R, UNIT), 0) - float(R) - tile[3:4, :], expo)
-    dy = iota((GY, UNIT), 0) - tile[4:5, :] - float(blocks.col_shifts[which] * GY)
-    if blocks.num_col == 2 and which == 1:
+RIM_X = tuple(range(R)) + tuple(range(GX + R, GX + 2 * R))
+CORE_X = tuple(range(R, GX + R))
+ALL_X = tuple(range(GX + 2 * R))
+
+
+def decay(tile):
+    return tile[6:7, :] + tile[7:8, :] + tile[8:9, :]
+
+
+def shapes_x(tile):
+    return bell(iota((GX + 2 * R, UNIT), 0) - float(R) - tile[3:4, :], decay(tile))
+
+
+def shapes_y(tile, shift, wraps):
+    dy = iota((GY, UNIT), 0) - tile[4:5, :] - float(shift * GY)
+    if wraps:
         dy = jnp.where(dy < -float(GY), dy + 2.0 * GY, dy)
-    ey = bell(dy, expo)
-    ez = bell(iota((GZ, UNIT), 0) - tile[5:6, :] - lift, expo) * coef
+    return bell(dy, decay(tile))
+
+
+def shapes_z(tile, lift):
+    return bell(iota((GZ, UNIT), 0) - tile[5:6, :] - lift, decay(tile))
+
+
+def fill_planes(ex, ey, places, at, planeh, planel):
     lanes = pl.ds(at * UNIT, UNIT)
-    ez_hi = ez.astype(BF16)
-    depth[0:GZ, lanes] = ez_hi
-    depth[GZ : 2 * GZ, lanes] = (ez - ez_hi.astype(F32)).astype(BF16)
-    for x in range(GX + 2 * R):
+    for spot, x in enumerate(places):
         plane = ex[x : x + 1, :] * ey
         plane_hi = plane.astype(BF16)
-        planeh[x * GY : x * GY + GY, lanes] = plane_hi
-        planel[x * GY : x * GY + GY, lanes] = (plane - plane_hi.astype(F32)).astype(BF16)
+        planeh[spot * GY : spot * GY + GY, lanes] = plane_hi
+        planel[spot * GY : spot * GY + GY, lanes] = (plane - plane_hi.astype(F32)).astype(BF16)
+
+
+def fill_depth(ez, coef, at, depth):
+    weighed = ez * coef
+    lanes = pl.ds(at * UNIT, UNIT)
+    weighed_hi = weighed.astype(BF16)
+    depth[0:GZ, lanes] = weighed_hi
+    depth[GZ : 2 * GZ, lanes] = (weighed - weighed_hi.astype(F32)).astype(BF16)
+
+
+def settle_kernel(block_ref, out_ref, planeh, planel, ez_ref):
+    out_ref[...] = block_ref[...]
+    for pair in range(PAIRS):
+        tile = block_ref[LANES + 16 * pair : LANES + 16 * pair + 16, :].astype(F32)
+        fill_planes(shapes_x(tile), shapes_y(tile, 0, False), ALL_X, pair, planeh, planel)
+        ez_ref[:, pair * UNIT : pair * UNIT + UNIT] = shapes_z(tile, 0.0)
+
+
+def settle(block):
+    plane = jax.ShapeDtypeStruct((FULL, PAIRS * UNIT), BF16)
+    return pl.pallas_call(
+        settle_kernel,
+        out_shape=(
+            jax.ShapeDtypeStruct(block.shape, BF16),
+            plane,
+            plane,
+            jax.ShapeDtypeStruct((GZ, PAIRS * UNIT), F32),
+        ),
+        in_specs=[VMEM],
+        out_specs=(VMEM,) * 4,
+        compiler_params=PARAMS,
+        cost_estimate=pl.CostEstimate(flops=1_500_000_000, bytes_accessed=1_000_000, transcendentals=0),
+        name="settle",
+    )(block)
+
+
+def set_planes(blocks, tile, which, places, at, planeh, planel):
+    wraps = blocks.num_col == 2 and which == 1
+    fill_planes(shapes_x(tile), shapes_y(tile, blocks.col_shifts[which], wraps), places, at, planeh, planel)
 
 
 def summed(planeh, planel, depth):
@@ -322,58 +336,107 @@
     return first[:, 0:GZ] + first[:, GZ : 2 * GZ] + second
 
 
-def collocate_kernel(num_col, num_layer, refs_in, *refs):
+def rims_kernel(num_col, num_layer, refs_in, *refs):
     blocks = Blocks(refs[:refs_in], num_col, num_layer)
-    coef_ref, long_ref, core_ref, low_ref, high_ref, planeh, planel, depth, acc = refs[refs_in:]
+    ownh, ownl, own_ez = refs[refs_in : refs_in + 3]
+    low_ref, high_ref, depth, extra, whole, planeh, planel, longh, longl, long_depth, acc = refs[refs_in + 3 :]
+    for index in range(blocks.total):
+        whole[index * LANES : index * LANES + LANES, :] = blocks.matrix(index)
+    over = blocks.over()
+    mine = pl.ds(0, PAIRS * UNIT)
+    for target, source in ((planeh, ownh), (planel, ownl)):
+        target[0:HALO, mine] = source[0:HALO, :]
+        target[HALO : 2 * HALO, mine] = source[HALO + CORE : FULL, :]
     for at, (which, pair) in enumerate(blocks.units()):
-        spread(
-            blocks, blocks.unit(which, pair), which, blocks.lifts(pair), coef_ref[at : at + 1, :], at,
-            planeh, planel, depth,
-        )
+        tile = blocks.unit(which, pair)
+        coef = weigh(blocks, whole, tile)
+        if pair == PAIRS:
+            coef = jnp.where(over > 0, 0.0, coef)
+        if at < PAIRS:
+            ez = own_ez[:, at * UNIT : at * UNIT + UNIT]
+        else:
+            set_planes(blocks, tile, which, RIM_X, at, planeh, planel)
+            ez = shapes_z(tile, blocks.lifts(pair))
+        fill_depth(ez, coef, at, depth)
     total = summed(planeh[...], planel[...], depth[...])
     low_ref[...] = total[0:HALO, :]
-    core_ref[...] = total[HALO : HALO + CORE, :]
-    high_ref[...] = total[HALO + CORE : FULL, :]
-
-    @pl.when(jnp.max(blocks.over()) > 0)
+    high_ref[...] = total[HALO:, :]
+
+    @pl.when(jnp.max(over) > 0)
     def _():
         acc[...] = jnp.zeros_like(acc)
-        for at, (which, side) in enumerate(blocks.long_steps()):
+        for which, side in blocks.long_steps():
 
             def step(pair, carry):
+                tile = blocks.tile(which, side, pair)
                 lift = blocks.side_shift(side) * float(GZ)
-                coef = long_ref[at, pl.ds(pair, 1), :]
-                spread(blocks, blocks.tile(which, side, pair), which, lift, coef, 0, planeh, planel, depth)
-                acc[...] += summed(planeh[:, 0:UNIT], planel[:, 0:UNIT], depth[:, 0:UNIT])
+                set_planes(blocks, tile, which, ALL_X, 0, longh, longl)
+                fill_depth(shapes_z(tile, lift), weigh(blocks, whole, tile), 0, long_depth)
+                acc[...] += summed(longh[...], longl[...], long_depth[...])
                 return carry
 
             lax.fori_loop(0, PAIRS, step, 0)
         low_ref[...] += acc[0:HALO, :]
-        core_ref[...] += acc[HALO : HALO + CORE, :]
+        extra[...] = acc[HALO : HALO + CORE, :]
         high_ref[...] += acc[HALO + CORE : FULL, :]
 
 
-def collocate(arrays, coef, long, num_col, num_layer):
-    gaussians = coef.shape[0] * UNIT
-    return pl.pallas_call(
-        functools.partial(collocate_kernel, num_col, num_layer, len(arrays)),
+def rims(arrays, shapes, num_col, num_layer):
+    gaussians = (2 if num_col == 2 else 3) * (PAIRS + 1) * UNIT
+    return pl.pallas_call(
+        functools.partial(rims_kernel, num_col, num_layer, len(arrays)),
         out_shape=(
-            jax.ShapeDtypeStruct((CORE, GZ), F32),
             jax.ShapeDtypeStruct((HALO, GZ), F32),
             jax.ShapeDtypeStruct((HALO, GZ), F32),
+            jax.ShapeDtypeStruct((2 * GZ, gaussians), BF16),
+            jax.ShapeDtypeStruct((CORE, GZ), F32),
         ),
-        in_specs=[VMEM] * (len(arrays) + 2),
-        out_specs=(VMEM, VMEM, VMEM),
+        in_specs=[VMEM] * (len(arrays) + len(shapes)),
+        out_specs=(VMEM,) * 4,
         scratch_shapes=[
-            pltpu.VMEM((FULL, gaussians), BF16),
-            pltpu.VMEM((FULL, gaussians), BF16),
-            pltpu.VMEM((2 * GZ, gaussians), BF16),
+            pltpu.VMEM((num_col * num_layer * LANES, arrays[0].shape[-1]), BF16),
+            pltpu.VMEM((2 * HALO, gaussians), BF16),
+            pltpu.VMEM((2 * HALO, gaussians), BF16),
+            pltpu.VMEM((FULL, UNIT), BF16),
+            pltpu.VMEM((FULL, UNIT), BF16),
+            pltpu.VMEM((2 * GZ, UNIT), BF16),
             pltpu.VMEM((FULL, GZ), F32),
         ],
         compiler_params=PARAMS,
         cost_estimate=pl.CostEstimate(flops=3_000_000_000, bytes_accessed=1_000_000, transcendentals=0),
-        name="collocate",
-    )(*arrays, coef, long)
+        name="rims",
+    )(*arrays, *shapes)
+
+
+def core_kernel(num_col, num_layer, refs_in, *refs):
+    blocks = Blocks(refs[:refs_in], num_col, num_layer)
+    ownh, ownl, depth, extra, core_ref, planeh, planel = refs[refs_in:]
+    for at, (which, pair) in enumerate(blocks.units()):
+        if at >= PAIRS:
+            set_planes(blocks, blocks.unit(which, pair), which, CORE_X, at - PAIRS, planeh, planel)
+    inner = pl.ds(HALO, CORE)
+    split = PAIRS * UNIT
+    core_ref[...] = summed(ownh[inner, :], ownl[inner, :], depth[:, 0:split]) + summed(
+        planeh[...], planel[...], depth[:, split:]
+    )
+
+    @pl.when(jnp.max(blocks.over()) > 0)
+    def _():
+        core_ref[...] += extra[...]
+
+
+def core_part(arrays, shapes, depth, extra, num_col, num_layer):
+    gaussians = depth.shape[1] - PAIRS * UNIT
+    return pl.pallas_call(
+        functools.partial(core_kernel, num_col, num_layer, len(arrays)),
+        out_shape=jax.ShapeDtypeStruct((CORE, GZ), F32),
+        in_specs=[VMEM] * (len(arrays) + 4),
+        out_specs=VMEM,
+        scratch_shapes=[pltpu.VMEM((CORE, gaussians), BF16), pltpu.VMEM((CORE, gaussians), BF16)],
+        compiler_params=PARAMS,
+        cost_estimate=pl.CostEstimate(flops=1_500_000_000, bytes_accessed=1_000_000, transcendentals=0),
+        name="core",
+    )(*arrays, *shapes, depth, extra)
 
 
 def product_kernel(num_row, num_col, num_layer, refs_in, *refs):
@@ -418,18 +481,17 @@
     )(*arrays, *parts)
 
 
-def stack_kernel(rows, own_ref, near_ref, far_ref, both_ref, out_ref):
-    out_ref[0] = own_ref[...]
+def stack_kernel(own_ref, near_ref, far_ref, both_ref, out_ref):
+    out_ref[0] = own_ref[BASE:, LANES:UNIT]
     out_ref[1] = near_ref[BASE:, 0:LANES]
     out_ref[2] = far_ref[BASE:, 0:LANES]
     out_ref[3] = both_ref[BASE:, LANES:UNIT]
 
 
 def stack(own, near, far, both):
-    rows = own.shape[0]
-    return pl.pallas_call(
-        functools.partial(stack_kernel, rows),
-        out_shape=jax.ShapeDtypeStruct((4, rows, LANES), BF16),
+    return pl.pallas_call(
+        stack_kernel,
+        out_shape=jax.ShapeDtypeStruct((4, own.shape[0] - BASE, LANES), BF16),
         in_specs=[VMEM] * 4,
         out_specs=VMEM,
         compiler_params=PARAMS,
@@ -472,7 +534,7 @@
     near_x = crossed(got_x, 0, 1)
     near_y = crossed(got_y, 0, 1)
     near_xy = crossed(got_xy, 0, 1)
-    return [base, near, got_y, near_y, got_x, near_x, got_xy, near_xy]
+    return [tall_core, near, got_y, near_y, got_x, near_x, got_xy, near_xy]
 
 
 def on_device(p_slabs, p_mask, h_slabs, h_mask, gauss_row, gauss_col, gauss_cell, gauss_expo, gauss_pref):
@@ -481,21 +543,27 @@
     flat = [x.reshape(8, LANES) for x in (gauss_row, gauss_col, gauss_cell, gauss_expo, gauss_pref)]
     made = prepare(paired, p_slabs[0], p_mask[0].T, h_slabs[0], h_mask[0], *flat)
     if paired:
-        base, tall_y, tall_core, own = made
-        arrays = gather_paired(base, tall_y, tall_core)
-        mine = stack(own, arrays[1], arrays[2], arrays[3])
+        base, tall_y, tall_core = made
+        settled, planeh, planel, ez = settle(tall_core)
+        arrays = gather_paired(base, tall_y, settled)
+        mine = stack(*arrays[:4])
     else:
         base, pieces = made
         arrays = [lax.all_gather(base, ("layer", "col"), axis=0)]
+        _, planeh, planel, ez = settle(base)
         mine = [pieces[0]] + [shifted(pieces[step], "layer", num_layer, step) for step in range(1, num_layer)]
         mine = jnp.stack(mine)
-    parts = [mine] + [
-        lax.ppermute(mine, "row", [(i, i ^ step) for i in range(num_row)]) for step in range(1, num_row)
-    ]
-    coef, long = weigh_all(arrays, num_col, num_layer)
-    core, low, high = collocate(arrays, coef, long, num_col, num_layer)
+
+    def over_row(value, step):
+        return lax.ppermute(value, "row", [(i, i ^ step) for i in range(num_row)])
+
+    parts = [mine] + [over_row(mine, step) for step in range(1, num_row)]
+    if num_row == 4:
+        parts[3] = over_row(parts[2], 1)
+    low, high, depth, extra = rims(arrays, (planeh, planel, ez), num_col, num_layer)
     below = shifted(high, "row", num_row, 1)
     above = shifted(low, "row", num_row, num_row - 1)
+    core = core_part(arrays, (planeh, planel), depth, extra, num_col, num_layer)
     product, token = multiply(arrays, parts, num_row, num_col, num_layer)
     density = fold(core, below, above, token).reshape(GX, GY, GZ)
     return (product, density)

time: 28.6 us -> 32.6 us (1.14)
  waiting for transfers between devices: 6.79 us -> 9.88 us
  starting transfers between devices: 12.9 us -> 13.3 us
  Pallas kernels: 7.24 us -> 7.6 us
    ppermute x3, waiting for transfers between devices: 0.01 us -> 3.39 us  [over_row(): return lax.ppermute(value, 'row', [(i, i ^ step) for i in range(num_row)])]
    ppermute x2, waiting for transfers between devices: 1.02 us -> 0.01 us  [shifted(): lax.ppermute(value, axis, [(i, (i + step) % count) for i in range(count)])]
    ppermute x7, waiting for transfers between devices: 5.76 us -> 6.48 us  [crossed(): return lax.ppermute(value, ('col', 'layer'), pairs)]
    ppermute x7, starting transfers between devices: 4.58 us -> 5.2 us  [crossed(): return lax.ppermute(value, ('col', 'layer'), pairs)]
    pallas_call x3 -> x4, Pallas kernels: 3.3 us -> 3.66 us  [the longest x1 2.34 us: rims(): pl.pallas_call(functools.partial(rims_kernel, num_col, num_layer, len(arr...]
    unnamed x4 -> x2, local copies, waits for them, and re-layouts: 0.72 us -> 0.91 us
  transfers between devices with their start and end apart: 12 -> 12, of which waited for: 4 -> 3; matrix products, arithmetic and copies ran while one was open for 0% -> 0% of each run, Pallas kernels for 15% -> 14%
where the time goes in v3:
time: 32.6 us; the launch traced here: 32.4 us
  starting transfers between devices  13.3 us (41%)
  waiting for transfers between devices  9.88 us (30%)
  Pallas kernels  7.6 us (23%)
  local copies, waits for them, and re-layouts  0.91 us (3%)
  between operations  0.69 us (2%)
    ppermute x7, waiting for transfers between devices, crossed(): return lax.ppermute(value, ('col', 'layer'), pairs)  6.48 us
    ppermute x7, starting transfers between devices, crossed(): return lax.ppermute(value, ('col', 'layer'), pairs)  5.2 us
    ppermute x3, starting transfers between devices, over_row(): return lax.ppermute(value, 'row', [(i, i ^ step) for i in range(num_row)])  4.23 us
    ppermute x2, starting transfers between devices, shifted(): lax.ppermute(value, axis, [(i, (i + step) % count) for i in range(count)])  3.88 us
    ppermute x3, waiting for transfers between devices, over_row(): return lax.ppermute(value, 'row', [(i, i ^ step) for i in range(num_row)])  3.39 us
    pallas_call x1, Pallas kernels, rims(): pl.pallas_call(functools.partial(rims_kernel, num_col, num_layer, len(arr...  2.34 us
    pallas_call x1, Pallas kernels, prepare(): pl.pallas_call(functools.partial(prepare_kernel, paired), out_shape=outs,...  2.29 us
    pallas_call x1, Pallas kernels, multiply(): pl.pallas_call(functools.partial(product_kernel, num_row, num_col, num_la...  0.97 us
  transfers between devices with their start and end apart: 12, of which 3 were waited for; matrix products, arithmetic and copies ran while one was open for 0% of the time, Pallas kernels for 14%

profile of v3, /device:TPU:0, one launch (start us, length us, event | category | flops | bytes accessed | tf_op | source)
XLA Modules:
  0.0 32.4 jit_solution(1343109866211985981)
XLA Ops:
  0.6 2.3 %prepare.1 = (bf16[208,256]{1,0:T(8,128)(2,1)}, bf16[272,256]{1,0:T(8,128)(2,1)}, bf16[272,256]{1,0:T(8,128)(2,1)}) custom-call(bf16[256,128]{1,0:T(8,128)(2,1)} %bitcast.13, s32[4,8]{1,0:T(4,128)} %bitcast.20, bf16[64,512]{1,0:T(8,128)(2,1)} %bitcast.14, s32[2,16]{1,0:T(2,128)} %bitcast.21, s32[8,128]{1,0:T(8,128)} %bitcast.15, s32[8,128]{1,0:T(8,128)} %bitcast.16, ...), custom_call_target="tpu_custom_call" | custom-call | tf_op jit(solution)/shard_map/prepare/pallas_call | solution.py:150
  2.9 3.0 %collective-permute-start.3 = (bf16[208,256]{1,0:T(8,128)(2,1)}, bf16[208,256]{1,0:T(8,128)(2,1)S(1)}, u32[]{:S(2)}, u32[]{:S(2)}) collective-permute-start(bf16[208,256]{1,0:T(8,128)(2,1)} %get-tuple-element.18), channel_id=1, source_target_pairs={{0,4},{1,5},{2,6},{3,7},{4,0},{5,1},{6,2},{7,3},{8,12},{9,13},{10,... | collective-permute-start | bytes 319496 | tf_op jit(solution)/shard_map/ppermute | solution.py:526
  5.9 1.5 %collective-permute-start.5 = (bf16[208,256]{1,0:T(8,128)(2,1)}, bf16[208,256]{1,0:T(8,128)(2,1)S(1)}, u32[]{:S(2)}, u32[]{:S(2)}) collective-permute-start(bf16[208,256]{1,0:T(8,128)(2,1)} %get-tuple-element.18), channel_id=1, source_target_pairs={{0,6},{1,7},{2,4},{3,5},{4,2},{5,3},{6,0},{7,1},{8,14},{9,15},{10,... | collective-permute-start | bytes 319496 | tf_op jit(solution)/shard_map/ppermute | solution.py:526
  7.4 0.1 collective-permute-start.1
  7.5 0.9 %copy-done = bf16[272,256]{1,0:T(8,128)(2,1)S(1)} copy-done((bf16[272,256]{1,0:T(8,128)(2,1)S(1)}, bf16[272,256]{1,0:T(8,128)(2,1)}, u32[]{:S(2)}) %copy-start) | copy-done | bytes 139288
  8.4 0.4 %settle.1 = (bf16[272,256]{1,0:T(8,128)(2,1)S(1)}, bf16[384,1024]{1,0:T(8,128)(2,1)S(1)}, bf16[384,1024]{1,0:T(8,128)(2,1)S(1)}, f32[128,1024]{1,0:T(8,128)S(1)}) custom-call(bf16[272,256]{1,0:T(8,128)(2,1)S(1)} %copy-done), custom_call_target="tpu_custom_call" | custom-call | flops 1500000000 | bytes 1000000 | tf_op jit(solution)/shard_map/settle/pallas_call | solution.py:312
  8.8 0.1 collective-permute-start
  8.9 5.7 %collective-permute-done.1.far_ref.refs_2_ = bf16[272,256]{1,0:T(8,128)(2,1)S(1)} collective-permute-done((bf16[272,256]{1,0:T(8,128)(2,1)}, bf16[272,256]{1,0:T(8,128)(2,1)S(1)}, u32[]{:S(2)}, u32[]{:S(2)}) %collective-permute-start.1) | collective-permute-done | bytes 139296 | tf_op jit(solution)/shard_map/ppermute | solution.py:526
  14.6 0.0 collective-permute-start.2
  14.6 0.0 collective-permute-done.3.refs_4_
  14.6 0.5 %collective-permute-start.4 = (bf16[208,256]{1,0:T(8,128)(2,1)S(1)}, bf16[208,256]{1,0:T(8,128)(2,1)S(1)}, u32[]{:S(2)}, u32[]{:S(2)}) collective-permute-start(bf16[208,256]{1,0:T(8,128)(2,1)S(1)} %collective-permute-done.3.refs_4_), channel_id=1, source_target_pairs={{0,1},{1,0},{2,3},{3,2},{4,5},{5,4},{6,7},{7,6},{8,9},{9,8},{10,11... | collective-permute-start | bytes 319496 | tf_op jit(solution)/shard_map/ppermute | solution.py:526
  15.1 0.0 collective-permute-done.5.refs_6_
  15.1 0.1 collective-permute-start.6
  15.2 0.0 collective-permute-done.near_ref.refs_1_
  15.2 0.8 %collective-permute-done.2.both_ref.refs_3_ = bf16[272,256]{1,0:T(8,128)(2,1)S(1)} collective-permute-done((bf16[272,256]{1,0:T(8,128)(2,1)S(1)}, bf16[272,256]{1,0:T(8,128)(2,1)S(1)}, u32[]{:S(2)}, u32[]{:S(2)}) %collective-permute-start.2) | collective-permute-done | bytes 139296 | tf_op jit(solution)/shard_map/ppermute | solution.py:526
  16.0 2.7 %collective-permute-start.8 = (bf16[4,64,128]{2,1,0:T(8,128)(2,1)S(1)}, bf16[4,64,128]{2,1,0:T(8,128)(2,1)S(1)}, u32[]{:S(2)}, u32[]{:S(2)}) collective-permute-start(bf16[4,64,128]{2,1,0:T(8,128)(2,1)S(1)} %stack.1.refs_8_), channel_id=1, source_target_pairs={{0,16},{8,24},{16,0},{24,8},{1,17},{9,25},{17,1},{25,9},{2,18},{10... | collective-permute-start | bytes 196616 | tf_op jit(solution)/shard_map/ppermute | solution.py:558
  18.6 1.6 %collective-permute-start.7 = (bf16[4,64,128]{2,1,0:T(8,128)(2,1)S(1)}, bf16[4,64,128]{2,1,0:T(8,128)(2,1)S(1)}, u32[]{:S(2)}, u32[]{:S(2)}) collective-permute-start(bf16[4,64,128]{2,1,0:T(8,128)(2,1)S(1)} %stack.1.refs_8_), channel_id=1, source_target_pairs={{0,8},{8,0},{16,24},{24,16},{1,9},{9,1},{17,25},{25,17},{2,10},{10... | collective-permute-start | bytes 196616 | tf_op jit(solution)/shard_map/ppermute | solution.py:558
  20.2 2.3 %rims.1 = (f32[64,128]{1,0:T(8,128)S(1)}, f32[64,128]{1,0:T(8,128)S(1)}, bf16[256,2560]{1,0:T(8,128)(2,1)S(1)}, f32[256,128]{1,0:T(8,128)S(1)}) custom-call(bf16[272,256]{1,0:T(8,128)(2,1)S(1)} %get-tuple-element.16.own_ref.refs_0_, bf16[272,256]{1,0:T(8,128)(2,1)S(1)} %collective-permute-done.near_ref.refs_1_, ...), custom_call_target="tpu_custom_call" | custom-call | flops 3000000000 | bytes 1000000 | tf_op jit(solution)/shard_map/rims/pallas_call | solution.py:386
  22.6 0.5 %collective-permute-start.10 = (f32[64,128]{1,0:T(8,128)S(1)}, f32[64,128]{1,0:T(8,128)S(1)}, u32[]{:S(2)}, u32[]{:S(2)}) collective-permute-start(f32[64,128]{1,0:T(8,128)S(1)} %get-tuple-element.25), channel_id=1, source_target_pairs={{0,8},{8,16},{16,24},{24,0},{1,9},{9,17},{17,25},{25,1},{2,10},{10... | collective-permute-start | bytes 98312 | tf_op jit(solution)/shard_map/ppermute | solution.py:521
  23.1 3.4 %collective-permute-start.11 = (f32[64,128]{1,0:T(8,128)S(1)}, f32[64,128]{1,0:T(8,128)S(1)}, u32[]{:S(2)}, u32[]{:S(2)}) collective-permute-start(f32[64,128]{1,0:T(8,128)S(1)} %get-tuple-element.26), channel_id=1, source_target_pairs={{0,24},{8,0},{16,8},{24,16},{1,25},{9,1},{17,9},{25,17},{2,26},{10... | collective-permute-start | bytes 98312 | tf_op jit(solution)/shard_map/ppermute | solution.py:521
  26.5 0.9 %core.1.core_ref = f32[256,128]{1,0:T(8,128)S(1)} custom-call(bf16[272,256]{1,0:T(8,128)(2,1)S(1)} %get-tuple-element.16.own_ref.refs_0_, bf16[272,256]{1,0:T(8,128)(2,1)S(1)} %collective-permute-done.near_ref.refs_1_, bf16[272,256]{1,0:T(8,128)(2,1)S(1)} %collective-permute-done.1.far_ref.refs_2_, ...), custom_call_target="tpu_custom_call" | custom-call | flops 1500000000 | bytes 1000000 | tf_op jit(solution)/shard_map/core/pallas_call | solution.py:430
  27.3 3.4 %collective-permute-done.9.refs_11_ = bf16[4,64,128]{2,1,0:T(8,128)(2,1)S(1)} collective-permute-done((bf16[4,64,128]{2,1,0:T(8,128)(2,1)S(1)}, bf16[4,64,128]{2,1,0:T(8,128)(2,1)S(1)}, u32[]{:S(2)}, u32[]{:S(2)}) %collective-permute-start.9) | collective-permute-done | bytes 65568 | tf_op jit(solution)/shard_map/ppermute | solution.py:558
  30.7 1.0 %multiply.1 = (bf16[256,128]{1,0:T(8,128)(2,1)}, f32[8,128]{1,0:T(8,128)S(1)}) custom-call(bf16[272,256]{1,0:T(8,128)(2,1)S(1)} %get-tuple-element.16.own_ref.refs_0_, bf16[272,256]{1,0:T(8,128)(2,1)S(1)} %collective-permute-done.near_ref.refs_1_, bf16[272,256]{1,0:T(8,128)(2,1)S(1)} %collective-permute-done.1.far_ref.refs_2_, ...), custom_call_target="tpu_custom_call" | custom-call | flops 500000000 | bytes 1000000 | tf_op jit(solution)/shard_map/multiply/pallas_call | solution.py:469
  31.7 0.7 %fold.1 = f32[256,128]{1,0:T(8,128)} custom-call(f32[256,128]{1,0:T(8,128)S(1)} %core.1.core_ref, f32[64,128]{1,0:T(8,128)S(1)} %collective-permute-done.10.below_ref, f32[64,128]{1,0:T(8,128)S(1)} %collective-permute-done.11.above_ref, f32[8,128]{1,0:T(8,128)S(1)} %get-tuple-element.27.after_ref), custom_call_target="tpu_custom_call" | custom-call | flops 1000000 | bytes 400000 | tf_op jit(solution)/shard_map/fold/pallas_call | solution.py:509
  (9 shorter events, 0.0 us)
Async XLA Ops:
  2.9 11.7 %collective-permute-start.3 = (bf16[208,256]{1,0:T(8,128)(2,1)}, bf16[208,256]{1,0:T(8,128)(2,1)S(1)}, u32[]{:S(2)}, u32[]{:S(2)}) collective-permute-start(bf16[208,256]{1,0:T(8,128)(2,1)} %get-tuple-element.18), channel_id=1, source_target_pairs={{0,4},{1,5},{2,6},{3,7},{4,0},{5,1},{6,2},{7,3},{8,12},{9,13},{10,... | collective-permute-start | bytes 319496 | tf_op jit(solution)/shard_map/ppermute | solution.py:526
  5.9 9.2 %collective-permute-start.5 = (bf16[208,256]{1,0:T(8,128)(2,1)}, bf16[208,256]{1,0:T(8,128)(2,1)S(1)}, u32[]{:S(2)}, u32[]{:S(2)}) collective-permute-start(bf16[208,256]{1,0:T(8,128)(2,1)} %get-tuple-element.18), channel_id=1, source_target_pairs={{0,6},{1,7},{2,4},{3,5},{4,2},{5,3},{6,0},{7,1},{8,14},{9,15},{10,... | collective-permute-start | bytes 319496 | tf_op jit(solution)/shard_map/ppermute | solution.py:526
  7.4 7.2 %collective-permute-start.1 = (bf16[272,256]{1,0:T(8,128)(2,1)}, bf16[272,256]{1,0:T(8,128)(2,1)S(1)}, u32[]{:S(2)}, u32[]{:S(2)}) collective-permute-start(bf16[272,256]{1,0:T(8,128)(2,1)} %get-tuple-element.17), channel_id=1, source_target_pairs={{0,2},{1,3},{2,0},{3,1},{4,6},{5,7},{6,4},{7,5},{8,10},{9,11},{10,... | collective-permute-start | bytes 417800 | tf_op jit(solution)/shard_map/ppermute | solution.py:526
  7.5 0.9 %copy-start = (bf16[272,256]{1,0:T(8,128)(2,1)S(1)}, bf16[272,256]{1,0:T(8,128)(2,1)}, u32[]{:S(2)}) copy-start(bf16[272,256]{1,0:T(8,128)(2,1)} %get-tuple-element.15.block_ref) | copy-start | bytes 417796
  8.8 6.4 %collective-permute-start = (bf16[272,256]{1,0:T(8,128)(2,1)S(1)}, bf16[272,256]{1,0:T(8,128)(2,1)S(1)}, u32[]{:S(2)}, u32[]{:S(2)}) collective-permute-start(bf16[272,256]{1,0:T(8,128)(2,1)S(1)} %get-tuple-element.16.own_ref.refs_0_), channel_id=1, source_target_pairs={{0,1},{1,0},{2,3},{3,2},{4,5},{5,4},{6,7},{7,6},{8,9},{9,8},{10,11... | collective-permute-start | bytes 417800 | tf_op jit(solution)/shard_map/ppermute | solution.py:526
  14.6 1.4 %collective-permute-start.2 = (bf16[272,256]{1,0:T(8,128)(2,1)S(1)}, bf16[272,256]{1,0:T(8,128)(2,1)S(1)}, u32[]{:S(2)}, u32[]{:S(2)}) collective-permute-start(bf16[272,256]{1,0:T(8,128)(2,1)S(1)} %collective-permute-done.1.far_ref.refs_2_), channel_id=1, source_target_pairs={{0,1},{1,0},{2,3},{3,2},{4,5},{5,4},{6,7},{7,6},{8,9},{9,8},{10,11... | collective-permute-start | bytes 417800 | tf_op jit(solution)/shard_map/ppermute | solution.py:526
  14.6 5.6 %collective-permute-start.4 = (bf16[208,256]{1,0:T(8,128)(2,1)S(1)}, bf16[208,256]{1,0:T(8,128)(2,1)S(1)}, u32[]{:S(2)}, u32[]{:S(2)}) collective-permute-start(bf16[208,256]{1,0:T(8,128)(2,1)S(1)} %collective-permute-done.3.refs_4_), channel_id=1, source_target_pairs={{0,1},{1,0},{2,3},{3,2},{4,5},{5,4},{6,7},{7,6},{8,9},{9,8},{10,11... | collective-permute-start | bytes 319496 | tf_op jit(solution)/shard_map/ppermute | solution.py:526
  15.1 5.1 %collective-permute-start.6 = (bf16[208,256]{1,0:T(8,128)(2,1)S(1)}, bf16[208,256]{1,0:T(8,128)(2,1)S(1)}, u32[]{:S(2)}, u32[]{:S(2)}) collective-permute-start(bf16[208,256]{1,0:T(8,128)(2,1)S(1)} %collective-permute-done.5.refs_6_), channel_id=1, source_target_pairs={{0,1},{1,0},{2,3},{3,2},{4,5},{5,4},{6,7},{7,6},{8,9},{9,8},{10,11... | collective-permute-start | bytes 319496 | tf_op jit(solution)/shard_map/ppermute | solution.py:526
  16.0 10.5 %collective-permute-start.8 = (bf16[4,64,128]{2,1,0:T(8,128)(2,1)S(1)}, bf16[4,64,128]{2,1,0:T(8,128)(2,1)S(1)}, u32[]{:S(2)}, u32[]{:S(2)}) collective-permute-start(bf16[4,64,128]{2,1,0:T(8,128)(2,1)S(1)} %stack.1.refs_8_), channel_id=1, source_target_pairs={{0,16},{8,24},{16,0},{24,8},{1,17},{9,25},{17,1},{25,9},{2,18},{10... | collective-permute-start | bytes 196616 | tf_op jit(solution)/shard_map/ppermute | solution.py:558
  18.6 8.7 %collective-permute-start.7 = (bf16[4,64,128]{2,1,0:T(8,128)(2,1)S(1)}, bf16[4,64,128]{2,1,0:T(8,128)(2,1)S(1)}, u32[]{:S(2)}, u32[]{:S(2)}) collective-permute-start(bf16[4,64,128]{2,1,0:T(8,128)(2,1)S(1)} %stack.1.refs_8_), channel_id=1, source_target_pairs={{0,8},{8,0},{16,24},{24,16},{1,9},{9,1},{17,25},{25,17},{2,10},{10... | collective-permute-start | bytes 196616 | tf_op jit(solution)/shard_map/ppermute | solution.py:558
  22.6 9.1 %collective-permute-start.10 = (f32[64,128]{1,0:T(8,128)S(1)}, f32[64,128]{1,0:T(8,128)S(1)}, u32[]{:S(2)}, u32[]{:S(2)}) collective-permute-start(f32[64,128]{1,0:T(8,128)S(1)} %get-tuple-element.25), channel_id=1, source_target_pairs={{0,8},{8,16},{16,24},{24,0},{1,9},{9,17},{17,25},{25,1},{2,10},{10... | collective-permute-start | bytes 98312 | tf_op jit(solution)/shard_map/ppermute | solution.py:521
  23.1 8.6 %collective-permute-start.11 = (f32[64,128]{1,0:T(8,128)S(1)}, f32[64,128]{1,0:T(8,128)S(1)}, u32[]{:S(2)}, u32[]{:S(2)}) collective-permute-start(f32[64,128]{1,0:T(8,128)S(1)} %get-tuple-element.26), channel_id=1, source_target_pairs={{0,24},{8,0},{16,8},{24,16},{1,25},{9,1},{17,9},{25,17},{2,26},{10... | collective-permute-start | bytes 98312 | tf_op jit(solution)/shard_map/ppermute | solution.py:521
  26.5 4.3 %collective-permute-start.9 = (bf16[4,64,128]{2,1,0:T(8,128)(2,1)S(1)}, bf16[4,64,128]{2,1,0:T(8,128)(2,1)S(1)}, u32[]{:S(2)}, u32[]{:S(2)}) collective-permute-start(bf16[4,64,128]{2,1,0:T(8,128)(2,1)S(1)} %collective-permute-done.8.refs_10_), channel_id=1, source_target_pairs={{0,8},{8,0},{16,24},{24,16},{1,9},{9,1},{17,25},{25,17},{2,10},{10... | collective-permute-start | bytes 196616 | tf_op jit(solution)/shard_map/ppermute | solution.py:558

commit v4 on v3

--- a/solution.py
+++ b/solution.py
@@ -299,32 +299,6 @@
     depth[GZ : 2 * GZ, lanes] = (weighed - weighed_hi.astype(F32)).astype(BF16)
 
 
-def settle_kernel(block_ref, out_ref, planeh, planel, ez_ref):
-    out_ref[...] = block_ref[...]
-    for pair in range(PAIRS):
-        tile = block_ref[LANES + 16 * pair : LANES + 16 * pair + 16, :].astype(F32)
-        fill_planes(shapes_x(tile), shapes_y(tile, 0, False), ALL_X, pair, planeh, planel)
-        ez_ref[:, pair * UNIT : pair * UNIT + UNIT] = shapes_z(tile, 0.0)
-
-
-def settle(block):
-    plane = jax.ShapeDtypeStruct((FULL, PAIRS * UNIT), BF16)
-    return pl.pallas_call(
-        settle_kernel,
-        out_shape=(
-            jax.ShapeDtypeStruct(block.shape, BF16),
-            plane,
-            plane,
-            jax.ShapeDtypeStruct((GZ, PAIRS * UNIT), F32),
-        ),
-        in_specs=[VMEM],
-        out_specs=(VMEM,) * 4,
-        compiler_params=PARAMS,
-        cost_estimate=pl.CostEstimate(flops=1_500_000_000, bytes_accessed=1_000_000, transcendentals=0),
-        name="settle",
-    )(block)
-
-
 def set_planes(blocks, tile, which, places, at, planeh, planel):
     wraps = blocks.num_col == 2 and which == 1
     fill_planes(shapes_x(tile), shapes_y(tile, blocks.col_shifts[which], wraps), places, at, planeh, planel)
@@ -338,26 +312,17 @@
 
 def rims_kernel(num_col, num_layer, refs_in, *refs):
     blocks = Blocks(refs[:refs_in], num_col, num_layer)
-    ownh, ownl, own_ez = refs[refs_in : refs_in + 3]
-    low_ref, high_ref, depth, extra, whole, planeh, planel, longh, longl, long_depth, acc = refs[refs_in + 3 :]
+    low_ref, high_ref, depth, extra, whole, planeh, planel, longh, longl, long_depth, acc = refs[refs_in:]
     for index in range(blocks.total):
         whole[index * LANES : index * LANES + LANES, :] = blocks.matrix(index)
     over = blocks.over()
-    mine = pl.ds(0, PAIRS * UNIT)
-    for target, source in ((planeh, ownh), (planel, ownl)):
-        target[0:HALO, mine] = source[0:HALO, :]
-        target[HALO : 2 * HALO, mine] = source[HALO + CORE : FULL, :]
     for at, (which, pair) in enumerate(blocks.units()):
         tile = blocks.unit(which, pair)
         coef = weigh(blocks, whole, tile)
         if pair == PAIRS:
             coef = jnp.where(over > 0, 0.0, coef)
-        if at < PAIRS:
-            ez = own_ez[:, at * UNIT : at * UNIT + UNIT]
-        else:
-            set_planes(blocks, tile, which, RIM_X, at, planeh, planel)
-            ez = shapes_z(tile, blocks.lifts(pair))
-        fill_depth(ez, coef, at, depth)
+        set_planes(blocks, tile, which, RIM_X, at, planeh, planel)
+        fill_depth(shapes_z(tile, blocks.lifts(pair)), coef, at, depth)
     total = summed(planeh[...], planel[...], depth[...])
     low_ref[...] = total[0:HALO, :]
     high_ref[...] = total[HALO:, :]
@@ -381,7 +346,7 @@
         high_ref[...] += acc[HALO + CORE : FULL, :]
 
 
-def rims(arrays, shapes, num_col, num_layer):
+def rims(arrays, num_col, num_layer):
     gaussians = (2 if num_col == 2 else 3) * (PAIRS + 1) * UNIT
     return pl.pallas_call(
         functools.partial(rims_kernel, num_col, num_layer, len(arrays)),
@@ -391,7 +356,7 @@
             jax.ShapeDtypeStruct((2 * GZ, gaussians), BF16),
             jax.ShapeDtypeStruct((CORE, GZ), F32),
         ),
-        in_specs=[VMEM] * (len(arrays) + len(shapes)),
+        in_specs=[VMEM] * len(arrays),
         out_specs=(VMEM,) * 4,
         scratch_shapes=[
             pltpu.VMEM((num_col * num_layer * LANES, arrays[0].shape[-1]), BF16),
@@ -405,38 +370,33 @@
         compiler_params=PARAMS,
         cost_estimate=pl.CostEstimate(flops=3_000_000_000, bytes_accessed=1_000_000, transcendentals=0),
         name="rims",
-    )(*arrays, *shapes)
+    )(*arrays)
 
 
 def core_kernel(num_col, num_layer, refs_in, *refs):
     blocks = Blocks(refs[:refs_in], num_col, num_layer)
-    ownh, ownl, depth, extra, core_ref, planeh, planel = refs[refs_in:]
+    depth, extra, core_ref, planeh, planel = refs[refs_in:]
     for at, (which, pair) in enumerate(blocks.units()):
-        if at >= PAIRS:
-            set_planes(blocks, blocks.unit(which, pair), which, CORE_X, at - PAIRS, planeh, planel)
-    inner = pl.ds(HALO, CORE)
-    split = PAIRS * UNIT
-    core_ref[...] = summed(ownh[inner, :], ownl[inner, :], depth[:, 0:split]) + summed(
-        planeh[...], planel[...], depth[:, split:]
-    )
+        set_planes(blocks, blocks.unit(which, pair), which, CORE_X, at, planeh, planel)
+    core_ref[...] = summed(planeh[...], planel[...], depth[...])
 
     @pl.when(jnp.max(blocks.over()) > 0)
     def _():
         core_ref[...] += extra[...]
 
 
-def core_part(arrays, shapes, depth, extra, num_col, num_layer):
-    gaussians = depth.shape[1] - PAIRS * UNIT
+def core_part(arrays, depth, extra, num_col, num_layer):
+    gaussians = depth.shape[1]
     return pl.pallas_call(
         functools.partial(core_kernel, num_col, num_layer, len(arrays)),
         out_shape=jax.ShapeDtypeStruct((CORE, GZ), F32),
-        in_specs=[VMEM] * (len(arrays) + 4),
+        in_specs=[VMEM] * (len(arrays) + 2),
         out_specs=VMEM,
         scratch_shapes=[pltpu.VMEM((CORE, gaussians), BF16), pltpu.VMEM((CORE, gaussians), BF16)],
         compiler_params=PARAMS,
         cost_estimate=pl.CostEstimate(flops=1_500_000_000, bytes_accessed=1_000_000, transcendentals=0),
         name="core",
-    )(*arrays, *shapes, depth, extra)
+    )(*arrays, depth, extra)
 
 
 def product_kernel(num_row, num_col, num_layer, refs_in, *refs):
@@ -543,27 +503,20 @@
     flat = [x.reshape(8, LANES) for x in (gauss_row, gauss_col, gauss_cell, gauss_expo, gauss_pref)]
     made = prepare(paired, p_slabs[0], p_mask[0].T, h_slabs[0], h_mask[0], *flat)
     if paired:
-        base, tall_y, tall_core = made
-        settled, planeh, planel, ez = settle(tall_core)
-        arrays = gather_paired(base, tall_y, settled)
+        arrays = gather_paired(*made)
         mine = stack(*arrays[:4])
     else:
         base, pieces = made
         arrays = [lax.all_gather(base, ("layer", "col"), axis=0)]
-        _, planeh, planel, ez = settle(base)
         mine = [pieces[0]] + [shifted(pieces[step], "layer", num_layer, step) for step in range(1, num_layer)]
         mine = jnp.stack(mine)
-
-    def over_row(value, step):
-        return lax.ppermute(value, "row", [(i, i ^ step) for i in range(num_row)])
-
-    parts = [mine] + [over_row(mine, step) for step in range(1, num_row)]
-    if num_row == 4:
-        parts[3] = over_row(parts[2], 1)
-    low, high, depth, extra = rims(arrays, (planeh, planel, ez), num_col, num_layer)
+    low, high, depth, extra = rims(arrays, num_col, num_layer)
+    parts = [mine] + [
+        lax.ppermute(mine, "row", [(i, i ^ step) for i in range(num_row)]) for step in range(1, num_row)
+    ]
     below = shifted(high, "row", num_row, 1)
     above = shifted(low, "row", num_row, num_row - 1)
-    core = core_part(arrays, (planeh, planel), depth, extra, num_col, num_layer)
+    core = core_part(arrays, depth, extra, num_col, num_layer)
     product, token = multiply(arrays, parts, num_row, num_col, num_layer)
     density = fold(core, below, above, token).reshape(GX, GY, GZ)
     return (product, density)

time: 32.6 us -> 27.8 us (0.85)
  waiting for transfers between devices: 9.88 us -> 5.84 us
  starting transfers between devices: 13.3 us -> 12.9 us
  Pallas kernels: 7.6 us -> 7.24 us
    ppermute x3, waiting for transfers between devices: 3.39 us -> 0.01 us  [on_device(): lax.ppermute(mine, 'row', [(i, i ^ step) for i in range(num_row)])]
    ppermute x7, waiting for transfers between devices: 6.48 us -> 5.76 us  [crossed(): return lax.ppermute(value, ('col', 'layer'), pairs)]
    ppermute x7, starting transfers between devices: 5.2 us -> 4.58 us  [crossed(): return lax.ppermute(value, ('col', 'layer'), pairs)]
    pallas_call x1 -> x0, Pallas kernels: 0.45 us -> none  [settle(): pl.pallas_call(settle_kernel, out_shape=(jax.ShapeDtypeStruct(block.shape...]
  transfers between devices with their start and end apart: 12 -> 12, of which waited for: 3 -> 4; matrix products, arithmetic and copies ran while one was open for 0% -> 0% of each run, Pallas kernels for 14% -> 16%
where the time goes in v4:
time: 27.8 us; the launch traced here: 27.6 us
  starting transfers between devices  12.9 us (46%)
  Pallas kernels  7.24 us (26%)
  waiting for transfers between devices  5.84 us (21%)
  local copies, waits for them, and re-layouts  0.9 us (3%)
  between operations  0.7 us (3%)
    ppermute x7, waiting for transfers between devices, crossed(): return lax.ppermute(value, ('col', 'layer'), pairs)  5.76 us
    ppermute x7, starting transfers between devices, crossed(): return lax.ppermute(value, ('col', 'layer'), pairs)  4.58 us
    ppermute x3, starting transfers between devices, on_device(): lax.ppermute(mine, 'row', [(i, i ^ step) for i in range(num_row)])  4.45 us
    ppermute x2, starting transfers between devices, shifted(): lax.ppermute(value, axis, [(i, (i + step) % count) for i in range(count)])  3.88 us
    pallas_call x1, Pallas kernels, rims(): pl.pallas_call(functools.partial(rims_kernel, num_col, num_layer, len(arr...  2.37 us
    pallas_call x1, Pallas kernels, prepare(): pl.pallas_call(functools.partial(prepare_kernel, paired), out_shape=outs,...  2.28 us
    pallas_call x1, Pallas kernels, multiply(): pl.pallas_call(functools.partial(product_kernel, num_row, num_col, num_la...  0.98 us
    pallas_call x1, Pallas kernels, core_part(): pl.pallas_call(functools.partial(core_kernel, num_col, num_layer, len(arr...  0.92 us
  transfers between devices with their start and end apart: 12, of which 4 were waited for; matrix products, arithmetic and copies ran while one was open for 0% of the time, Pallas kernels for 16%

profile of v4, /device:TPU:0, one launch (start us, length us, event | category | flops | bytes accessed | tf_op | source)
XLA Modules:
  0.0 27.6 jit_solution(10762969585359999080)
XLA Ops:
  0.6 2.3 %prepare.1 = (bf16[208,256]{1,0:T(8,128)(2,1)}, bf16[272,256]{1,0:T(8,128)(2,1)}, bf16[272,256]{1,0:T(8,128)(2,1)}) custom-call(bf16[256,128]{1,0:T(8,128)(2,1)} %bitcast.13, s32[4,8]{1,0:T(4,128)} %bitcast.20, bf16[64,512]{1,0:T(8,128)(2,1)} %bitcast.14, s32[2,16]{1,0:T(2,128)} %bitcast.21, s32[8,128]{1,0:T(8,128)} %bitcast.15, s32[8,128]{1,0:T(8,128)} %bitcast.16, ...), custom_call_target="tpu_custom_call" | custom-call | tf_op jit(solution)/shard_map/prepare/pallas_call | solution.py:150
  2.9 3.0 %collective-permute-start.1 = (bf16[272,256]{1,0:T(8,128)(2,1)}, bf16[272,256]{1,0:T(8,128)(2,1)S(1)}, u32[]{:S(2)}, u32[]{:S(2)}) collective-permute-start(bf16[272,256]{1,0:T(8,128)(2,1)} %get-tuple-element.12), channel_id=1, source_target_pairs={{0,2},{1,3},{2,0},{3,1},{4,6},{5,7},{6,4},{7,5},{8,10},{9,11},{10,... | collective-permute-start | bytes 417800 | tf_op jit(solution)/shard_map/ppermute | solution.py:486
  5.9 1.5 %collective-permute-start.3 = (bf16[208,256]{1,0:T(8,128)(2,1)}, bf16[208,256]{1,0:T(8,128)(2,1)S(1)}, u32[]{:S(2)}, u32[]{:S(2)}) collective-permute-start(bf16[208,256]{1,0:T(8,128)(2,1)} %get-tuple-element.13), channel_id=1, source_target_pairs={{0,4},{1,5},{2,6},{3,7},{4,0},{5,1},{6,2},{7,3},{8,12},{9,13},{10,... | collective-permute-start | bytes 319496 | tf_op jit(solution)/shard_map/ppermute | solution.py:486
  7.4 0.0 collective-permute-start.5
  7.5 0.0 collective-permute-start
  7.5 2.5 %collective-permute-done.1.far_ref.refs_2_ = bf16[272,256]{1,0:T(8,128)(2,1)S(1)} collective-permute-done((bf16[272,256]{1,0:T(8,128)(2,1)}, bf16[272,256]{1,0:T(8,128)(2,1)S(1)}, u32[]{:S(2)}, u32[]{:S(2)}) %collective-permute-start.1) | collective-permute-done | bytes 139296 | tf_op jit(solution)/shard_map/ppermute | solution.py:486
  10.0 0.0 collective-permute-start.2
  10.0 1.8 %collective-permute-done.3.refs_4_ = bf16[208,256]{1,0:T(8,128)(2,1)S(1)} collective-permute-done((bf16[208,256]{1,0:T(8,128)(2,1)}, bf16[208,256]{1,0:T(8,128)(2,1)S(1)}, u32[]{:S(2)}, u32[]{:S(2)}) %collective-permute-start.3) | collective-permute-done | bytes 106528 | tf_op jit(solution)/shard_map/ppermute | solution.py:486
  11.7 1.5 %collective-permute-done.5.refs_6_ = bf16[208,256]{1,0:T(8,128)(2,1)S(1)} collective-permute-done((bf16[208,256]{1,0:T(8,128)(2,1)}, bf16[208,256]{1,0:T(8,128)(2,1)S(1)}, u32[]{:S(2)}, u32[]{:S(2)}) %collective-permute-start.5) | collective-permute-done | bytes 106528 | tf_op jit(solution)/shard_map/ppermute | solution.py:486
  13.3 0.0 collective-permute-start.6
  13.3 0.0 collective-permute-done.near_ref.refs_1_
  13.3 0.0 collective-permute-done.2.both_ref.refs_3_
  13.3 0.9 %copy-done = bf16[272,256]{1,0:T(8,128)(2,1)S(1)} copy-done((bf16[272,256]{1,0:T(8,128)(2,1)S(1)}, bf16[272,256]{1,0:T(8,128)(2,1)}, u32[]{:S(2)}) %copy-start) | copy-done | bytes 139288
  14.2 1.6 %collective-permute-start.7 = (bf16[4,64,128]{2,1,0:T(8,128)(2,1)S(1)}, bf16[4,64,128]{2,1,0:T(8,128)(2,1)S(1)}, u32[]{:S(2)}, u32[]{:S(2)}) collective-permute-start(bf16[4,64,128]{2,1,0:T(8,128)(2,1)S(1)} %stack.1.refs_8_), channel_id=1, source_target_pairs={{0,8},{8,0},{16,24},{24,16},{1,9},{9,1},{17,25},{25,17},{2,10},{10... | collective-permute-start | bytes 196616 | tf_op jit(solution)/shard_map/ppermute | solution.py:515
  15.8 2.6 %collective-permute-start.8 = (bf16[4,64,128]{2,1,0:T(8,128)(2,1)S(1)}, bf16[4,64,128]{2,1,0:T(8,128)(2,1)S(1)}, u32[]{:S(2)}, u32[]{:S(2)}) collective-permute-start(bf16[4,64,128]{2,1,0:T(8,128)(2,1)S(1)} %stack.1.refs_8_), channel_id=1, source_target_pairs={{0,16},{8,24},{16,0},{24,8},{1,17},{9,25},{17,1},{25,9},{2,18},{10... | collective-permute-start | bytes 196616 | tf_op jit(solution)/shard_map/ppermute | solution.py:515
  18.4 0.2 collective-permute-start.9
  18.6 0.0 collective-permute-done.4.refs_5_
  18.7 2.4 %rims.1 = (f32[64,128]{1,0:T(8,128)S(1)}, f32[64,128]{1,0:T(8,128)S(1)}, bf16[256,2560]{1,0:T(8,128)(2,1)S(1)}, f32[256,128]{1,0:T(8,128)S(1)}) custom-call(bf16[272,256]{1,0:T(8,128)(2,1)S(1)} %copy-done, bf16[272,256]{1,0:T(8,128)(2,1)S(1)} %collective-permute-done.near_ref.refs_1_, bf16[272,256]{1,0:T(8,128)(2,1)S(1)} %collective-permute-done.1.far_ref.refs_2_, ...), custom_call_target="tpu_custom_call" | custom-call | flops 3000000000 | bytes 1000000 | tf_op jit(solution)/shard_map/rims/pallas_call | solution.py:351
  21.0 0.7 %collective-permute-start.10 = (f32[64,128]{1,0:T(8,128)S(1)}, f32[64,128]{1,0:T(8,128)S(1)}, u32[]{:S(2)}, u32[]{:S(2)}) collective-permute-start(f32[64,128]{1,0:T(8,128)S(1)} %get-tuple-element.17), channel_id=1, source_target_pairs={{0,8},{8,16},{16,24},{24,0},{1,9},{9,17},{17,25},{25,1},{2,10},{10... | collective-permute-start | bytes 98312 | tf_op jit(solution)/shard_map/ppermute | solution.py:481
  21.8 3.1 %collective-permute-start.11 = (f32[64,128]{1,0:T(8,128)S(1)}, f32[64,128]{1,0:T(8,128)S(1)}, u32[]{:S(2)}, u32[]{:S(2)}) collective-permute-start(f32[64,128]{1,0:T(8,128)S(1)} %get-tuple-element.18), channel_id=1, source_target_pairs={{0,24},{8,0},{16,8},{24,16},{1,25},{9,1},{17,9},{25,17},{2,26},{10... | collective-permute-start | bytes 98312 | tf_op jit(solution)/shard_map/ppermute | solution.py:481
  24.9 0.9 %core.1.core_ref = f32[256,128]{1,0:T(8,128)S(1)} custom-call(bf16[272,256]{1,0:T(8,128)(2,1)S(1)} %copy-done, bf16[272,256]{1,0:T(8,128)(2,1)S(1)} %collective-permute-done.near_ref.refs_1_, bf16[272,256]{1,0:T(8,128)(2,1)S(1)} %collective-permute-done.1.far_ref.refs_2_, bf16[272,256]{1,0:T(8,128)(2,1)S(1)} %collective-permute-done.2.both_ref.refs_3_, ...), custom_call_target="tpu_custom_call" | custom-call | flops 1500000000 | bytes 1000000 | tf_op jit(solution)/shard_map/core/pallas_call | solution.py:390
  25.9 1.0 %multiply.1 = (bf16[256,128]{1,0:T(8,128)(2,1)}, f32[8,128]{1,0:T(8,128)S(1)}) custom-call(bf16[272,256]{1,0:T(8,128)(2,1)S(1)} %copy-done, bf16[272,256]{1,0:T(8,128)(2,1)S(1)} %collective-permute-done.near_ref.refs_1_, bf16[272,256]{1,0:T(8,128)(2,1)S(1)} %collective-permute-done.1.far_ref.refs_2_, ...), custom_call_target="tpu_custom_call" | custom-call | flops 500000000 | bytes 1000000 | tf_op jit(solution)/shard_map/multiply/pallas_call | solution.py:429
  26.9 0.1 collective-permute-done.10.below_ref
  26.9 0.7 %fold.1 = f32[256,128]{1,0:T(8,128)} custom-call(f32[256,128]{1,0:T(8,128)S(1)} %core.1.core_ref, f32[64,128]{1,0:T(8,128)S(1)} %collective-permute-done.10.below_ref, f32[64,128]{1,0:T(8,128)S(1)} %collective-permute-done.11.above_ref, f32[8,128]{1,0:T(8,128)S(1)} %get-tuple-element.19.after_ref), custom_call_target="tpu_custom_call" | custom-call | flops 1000000 | bytes 400000 | tf_op jit(solution)/shard_map/fold/pallas_call | solution.py:469
  (8 shorter events, 0.0 us)
Async XLA Ops:
  2.9 7.0 %collective-permute-start.1 = (bf16[272,256]{1,0:T(8,128)(2,1)}, bf16[272,256]{1,0:T(8,128)(2,1)S(1)}, u32[]{:S(2)}, u32[]{:S(2)}) collective-permute-start(bf16[272,256]{1,0:T(8,128)(2,1)} %get-tuple-element.12), channel_id=1, source_target_pairs={{0,2},{1,3},{2,0},{3,1},{4,6},{5,7},{6,4},{7,5},{8,10},{9,11},{10,... | collective-permute-start | bytes 417800 | tf_op jit(solution)/shard_map/ppermute | solution.py:486
  5.9 5.8 %collective-permute-start.3 = (bf16[208,256]{1,0:T(8,128)(2,1)}, bf16[208,256]{1,0:T(8,128)(2,1)S(1)}, u32[]{:S(2)}, u32[]{:S(2)}) collective-permute-start(bf16[208,256]{1,0:T(8,128)(2,1)} %get-tuple-element.13), channel_id=1, source_target_pairs={{0,4},{1,5},{2,6},{3,7},{4,0},{5,1},{6,2},{7,3},{8,12},{9,13},{10,... | collective-permute-start | bytes 319496 | tf_op jit(solution)/shard_map/ppermute | solution.py:486
  7.4 5.8 %collective-permute-start.5 = (bf16[208,256]{1,0:T(8,128)(2,1)}, bf16[208,256]{1,0:T(8,128)(2,1)S(1)}, u32[]{:S(2)}, u32[]{:S(2)}) collective-permute-start(bf16[208,256]{1,0:T(8,128)(2,1)} %get-tuple-element.13), channel_id=1, source_target_pairs={{0,6},{1,7},{2,4},{3,5},{4,2},{5,3},{6,0},{7,1},{8,14},{9,15},{10,... | collective-permute-start | bytes 319496 | tf_op jit(solution)/shard_map/ppermute | solution.py:486
  7.5 5.8 %collective-permute-start = (bf16[272,256]{1,0:T(8,128)(2,1)}, bf16[272,256]{1,0:T(8,128)(2,1)S(1)}, u32[]{:S(2)}, u32[]{:S(2)}) collective-permute-start(bf16[272,256]{1,0:T(8,128)(2,1)} %get-tuple-element.11.own_ref.refs_0_), channel_id=1, source_target_pairs={{0,1},{1,0},{2,3},{3,2},{4,5},{5,4},{6,7},{7,6},{8,9},{9,8},{10,11... | collective-permute-start | bytes 417800 | tf_op jit(solution)/shard_map/ppermute | solution.py:486
  10.0 3.3 %collective-permute-start.2 = (bf16[272,256]{1,0:T(8,128)(2,1)S(1)}, bf16[272,256]{1,0:T(8,128)(2,1)S(1)}, u32[]{:S(2)}, u32[]{:S(2)}) collective-permute-start(bf16[272,256]{1,0:T(8,128)(2,1)S(1)} %collective-permute-done.1.far_ref.refs_2_), channel_id=1, source_target_pairs={{0,1},{1,0},{2,3},{3,2},{4,5},{5,4},{6,7},{7,6},{8,9},{9,8},{10,11... | collective-permute-start | bytes 417800 | tf_op jit(solution)/shard_map/ppermute | solution.py:486
  11.7 6.9 %collective-permute-start.4 = (bf16[208,256]{1,0:T(8,128)(2,1)S(1)}, bf16[208,256]{1,0:T(8,128)(2,1)S(1)}, u32[]{:S(2)}, u32[]{:S(2)}) collective-permute-start(bf16[208,256]{1,0:T(8,128)(2,1)S(1)} %collective-permute-done.3.refs_4_), channel_id=1, source_target_pairs={{0,1},{1,0},{2,3},{3,2},{4,5},{5,4},{6,7},{7,6},{8,9},{9,8},{10,11... | collective-permute-start | bytes 319496 | tf_op jit(solution)/shard_map/ppermute | solution.py:486
  13.3 5.4 %collective-permute-start.6 = (bf16[208,256]{1,0:T(8,128)(2,1)S(1)}, bf16[208,256]{1,0:T(8,128)(2,1)S(1)}, u32[]{:S(2)}, u32[]{:S(2)}) collective-permute-start(bf16[208,256]{1,0:T(8,128)(2,1)S(1)} %collective-permute-done.5.refs_6_), channel_id=1, source_target_pairs={{0,1},{1,0},{2,3},{3,2},{4,5},{5,4},{6,7},{7,6},{8,9},{9,8},{10,11... | collective-permute-start | bytes 319496 | tf_op jit(solution)/shard_map/ppermute | solution.py:486
  13.3 0.9 %copy-start = (bf16[272,256]{1,0:T(8,128)(2,1)S(1)}, bf16[272,256]{1,0:T(8,128)(2,1)}, u32[]{:S(2)}) copy-start(bf16[272,256]{1,0:T(8,128)(2,1)} %get-tuple-element.11.own_ref.refs_0_) | copy-start | bytes 417796
  14.2 11.6 %collective-permute-start.7 = (bf16[4,64,128]{2,1,0:T(8,128)(2,1)S(1)}, bf16[4,64,128]{2,1,0:T(8,128)(2,1)S(1)}, u32[]{:S(2)}, u32[]{:S(2)}) collective-permute-start(bf16[4,64,128]{2,1,0:T(8,128)(2,1)S(1)} %stack.1.refs_8_), channel_id=1, source_target_pairs={{0,8},{8,0},{16,24},{24,16},{1,9},{9,1},{17,25},{25,17},{2,10},{10... | collective-permute-start | bytes 196616 | tf_op jit(solution)/shard_map/ppermute | solution.py:515
  15.8 10.0 %collective-permute-start.8 = (bf16[4,64,128]{2,1,0:T(8,128)(2,1)S(1)}, bf16[4,64,128]{2,1,0:T(8,128)(2,1)S(1)}, u32[]{:S(2)}, u32[]{:S(2)}) collective-permute-start(bf16[4,64,128]{2,1,0:T(8,128)(2,1)S(1)} %stack.1.refs_8_), channel_id=1, source_target_pairs={{0,16},{8,24},{16,0},{24,8},{1,17},{9,25},{17,1},{25,9},{2,18},{10... | collective-permute-start | bytes 196616 | tf_op jit(solution)/shard_map/ppermute | solution.py:515
  18.4 7.4 %collective-permute-start.9 = (bf16[4,64,128]{2,1,0:T(8,128)(2,1)S(1)}, bf16[4,64,128]{2,1,0:T(8,128)(2,1)S(1)}, u32[]{:S(2)}, u32[]{:S(2)}) collective-permute-start(bf16[4,64,128]{2,1,0:T(8,128)(2,1)S(1)} %stack.1.refs_8_), channel_id=1, source_target_pairs={{0,24},{8,16},{16,8},{24,0},{1,25},{9,17},{17,9},{25,1},{2,26},{10... | collective-permute-start | bytes 196616 | tf_op jit(solution)/shard_map/ppermute | solution.py:515
  21.0 5.9 %collective-permute-start.10 = (f32[64,128]{1,0:T(8,128)S(1)}, f32[64,128]{1,0:T(8,128)S(1)}, u32[]{:S(2)}, u32[]{:S(2)}) collective-permute-start(f32[64,128]{1,0:T(8,128)S(1)} %get-tuple-element.17), channel_id=1, source_target_pairs={{0,8},{8,16},{16,24},{24,0},{1,9},{9,17},{17,25},{25,1},{2,10},{10... | collective-permute-start | bytes 98312 | tf_op jit(solution)/shard_map/ppermute | solution.py:481
  21.8 5.2 %collective-permute-start.11 = (f32[64,128]{1,0:T(8,128)S(1)}, f32[64,128]{1,0:T(8,128)S(1)}, u32[]{:S(2)}, u32[]{:S(2)}) collective-permute-start(f32[64,128]{1,0:T(8,128)S(1)} %get-tuple-element.18), channel_id=1, source_target_pairs={{0,24},{8,0},{16,8},{24,16},{1,25},{9,1},{17,9},{25,17},{2,26},{10... | collective-permute-start | bytes 98312 | tf_op jit(solution)/shard_map/ppermute | solution.py:481

commit v5 on v4

--- a/solution.py
+++ b/solution.py
@@ -441,6 +441,22 @@
     )(*arrays, *parts)
 
 
+def settle_kernel(block_ref, out_ref):
+    out_ref[...] = block_ref[...]
+
+
+def settle(block):
+    return pl.pallas_call(
+        settle_kernel,
+        out_shape=jax.ShapeDtypeStruct(block.shape, BF16),
+        in_specs=[VMEM],
+        out_specs=VMEM,
+        compiler_params=PARAMS,
+        cost_estimate=pl.CostEstimate(flops=1000, bytes_accessed=1000, transcendentals=0),
+        name="settle",
+    )(block)
+
+
 def stack_kernel(own_ref, near_ref, far_ref, both_ref, out_ref):
     out_ref[0] = own_ref[BASE:, LANES:UNIT]
     out_ref[1] = near_ref[BASE:, 0:LANES]
@@ -503,7 +519,7 @@
     flat = [x.reshape(8, LANES) for x in (gauss_row, gauss_col, gauss_cell, gauss_expo, gauss_pref)]
     made = prepare(paired, p_slabs[0], p_mask[0].T, h_slabs[0], h_mask[0], *flat)
     if paired:
-        arrays = gather_paired(*made)
+        arrays = gather_paired(*made[:2], settle(made[2]))
         mine = stack(*arrays[:4])
     else:
         base, pieces = made

time: 27.8 us -> 26.9 us (0.968)
  waiting for transfers between devices: 5.84 us -> 4.86 us
    ppermute x7, waiting for transfers between devices: 5.76 us -> 4.77 us  [crossed(): return lax.ppermute(value, ('col', 'layer'), pairs)]
where the time goes in v5:
time: 26.9 us; the launch traced here: 26.7 us
  starting transfers between devices  13 us (48%)
  Pallas kernels  7.26 us (27%)
  waiting for transfers between devices  4.86 us (18%)
  local copies, waits for them, and re-layouts  0.91 us (3%)
  between operations  0.71 us (3%)
    ppermute x7, waiting for transfers between devices, crossed(): return lax.ppermute(value, ('col', 'layer'), pairs)  4.77 us
    ppermute x7, starting transfers between devices, crossed(): return lax.ppermute(value, ('col', 'layer'), pairs)  4.65 us
    ppermute x3, starting transfers between devices, on_device(): lax.ppermute(mine, 'row', [(i, i ^ step) for i in range(num_row)])  4.45 us
    ppermute x2, starting transfers between devices, shifted(): lax.ppermute(value, axis, [(i, (i + step) % count) for i in range(count)])  3.88 us
    pallas_call x1, Pallas kernels, rims(): pl.pallas_call(functools.partial(rims_kernel, num_col, num_layer, len(arr...  2.39 us
    pallas_call x1, Pallas kernels, prepare(): pl.pallas_call(functools.partial(prepare_kernel, paired), out_shape=outs,...  2.28 us
    pallas_call x1, Pallas kernels, multiply(): pl.pallas_call(functools.partial(product_kernel, num_row, num_col, num_la...  0.98 us
    pallas_call x1, Pallas kernels, core_part(): pl.pallas_call(functools.partial(core_kernel, num_col, num_layer, len(arr...  0.92 us
  transfers between devices with their start and end apart: 12, of which 4 were waited for; matrix products, arithmetic and copies ran while one was open for 0% of the time, Pallas kernels for 16%

profile of v5, /device:TPU:0, one launch (start us, length us, event | category | flops | bytes accessed | tf_op | source)
XLA Modules:
  0.0 26.7 jit_solution(11449849305839020950)
XLA Ops:
  0.6 2.3 %prepare.1 = (bf16[208,256]{1,0:T(8,128)(2,1)}, bf16[272,256]{1,0:T(8,128)(2,1)}, bf16[272,256]{1,0:T(8,128)(2,1)}) custom-call(bf16[256,128]{1,0:T(8,128)(2,1)} %bitcast.13, s32[4,8]{1,0:T(4,128)} %bitcast.20, bf16[64,512]{1,0:T(8,128)(2,1)} %bitcast.14, s32[2,16]{1,0:T(2,128)} %bitcast.21, s32[8,128]{1,0:T(8,128)} %bitcast.15, s32[8,128]{1,0:T(8,128)} %bitcast.16, ...), custom_call_target="tpu_custom_call" | custom-call | tf_op jit(solution)/shard_map/prepare/pallas_call | solution.py:150
  2.9 3.0 %collective-permute-start.1 = (bf16[272,256]{1,0:T(8,128)(2,1)}, bf16[272,256]{1,0:T(8,128)(2,1)S(1)}, u32[]{:S(2)}, u32[]{:S(2)}) collective-permute-start(bf16[272,256]{1,0:T(8,128)(2,1)} %get-tuple-element.12), channel_id=1, source_target_pairs={{0,2},{1,3},{2,0},{3,1},{4,6},{5,7},{6,4},{7,5},{8,10},{9,11},{10,... | collective-permute-start | bytes 417800 | tf_op jit(solution)/shard_map/ppermute | solution.py:502
  5.9 1.5 %collective-permute-start.3 = (bf16[208,256]{1,0:T(8,128)(2,1)}, bf16[208,256]{1,0:T(8,128)(2,1)S(1)}, u32[]{:S(2)}, u32[]{:S(2)}) collective-permute-start(bf16[208,256]{1,0:T(8,128)(2,1)} %get-tuple-element.13), channel_id=1, source_target_pairs={{0,4},{1,5},{2,6},{3,7},{4,0},{5,1},{6,2},{7,3},{8,12},{9,13},{10,... | collective-permute-start | bytes 319496 | tf_op jit(solution)/shard_map/ppermute | solution.py:502
  7.4 0.0 collective-permute-start.5
  7.5 0.9 %copy-done = bf16[272,256]{1,0:T(8,128)(2,1)S(1)} copy-done((bf16[272,256]{1,0:T(8,128)(2,1)S(1)}, bf16[272,256]{1,0:T(8,128)(2,1)}, u32[]{:S(2)}) %copy-start) | copy-done | bytes 139288
  8.4 0.1 collective-permute-start
  8.5 1.5 %collective-permute-done.1.far_ref.refs_2_ = bf16[272,256]{1,0:T(8,128)(2,1)S(1)} collective-permute-done((bf16[272,256]{1,0:T(8,128)(2,1)}, bf16[272,256]{1,0:T(8,128)(2,1)S(1)}, u32[]{:S(2)}, u32[]{:S(2)}) %collective-permute-start.1) | collective-permute-done | bytes 139296 | tf_op jit(solution)/shard_map/ppermute | solution.py:502
  10.0 1.8 %collective-permute-done.3.refs_4_ = bf16[208,256]{1,0:T(8,128)(2,1)S(1)} collective-permute-done((bf16[208,256]{1,0:T(8,128)(2,1)}, bf16[208,256]{1,0:T(8,128)(2,1)S(1)}, u32[]{:S(2)}, u32[]{:S(2)}) %collective-permute-start.3) | collective-permute-done | bytes 106528 | tf_op jit(solution)/shard_map/ppermute | solution.py:502
  11.7 0.0 collective-permute-start.4
  11.7 1.5 %collective-permute-done.5.refs_6_ = bf16[208,256]{1,0:T(8,128)(2,1)S(1)} collective-permute-done((bf16[208,256]{1,0:T(8,128)(2,1)}, bf16[208,256]{1,0:T(8,128)(2,1)S(1)}, u32[]{:S(2)}, u32[]{:S(2)}) %collective-permute-start.5) | collective-permute-done | bytes 106528 | tf_op jit(solution)/shard_map/ppermute | solution.py:502
  13.3 0.0 collective-permute-start.6
  13.3 0.0 collective-permute-done.near_ref.refs_1_
  13.3 0.0 collective-permute-done.2.both_ref.refs_3_
  13.3 1.6 %collective-permute-start.7 = (bf16[4,64,128]{2,1,0:T(8,128)(2,1)S(1)}, bf16[4,64,128]{2,1,0:T(8,128)(2,1)S(1)}, u32[]{:S(2)}, u32[]{:S(2)}) collective-permute-start(bf16[4,64,128]{2,1,0:T(8,128)(2,1)S(1)} %stack.1.refs_8_), channel_id=1, source_target_pairs={{0,8},{8,0},{16,24},{24,16},{1,9},{9,1},{17,25},{25,17},{2,10},{10... | collective-permute-start | bytes 196616 | tf_op jit(solution)/shard_map/ppermute | solution.py:531
  14.9 2.6 %collective-permute-start.8 = (bf16[4,64,128]{2,1,0:T(8,128)(2,1)S(1)}, bf16[4,64,128]{2,1,0:T(8,128)(2,1)S(1)}, u32[]{:S(2)}, u32[]{:S(2)}) collective-permute-start(bf16[4,64,128]{2,1,0:T(8,128)(2,1)S(1)} %stack.1.refs_8_), channel_id=1, source_target_pairs={{0,16},{8,24},{16,0},{24,8},{1,17},{9,25},{17,1},{25,9},{2,18},{10... | collective-permute-start | bytes 196616 | tf_op jit(solution)/shard_map/ppermute | solution.py:531
  17.5 0.2 collective-permute-start.9
  17.7 0.0 collective-permute-done.4.refs_5_
  17.7 2.4 %rims.1 = (f32[64,128]{1,0:T(8,128)S(1)}, f32[64,128]{1,0:T(8,128)S(1)}, bf16[256,2560]{1,0:T(8,128)(2,1)S(1)}, f32[256,128]{1,0:T(8,128)S(1)}) custom-call(bf16[272,256]{1,0:T(8,128)(2,1)S(1)} %settle.1.own_ref.refs_0_, bf16[272,256]{1,0:T(8,128)(2,1)S(1)} %collective-permute-done.near_ref.refs_1_, ...), custom_call_target="tpu_custom_call" | custom-call | flops 3000000000 | bytes 1000000 | tf_op jit(solution)/shard_map/rims/pallas_call | solution.py:351
  20.1 0.7 %collective-permute-start.10 = (f32[64,128]{1,0:T(8,128)S(1)}, f32[64,128]{1,0:T(8,128)S(1)}, u32[]{:S(2)}, u32[]{:S(2)}) collective-permute-start(f32[64,128]{1,0:T(8,128)S(1)} %get-tuple-element.17), channel_id=1, source_target_pairs={{0,8},{8,16},{16,24},{24,0},{1,9},{9,17},{17,25},{25,1},{2,10},{10... | collective-permute-start | bytes 98312 | tf_op jit(solution)/shard_map/ppermute | solution.py:497
  20.9 3.1 %collective-permute-start.11 = (f32[64,128]{1,0:T(8,128)S(1)}, f32[64,128]{1,0:T(8,128)S(1)}, u32[]{:S(2)}, u32[]{:S(2)}) collective-permute-start(f32[64,128]{1,0:T(8,128)S(1)} %get-tuple-element.18), channel_id=1, source_target_pairs={{0,24},{8,0},{16,8},{24,16},{1,25},{9,1},{17,9},{25,17},{2,26},{10... | collective-permute-start | bytes 98312 | tf_op jit(solution)/shard_map/ppermute | solution.py:497
  24.0 0.9 %core.1.core_ref = f32[256,128]{1,0:T(8,128)S(1)} custom-call(bf16[272,256]{1,0:T(8,128)(2,1)S(1)} %settle.1.own_ref.refs_0_, bf16[272,256]{1,0:T(8,128)(2,1)S(1)} %collective-permute-done.near_ref.refs_1_, bf16[272,256]{1,0:T(8,128)(2,1)S(1)} %collective-permute-done.1.far_ref.refs_2_, bf16[272,256]{1,0:T(8,128)(2,1)S(1)} %collective-permute-done.2.both_ref.refs_3_, ...), custom_call_target="tpu_custom_call" | custom-call | flops 1500000000 | bytes 1000000 | tf_op jit(solution)/shard_map/core/pallas_call | solution.py:390
  25.0 1.0 %multiply.1 = (bf16[256,128]{1,0:T(8,128)(2,1)}, f32[8,128]{1,0:T(8,128)S(1)}) custom-call(bf16[272,256]{1,0:T(8,128)(2,1)S(1)} %settle.1.own_ref.refs_0_, bf16[272,256]{1,0:T(8,128)(2,1)S(1)} %collective-permute-done.near_ref.refs_1_, bf16[272,256]{1,0:T(8,128)(2,1)S(1)} %collective-permute-done.1.far_ref.refs_2_, ...), custom_call_target="tpu_custom_call" | custom-call | flops 500000000 | bytes 1000000 | tf_op jit(solution)/shard_map/multiply/pallas_call | solution.py:429
  26.0 0.1 collective-permute-done.10.below_ref
  26.0 0.7 %fold.1 = f32[256,128]{1,0:T(8,128)} custom-call(f32[256,128]{1,0:T(8,128)S(1)} %core.1.core_ref, f32[64,128]{1,0:T(8,128)S(1)} %collective-permute-done.10.below_ref, f32[64,128]{1,0:T(8,128)S(1)} %collective-permute-done.11.above_ref, f32[8,128]{1,0:T(8,128)S(1)} %get-tuple-element.19.after_ref), custom_call_target="tpu_custom_call" | custom-call | flops 1000000 | bytes 400000 | tf_op jit(solution)/shard_map/fold/pallas_call | solution.py:485
  (9 shorter events, 0.0 us)
Async XLA Ops:
  2.9 7.0 %collective-permute-start.1 = (bf16[272,256]{1,0:T(8,128)(2,1)}, bf16[272,256]{1,0:T(8,128)(2,1)S(1)}, u32[]{:S(2)}, u32[]{:S(2)}) collective-permute-start(bf16[272,256]{1,0:T(8,128)(2,1)} %get-tuple-element.12), channel_id=1, source_target_pairs={{0,2},{1,3},{2,0},{3,1},{4,6},{5,7},{6,4},{7,5},{8,10},{9,11},{10,... | collective-permute-start | bytes 417800 | tf_op jit(solution)/shard_map/ppermute | solution.py:502
  5.9 5.8 %collective-permute-start.3 = (bf16[208,256]{1,0:T(8,128)(2,1)}, bf16[208,256]{1,0:T(8,128)(2,1)S(1)}, u32[]{:S(2)}, u32[]{:S(2)}) collective-permute-start(bf16[208,256]{1,0:T(8,128)(2,1)} %get-tuple-element.13), channel_id=1, source_target_pairs={{0,4},{1,5},{2,6},{3,7},{4,0},{5,1},{6,2},{7,3},{8,12},{9,13},{10,... | collective-permute-start | bytes 319496 | tf_op jit(solution)/shard_map/ppermute | solution.py:502
  7.4 5.8 %collective-permute-start.5 = (bf16[208,256]{1,0:T(8,128)(2,1)}, bf16[208,256]{1,0:T(8,128)(2,1)S(1)}, u32[]{:S(2)}, u32[]{:S(2)}) collective-permute-start(bf16[208,256]{1,0:T(8,128)(2,1)} %get-tuple-element.13), channel_id=1, source_target_pairs={{0,6},{1,7},{2,4},{3,5},{4,2},{5,3},{6,0},{7,1},{8,14},{9,15},{10,... | collective-permute-start | bytes 319496 | tf_op jit(solution)/shard_map/ppermute | solution.py:502
  7.5 0.9 %copy-start = (bf16[272,256]{1,0:T(8,128)(2,1)S(1)}, bf16[272,256]{1,0:T(8,128)(2,1)}, u32[]{:S(2)}) copy-start(bf16[272,256]{1,0:T(8,128)(2,1)} %get-tuple-element.11.block_ref) | copy-start | bytes 417796
  8.4 4.9 %collective-permute-start = (bf16[272,256]{1,0:T(8,128)(2,1)S(1)}, bf16[272,256]{1,0:T(8,128)(2,1)S(1)}, u32[]{:S(2)}, u32[]{:S(2)}) collective-permute-start(bf16[272,256]{1,0:T(8,128)(2,1)S(1)} %settle.1.own_ref.refs_0_), channel_id=1, source_target_pairs={{0,1},{1,0},{2,3},{3,2},{4,5},{5,4},{6,7},{7,6},{8,9},{9,8},{10,11... | collective-permute-start | bytes 417800 | tf_op jit(solution)/shard_map/ppermute | solution.py:502
  10.0 3.3 %collective-permute-start.2 = (bf16[272,256]{1,0:T(8,128)(2,1)S(1)}, bf16[272,256]{1,0:T(8,128)(2,1)S(1)}, u32[]{:S(2)}, u32[]{:S(2)}) collective-permute-start(bf16[272,256]{1,0:T(8,128)(2,1)S(1)} %collective-permute-done.1.far_ref.refs_2_), channel_id=1, source_target_pairs={{0,1},{1,0},{2,3},{3,2},{4,5},{5,4},{6,7},{7,6},{8,9},{9,8},{10,11... | collective-permute-start | bytes 417800 | tf_op jit(solution)/shard_map/ppermute | solution.py:502
  11.7 6.0 %collective-permute-start.4 = (bf16[208,256]{1,0:T(8,128)(2,1)S(1)}, bf16[208,256]{1,0:T(8,128)(2,1)S(1)}, u32[]{:S(2)}, u32[]{:S(2)}) collective-permute-start(bf16[208,256]{1,0:T(8,128)(2,1)S(1)} %collective-permute-done.3.refs_4_), channel_id=1, source_target_pairs={{0,1},{1,0},{2,3},{3,2},{4,5},{5,4},{6,7},{7,6},{8,9},{9,8},{10,11... | collective-permute-start | bytes 319496 | tf_op jit(solution)/shard_map/ppermute | solution.py:502
  13.3 4.5 %collective-permute-start.6 = (bf16[208,256]{1,0:T(8,128)(2,1)S(1)}, bf16[208,256]{1,0:T(8,128)(2,1)S(1)}, u32[]{:S(2)}, u32[]{:S(2)}) collective-permute-start(bf16[208,256]{1,0:T(8,128)(2,1)S(1)} %collective-permute-done.5.refs_6_), channel_id=1, source_target_pairs={{0,1},{1,0},{2,3},{3,2},{4,5},{5,4},{6,7},{7,6},{8,9},{9,8},{10,11... | collective-permute-start | bytes 319496 | tf_op jit(solution)/shard_map/ppermute | solution.py:502
  13.3 11.7 %collective-permute-start.7 = (bf16[4,64,128]{2,1,0:T(8,128)(2,1)S(1)}, bf16[4,64,128]{2,1,0:T(8,128)(2,1)S(1)}, u32[]{:S(2)}, u32[]{:S(2)}) collective-permute-start(bf16[4,64,128]{2,1,0:T(8,128)(2,1)S(1)} %stack.1.refs_8_), channel_id=1, source_target_pairs={{0,8},{8,0},{16,24},{24,16},{1,9},{9,1},{17,25},{25,17},{2,10},{10... | collective-permute-start | bytes 196616 | tf_op jit(solution)/shard_map/ppermute | solution.py:531
  14.9 10.0 %collective-permute-start.8 = (bf16[4,64,128]{2,1,0:T(8,128)(2,1)S(1)}, bf16[4,64,128]{2,1,0:T(8,128)(2,1)S(1)}, u32[]{:S(2)}, u32[]{:S(2)}) collective-permute-start(bf16[4,64,128]{2,1,0:T(8,128)(2,1)S(1)} %stack.1.refs_8_), channel_id=1, source_target_pairs={{0,16},{8,24},{16,0},{24,8},{1,17},{9,25},{17,1},{25,9},{2,18},{10... | collective-permute-start | bytes 196616 | tf_op jit(solution)/shard_map/ppermute | solution.py:531
  17.5 7.5 %collective-permute-start.9 = (bf16[4,64,128]{2,1,0:T(8,128)(2,1)S(1)}, bf16[4,64,128]{2,1,0:T(8,128)(2,1)S(1)}, u32[]{:S(2)}, u32[]{:S(2)}) collective-permute-start(bf16[4,64,128]{2,1,0:T(8,128)(2,1)S(1)} %stack.1.refs_8_), channel_id=1, source_target_pairs={{0,24},{8,16},{16,8},{24,0},{1,25},{9,17},{17,9},{25,1},{2,26},{10... | collective-permute-start | bytes 196616 | tf_op jit(solution)/shard_map/ppermute | solution.py:531
  20.1 5.9 %collective-permute-start.10 = (f32[64,128]{1,0:T(8,128)S(1)}, f32[64,128]{1,0:T(8,128)S(1)}, u32[]{:S(2)}, u32[]{:S(2)}) collective-permute-start(f32[64,128]{1,0:T(8,128)S(1)} %get-tuple-element.17), channel_id=1, source_target_pairs={{0,8},{8,16},{16,24},{24,0},{1,9},{9,17},{17,25},{25,1},{2,10},{10... | collective-permute-start | bytes 98312 | tf_op jit(solution)/shard_map/ppermute | solution.py:497
  20.9 5.2 %collective-permute-start.11 = (f32[64,128]{1,0:T(8,128)S(1)}, f32[64,128]{1,0:T(8,128)S(1)}, u32[]{:S(2)}, u32[]{:S(2)}) collective-permute-start(f32[64,128]{1,0:T(8,128)S(1)} %get-tuple-element.18), channel_id=1, source_target_pairs={{0,24},{8,0},{16,8},{24,16},{1,25},{9,1},{17,9},{25,17},{2,26},{10... | collective-permute-start | bytes 98312 | tf_op jit(solution)/shard_map/ppermute | solution.py:497

commit v6 on v5

--- a/solution.py
+++ b/solution.py
@@ -324,8 +324,13 @@
         set_planes(blocks, tile, which, RIM_X, at, planeh, planel)
         fill_depth(shapes_z(tile, blocks.lifts(pair)), coef, at, depth)
     total = summed(planeh[...], planel[...], depth[...])
-    low_ref[...] = total[0:HALO, :]
-    high_ref[...] = total[HALO:, :]
+    swap = lax.rem(lax.axis_index("row"), 2) * int(lax.axis_size("row") == 4)
+
+    def put(low, high, base_low, base_high):
+        low_ref[...] = jnp.where(swap > 0, high, low) + base_low
+        high_ref[...] = jnp.where(swap > 0, low, high) + base_high
+
+    put(total[0:HALO, :], total[HALO:, :], 0.0, 0.0)
 
     @pl.when(jnp.max(over) > 0)
     def _():
@@ -341,9 +346,8 @@
                 return carry
 
             lax.fori_loop(0, PAIRS, step, 0)
-        low_ref[...] += acc[0:HALO, :]
+        put(acc[0:HALO, :], acc[HALO + CORE : FULL, :], low_ref[...], high_ref[...])
         extra[...] = acc[HALO : HALO + CORE, :]
-        high_ref[...] += acc[HALO + CORE : FULL, :]
 
 
 def rims(arrays, num_col, num_layer):
@@ -476,9 +480,11 @@
 
 
 def fold_kernel(core_ref, below_ref, above_ref, after_ref, out_ref):
-    out_ref[0:HALO, :] = core_ref[0:HALO, :] + below_ref[...]
+    swap = lax.rem(lax.axis_index("row"), 2) * int(lax.axis_size("row") == 4)
+    below, above = below_ref[...], above_ref[...]
+    out_ref[0:HALO, :] = core_ref[0:HALO, :] + jnp.where(swap > 0, above, below)
     out_ref[HALO : CORE - HALO, :] = core_ref[HALO : CORE - HALO, :]
-    out_ref[CORE - HALO : CORE, :] = core_ref[CORE - HALO : CORE, :] + above_ref[...]
+    out_ref[CORE - HALO : CORE, :] = core_ref[CORE - HALO : CORE, :] + jnp.where(swap > 0, below, above)
 
 
 def fold(core, below, above, after):
@@ -530,8 +536,12 @@
     parts = [mine] + [
         lax.ppermute(mine, "row", [(i, i ^ step) for i in range(num_row)]) for step in range(1, num_row)
     ]
-    below = shifted(high, "row", num_row, 1)
-    above = shifted(low, "row", num_row, num_row - 1)
+    if num_row == 4:
+        below = lax.ppermute(low, "row", [(i, i ^ 3) for i in range(4)])
+        above = lax.ppermute(high, "row", [(i, i ^ 1) for i in range(4)])
+    else:
+        below = shifted(high, "row", num_row, 1)
+        above = shifted(low, "row", num_row, num_row - 1)
     core = core_part(arrays, depth, extra, num_col, num_layer)
     product, token = multiply(arrays, parts, num_row, num_col, num_layer)
     density = fold(core, below, above, token).reshape(GX, GY, GZ)

time: 26.9 us -> 28.6 us (1.063)
  waiting for transfers between devices: 4.86 us -> 6.74 us
    ppermute x2, waiting for transfers between devices: 0.08 us -> 1.96 us  [the longest x1 1.8 us: on_device(): above = lax.ppermute(high, 'row', [(i, i ^ 1) for i in range(4)])]
  transfers between devices with their start and end apart: 12 -> 12, of which waited for: 4 -> 5; matrix products, arithmetic and copies ran while one was open for 0% -> 0% of each run, Pallas kernels for 16% -> 15%
where the time goes in v6:
time: 28.6 us; the launch traced here: 28.4 us
  starting transfers between devices  12.8 us (45%)
  Pallas kernels  7.27 us (25%)
  waiting for transfers between devices  6.74 us (24%)
  local copies, waits for them, and re-layouts  0.91 us (3%)
  between operations  0.71 us (2%)
    ppermute x7, waiting for transfers between devices, crossed(): return lax.ppermute(value, ('col', 'layer'), pairs)  4.77 us
    ppermute x7, starting transfers between devices, crossed(): return lax.ppermute(value, ('col', 'layer'), pairs)  4.65 us
    ppermute x3, starting transfers between devices, on_device(): lax.ppermute(mine, 'row', [(i, i ^ step) for i in range(num_row)])  4.45 us
    ppermute x1, starting transfers between devices, on_device(): below = lax.ppermute(low, 'row', [(i, i ^ 3) for i in range(4)])  3.67 us
    pallas_call x1, Pallas kernels, rims(): pl.pallas_call(functools.partial(rims_kernel, num_col, num_layer, len(arr...  2.39 us
    pallas_call x1, Pallas kernels, prepare(): pl.pallas_call(functools.partial(prepare_kernel, paired), out_shape=outs,...  2.28 us
    ppermute x1, waiting for transfers between devices, on_device(): above = lax.ppermute(high, 'row', [(i, i ^ 1) for i in range(4)])  1.8 us
    pallas_call x1, Pallas kernels, multiply(): pl.pallas_call(functools.partial(product_kernel, num_row, num_col, num_la...  0.98 us
  transfers between devices with their start and end apart: 12, of which 5 were waited for; matrix products, arithmetic and copies ran while one was open for 0% of the time, Pallas kernels for 15%

profile of v6, /device:TPU:0, one launch (start us, length us, event | category | flops | bytes accessed | tf_op | source)
XLA Modules:
  0.0 28.4 jit_solution(18207128308468082852)
XLA Ops:
  0.6 2.3 %prepare.1 = (bf16[208,256]{1,0:T(8,128)(2,1)}, bf16[272,256]{1,0:T(8,128)(2,1)}, bf16[272,256]{1,0:T(8,128)(2,1)}) custom-call(bf16[256,128]{1,0:T(8,128)(2,1)} %bitcast.13, s32[4,8]{1,0:T(4,128)} %bitcast.20, bf16[64,512]{1,0:T(8,128)(2,1)} %bitcast.14, s32[2,16]{1,0:T(2,128)} %bitcast.21, s32[8,128]{1,0:T(8,128)} %bitcast.15, s32[8,128]{1,0:T(8,128)} %bitcast.16, ...), custom_call_target="tpu_custom_call" | custom-call | tf_op jit(solution)/shard_map/prepare/pallas_call | solution.py:150
  2.9 3.0 %collective-permute-start.1 = (bf16[272,256]{1,0:T(8,128)(2,1)}, bf16[272,256]{1,0:T(8,128)(2,1)S(1)}, u32[]{:S(2)}, u32[]{:S(2)}) collective-permute-start(bf16[272,256]{1,0:T(8,128)(2,1)} %get-tuple-element.12), channel_id=1, source_target_pairs={{0,2},{1,3},{2,0},{3,1},{4,6},{5,7},{6,4},{7,5},{8,10},{9,11},{10,... | collective-permute-start | bytes 417800 | tf_op jit(solution)/shard_map/ppermute | solution.py:508
  5.9 1.5 %collective-permute-start.3 = (bf16[208,256]{1,0:T(8,128)(2,1)}, bf16[208,256]{1,0:T(8,128)(2,1)S(1)}, u32[]{:S(2)}, u32[]{:S(2)}) collective-permute-start(bf16[208,256]{1,0:T(8,128)(2,1)} %get-tuple-element.13), channel_id=1, source_target_pairs={{0,4},{1,5},{2,6},{3,7},{4,0},{5,1},{6,2},{7,3},{8,12},{9,13},{10,... | collective-permute-start | bytes 319496 | tf_op jit(solution)/shard_map/ppermute | solution.py:508
  7.4 0.0 collective-permute-start.5
  7.5 0.9 %copy-done = bf16[272,256]{1,0:T(8,128)(2,1)S(1)} copy-done((bf16[272,256]{1,0:T(8,128)(2,1)S(1)}, bf16[272,256]{1,0:T(8,128)(2,1)}, u32[]{:S(2)}) %copy-start) | copy-done | bytes 139288
  8.4 0.1 collective-permute-start
  8.5 1.5 %collective-permute-done.1.far_ref.refs_2_ = bf16[272,256]{1,0:T(8,128)(2,1)S(1)} collective-permute-done((bf16[272,256]{1,0:T(8,128)(2,1)}, bf16[272,256]{1,0:T(8,128)(2,1)S(1)}, u32[]{:S(2)}, u32[]{:S(2)}) %collective-permute-start.1) | collective-permute-done | bytes 139296 | tf_op jit(solution)/shard_map/ppermute | solution.py:508
  10.0 0.0 collective-permute-start.2
  10.0 1.8 %collective-permute-done.3.refs_4_ = bf16[208,256]{1,0:T(8,128)(2,1)S(1)} collective-permute-done((bf16[208,256]{1,0:T(8,128)(2,1)}, bf16[208,256]{1,0:T(8,128)(2,1)S(1)}, u32[]{:S(2)}, u32[]{:S(2)}) %collective-permute-start.3) | collective-permute-done | bytes 106528 | tf_op jit(solution)/shard_map/ppermute | solution.py:508
  11.7 0.0 collective-permute-start.4
  11.7 1.5 %collective-permute-done.5.refs_6_ = bf16[208,256]{1,0:T(8,128)(2,1)S(1)} collective-permute-done((bf16[208,256]{1,0:T(8,128)(2,1)}, bf16[208,256]{1,0:T(8,128)(2,1)S(1)}, u32[]{:S(2)}, u32[]{:S(2)}) %collective-permute-start.5) | collective-permute-done | bytes 106528 | tf_op jit(solution)/shard_map/ppermute | solution.py:508
  13.3 0.0 collective-permute-start.6
  13.3 0.0 collective-permute-done.2.both_ref.refs_3_
  13.3 1.6 %collective-permute-start.7 = (bf16[4,64,128]{2,1,0:T(8,128)(2,1)S(1)}, bf16[4,64,128]{2,1,0:T(8,128)(2,1)S(1)}, u32[]{:S(2)}, u32[]{:S(2)}) collective-permute-start(bf16[4,64,128]{2,1,0:T(8,128)(2,1)S(1)} %stack.1.refs_8_), channel_id=1, source_target_pairs={{0,8},{8,0},{16,24},{24,16},{1,9},{9,1},{17,25},{25,17},{2,10},{10... | collective-permute-start | bytes 196616 | tf_op jit(solution)/shard_map/ppermute | solution.py:537
  14.9 2.6 %collective-permute-start.8 = (bf16[4,64,128]{2,1,0:T(8,128)(2,1)S(1)}, bf16[4,64,128]{2,1,0:T(8,128)(2,1)S(1)}, u32[]{:S(2)}, u32[]{:S(2)}) collective-permute-start(bf16[4,64,128]{2,1,0:T(8,128)(2,1)S(1)} %stack.1.refs_8_), channel_id=1, source_target_pairs={{0,16},{8,24},{16,0},{24,8},{1,17},{9,25},{17,1},{25,9},{2,18},{10... | collective-permute-start | bytes 196616 | tf_op jit(solution)/shard_map/ppermute | solution.py:537
  17.5 0.2 collective-permute-start.9
  17.7 2.4 %rims.1 = (f32[64,128]{1,0:T(8,128)S(1)}, f32[64,128]{1,0:T(8,128)S(1)}, bf16[256,2560]{1,0:T(8,128)(2,1)S(1)}, f32[256,128]{1,0:T(8,128)S(1)}) custom-call(bf16[272,256]{1,0:T(8,128)(2,1)S(1)} %settle.1.own_ref.refs_0_, bf16[272,256]{1,0:T(8,128)(2,1)S(1)} %collective-permute-done.near_ref.refs_1_, ...), custom_call_target="tpu_custom_call" | custom-call | flops 3000000000 | bytes 1000000 | tf_op jit(solution)/shard_map/rims/pallas_call | solution.py:355
  20.1 3.7 %collective-permute-start.10 = (f32[64,128]{1,0:T(8,128)S(1)}, f32[64,128]{1,0:T(8,128)S(1)}, u32[]{:S(2)}, u32[]{:S(2)}) collective-permute-start(f32[64,128]{1,0:T(8,128)S(1)} %get-tuple-element.17), channel_id=1, source_target_pairs={{0,24},{8,16},{16,8},{24,0},{1,25},{9,17},{17,9},{25,1},{2,26},{10... | collective-permute-start | bytes 98312 | tf_op jit(solution)/shard_map/ppermute | solution.py:540
  23.8 0.9 %core.1.core_ref = f32[256,128]{1,0:T(8,128)S(1)} custom-call(bf16[272,256]{1,0:T(8,128)(2,1)S(1)} %settle.1.own_ref.refs_0_, bf16[272,256]{1,0:T(8,128)(2,1)S(1)} %collective-permute-done.near_ref.refs_1_, bf16[272,256]{1,0:T(8,128)(2,1)S(1)} %collective-permute-done.1.far_ref.refs_2_, bf16[272,256]{1,0:T(8,128)(2,1)S(1)} %collective-permute-done.2.both_ref.refs_3_, ...), custom_call_target="tpu_custom_call" | custom-call | flops 1500000000 | bytes 1000000 | tf_op jit(solution)/shard_map/core/pallas_call | solution.py:394
  24.8 0.0 collective-permute-done.9.refs_11_
  24.8 1.0 %multiply.1 = (bf16[256,128]{1,0:T(8,128)(2,1)}, f32[8,128]{1,0:T(8,128)S(1)}) custom-call(bf16[272,256]{1,0:T(8,128)(2,1)S(1)} %settle.1.own_ref.refs_0_, bf16[272,256]{1,0:T(8,128)(2,1)S(1)} %collective-permute-done.near_ref.refs_1_, bf16[272,256]{1,0:T(8,128)(2,1)S(1)} %collective-permute-done.1.far_ref.refs_2_, ...), custom_call_target="tpu_custom_call" | custom-call | flops 500000000 | bytes 1000000 | tf_op jit(solution)/shard_map/multiply/pallas_call | solution.py:433
  25.8 0.2 collective-permute-done.10.below_ref
  25.9 1.8 %collective-permute-done.11.above_ref = f32[64,128]{1,0:T(8,128)S(1)} collective-permute-done((f32[64,128]{1,0:T(8,128)S(1)}, f32[64,128]{1,0:T(8,128)S(1)}, u32[]{:S(2)}, u32[]{:S(2)}) %collective-permute-start.11) | collective-permute-done | bytes 32800 | tf_op jit(solution)/shard_map/ppermute | solution.py:541
  27.7 0.7 %fold.1 = f32[256,128]{1,0:T(8,128)} custom-call(f32[256,128]{1,0:T(8,128)S(1)} %core.1.core_ref, f32[64,128]{1,0:T(8,128)S(1)} %collective-permute-done.10.below_ref, f32[64,128]{1,0:T(8,128)S(1)} %collective-permute-done.11.above_ref, f32[8,128]{1,0:T(8,128)S(1)} %get-tuple-element.19.after_ref), custom_call_target="tpu_custom_call" | custom-call | flops 1000000 | bytes 400000 | tf_op jit(solution)/shard_map/fold/pallas_call | solution.py:491
  (9 shorter events, 0.0 us)
Async XLA Ops:
  2.9 7.0 %collective-permute-start.1 = (bf16[272,256]{1,0:T(8,128)(2,1)}, bf16[272,256]{1,0:T(8,128)(2,1)S(1)}, u32[]{:S(2)}, u32[]{:S(2)}) collective-permute-start(bf16[272,256]{1,0:T(8,128)(2,1)} %get-tuple-element.12), channel_id=1, source_target_pairs={{0,2},{1,3},{2,0},{3,1},{4,6},{5,7},{6,4},{7,5},{8,10},{9,11},{10,... | collective-permute-start | bytes 417800 | tf_op jit(solution)/shard_map/ppermute | solution.py:508
  5.9 5.8 %collective-permute-start.3 = (bf16[208,256]{1,0:T(8,128)(2,1)}, bf16[208,256]{1,0:T(8,128)(2,1)S(1)}, u32[]{:S(2)}, u32[]{:S(2)}) collective-permute-start(bf16[208,256]{1,0:T(8,128)(2,1)} %get-tuple-element.13), channel_id=1, source_target_pairs={{0,4},{1,5},{2,6},{3,7},{4,0},{5,1},{6,2},{7,3},{8,12},{9,13},{10,... | collective-permute-start | bytes 319496 | tf_op jit(solution)/shard_map/ppermute | solution.py:508
  7.4 5.8 %collective-permute-start.5 = (bf16[208,256]{1,0:T(8,128)(2,1)}, bf16[208,256]{1,0:T(8,128)(2,1)S(1)}, u32[]{:S(2)}, u32[]{:S(2)}) collective-permute-start(bf16[208,256]{1,0:T(8,128)(2,1)} %get-tuple-element.13), channel_id=1, source_target_pairs={{0,6},{1,7},{2,4},{3,5},{4,2},{5,3},{6,0},{7,1},{8,14},{9,15},{10,... | collective-permute-start | bytes 319496 | tf_op jit(solution)/shard_map/ppermute | solution.py:508
  7.5 0.9 %copy-start = (bf16[272,256]{1,0:T(8,128)(2,1)S(1)}, bf16[272,256]{1,0:T(8,128)(2,1)}, u32[]{:S(2)}) copy-start(bf16[272,256]{1,0:T(8,128)(2,1)} %get-tuple-element.11.block_ref) | copy-start | bytes 417796
  8.4 4.9 %collective-permute-start = (bf16[272,256]{1,0:T(8,128)(2,1)S(1)}, bf16[272,256]{1,0:T(8,128)(2,1)S(1)}, u32[]{:S(2)}, u32[]{:S(2)}) collective-permute-start(bf16[272,256]{1,0:T(8,128)(2,1)S(1)} %settle.1.own_ref.refs_0_), channel_id=1, source_target_pairs={{0,1},{1,0},{2,3},{3,2},{4,5},{5,4},{6,7},{7,6},{8,9},{9,8},{10,11... | collective-permute-start | bytes 417800 | tf_op jit(solution)/shard_map/ppermute | solution.py:508
  10.0 3.3 %collective-permute-start.2 = (bf16[272,256]{1,0:T(8,128)(2,1)S(1)}, bf16[272,256]{1,0:T(8,128)(2,1)S(1)}, u32[]{:S(2)}, u32[]{:S(2)}) collective-permute-start(bf16[272,256]{1,0:T(8,128)(2,1)S(1)} %collective-permute-done.1.far_ref.refs_2_), channel_id=1, source_target_pairs={{0,1},{1,0},{2,3},{3,2},{4,5},{5,4},{6,7},{7,6},{8,9},{9,8},{10,11... | collective-permute-start | bytes 417800 | tf_op jit(solution)/shard_map/ppermute | solution.py:508
  11.7 6.0 %collective-permute-start.4 = (bf16[208,256]{1,0:T(8,128)(2,1)S(1)}, bf16[208,256]{1,0:T(8,128)(2,1)S(1)}, u32[]{:S(2)}, u32[]{:S(2)}) collective-permute-start(bf16[208,256]{1,0:T(8,128)(2,1)S(1)} %collective-permute-done.3.refs_4_), channel_id=1, source_target_pairs={{0,1},{1,0},{2,3},{3,2},{4,5},{5,4},{6,7},{7,6},{8,9},{9,8},{10,11... | collective-permute-start | bytes 319496 | tf_op jit(solution)/shard_map/ppermute | solution.py:508
  13.3 4.5 %collective-permute-start.6 = (bf16[208,256]{1,0:T(8,128)(2,1)S(1)}, bf16[208,256]{1,0:T(8,128)(2,1)S(1)}, u32[]{:S(2)}, u32[]{:S(2)}) collective-permute-start(bf16[208,256]{1,0:T(8,128)(2,1)S(1)} %collective-permute-done.5.refs_6_), channel_id=1, source_target_pairs={{0,1},{1,0},{2,3},{3,2},{4,5},{5,4},{6,7},{7,6},{8,9},{9,8},{10,11... | collective-permute-start | bytes 319496 | tf_op jit(solution)/shard_map/ppermute | solution.py:508
  13.3 11.5 %collective-permute-start.7 = (bf16[4,64,128]{2,1,0:T(8,128)(2,1)S(1)}, bf16[4,64,128]{2,1,0:T(8,128)(2,1)S(1)}, u32[]{:S(2)}, u32[]{:S(2)}) collective-permute-start(bf16[4,64,128]{2,1,0:T(8,128)(2,1)S(1)} %stack.1.refs_8_), channel_id=1, source_target_pairs={{0,8},{8,0},{16,24},{24,16},{1,9},{9,1},{17,25},{25,17},{2,10},{10... | collective-permute-start | bytes 196616 | tf_op jit(solution)/shard_map/ppermute | solution.py:537
  14.9 9.8 %collective-permute-start.8 = (bf16[4,64,128]{2,1,0:T(8,128)(2,1)S(1)}, bf16[4,64,128]{2,1,0:T(8,128)(2,1)S(1)}, u32[]{:S(2)}, u32[]{:S(2)}) collective-permute-start(bf16[4,64,128]{2,1,0:T(8,128)(2,1)S(1)} %stack.1.refs_8_), channel_id=1, source_target_pairs={{0,16},{8,24},{16,0},{24,8},{1,17},{9,25},{17,1},{25,9},{2,18},{10... | collective-permute-start | bytes 196616 | tf_op jit(solution)/shard_map/ppermute | solution.py:537
  17.5 7.3 %collective-permute-start.9 = (bf16[4,64,128]{2,1,0:T(8,128)(2,1)S(1)}, bf16[4,64,128]{2,1,0:T(8,128)(2,1)S(1)}, u32[]{:S(2)}, u32[]{:S(2)}) collective-permute-start(bf16[4,64,128]{2,1,0:T(8,128)(2,1)S(1)} %stack.1.refs_8_), channel_id=1, source_target_pairs={{0,24},{8,16},{16,8},{24,0},{1,25},{9,17},{17,9},{25,1},{2,26},{10... | collective-permute-start | bytes 196616 | tf_op jit(solution)/shard_map/ppermute | solution.py:537
  20.1 5.8 %collective-permute-start.10 = (f32[64,128]{1,0:T(8,128)S(1)}, f32[64,128]{1,0:T(8,128)S(1)}, u32[]{:S(2)}, u32[]{:S(2)}) collective-permute-start(f32[64,128]{1,0:T(8,128)S(1)} %get-tuple-element.17), channel_id=1, source_target_pairs={{0,24},{8,16},{16,8},{24,0},{1,25},{9,17},{17,9},{25,1},{2,26},{10... | collective-permute-start | bytes 98312 | tf_op jit(solution)/shard_map/ppermute | solution.py:540
  23.8 3.9 %collective-permute-start.11 = (f32[64,128]{1,0:T(8,128)S(1)}, f32[64,128]{1,0:T(8,128)S(1)}, u32[]{:S(2)}, u32[]{:S(2)}) collective-permute-start(f32[64,128]{1,0:T(8,128)S(1)} %get-tuple-element.18), channel_id=1, source_target_pairs={{0,8},{8,0},{16,24},{24,16},{1,9},{9,1},{17,25},{25,17},{2,10},{10... | collective-permute-start | bytes 98312 | tf_op jit(solution)/shard_map/ppermute | solution.py:541

commit v7 on v5

--- a/solution.py
+++ b/solution.py
@@ -20,9 +20,10 @@
 FULL = CORE + 2 * HALO
 UNIT = 2 * LANES
 PAIRS = 4
-META = (PAIRS + 1) * 16
+META = (PAIRS // 2 + 1) * 16
 BASE = LANES + META
-FLAG = 12
+FLAG = 8
+FIELDS = 8
 VMEM = pl.BlockSpec(memory_space=pltpu.VMEM)
 HBM = pl.BlockSpec(memory_space=pltpu.HBM)
 PARAMS = pltpu.CompilerParams(vmem_limit_bytes=40 * 1024 * 1024)
@@ -34,11 +35,25 @@
     return lax.broadcasted_iota(jnp.int32, shape, axis).astype(F32)
 
 
-def split3(value):
+def split2(value):
     first = value.astype(BF16).astype(F32)
-    rest = value - first
-    second = rest.astype(BF16).astype(F32)
-    return first, second, rest - second
+    return first, value - first
+
+
+class Gaussians:
+    def __init__(self, tile):
+        first, second, third, fourth = (tile[at : at + 1, :].astype(jnp.int32) for at in range(4))
+        first, second, third = first + 256, second + 256, third + 256
+        column = third + ((fourth >> 7) << 9) + ((second >> 8) << 10) + ((first >> 8) << 11)
+        cell = second & 255
+        self.row = (first & 255).astype(F32)
+        self.block = (column // LANES).astype(F32)
+        self.lane = (column % LANES).astype(F32)
+        self.x = (cell // GY).astype(F32)
+        self.y = (cell % GY).astype(F32)
+        self.z = (fourth & 127).astype(F32)
+        self.expo = tile[4:5, :] + tile[5:6, :]
+        self.pref = tile[6:7, :] + tile[7:8, :]
 
 
 def masked(values, bits):
@@ -93,20 +108,18 @@
     cell = cell_ref[...]
     cell_z = (cell % GZ).astype(F32)
     values = [
-        row_ref[...].astype(F32),
-        (col // LANES).astype(F32),
-        (col % LANES).astype(F32),
-        (cell // (GY * GZ)).astype(F32),
-        (cell // GZ % GY).astype(F32),
-        cell_z,
-        *split3(expo_ref[...]),
-        *split3(pref_ref[...]),
+        (row_ref[...] + ((col >> 11) & 1) * 256 - 256).astype(F32),
+        (cell // GZ + ((col >> 10) & 1) * 256 - 256).astype(F32),
+        ((col & 511) - 256).astype(F32),
+        (cell % GZ + ((col >> 9) & 1) * 128).astype(F32),
+        *split2(expo_ref[...]),
+        *split2(pref_ref[...]),
     ]
-    for index in range(16):
-        fields[8 * index : 8 * index + 8, :] = values[index] if index < len(values) else jnp.zeros((8, LANES), F32)
-    tiles = [fields[pl.ds(part, 16, stride=8), :].astype(BF16) for part in range(2 * PAIRS)]
+    for index in range(FIELDS):
+        fields[8 * index : 8 * index + 8, :] = values[index]
     for part in range(2 * PAIRS):
-        matrix[:, part * LANES : part * LANES + LANES] = tiles[part]
+        matrix[0:FIELDS, part * LANES : part * LANES + LANES] = fields[pl.ds(part, FIELDS, stride=8), :]
+    matrix[FIELDS : 2 * FIELDS, :] = jnp.zeros((FIELDS, 2 * PAIRS * LANES), F32)
     faces = jnp.concatenate([jnp.where(cell_z < R, 1.0, 0.0), jnp.where(cell_z >= GZ - R, 1.0, 0.0)], axis=0)
     place, many = ranks(faces)
     slot = iota((LANES, LANES), 0)
@@ -115,16 +128,17 @@
         for face in range(2):
             hit = slot == place[face * 8 + part : face * 8 + part + 1, :]
             onehot[face * LANES : face * LANES + LANES, lanes] = jnp.where(hit, 1.0, 0.0).astype(BF16)
-    listed = lax.dot_general(matrix[...], onehot[...], NT, preferred_element_type=F32)
+    listed = lax.dot_general(matrix[...].astype(BF16), onehot[...], NT, preferred_element_type=F32)
     over = jnp.where(jnp.max(many, axis=0, keepdims=True) > LANES, 1.0, 0.0)
     over = jnp.concatenate([over, over], axis=1)
     listed = jnp.where(iota(listed.shape, 0) == FLAG, over, listed).astype(BF16)
     copies = outs[:3] if paired else outs[:1]
     for out in copies:
         out[0:LANES, :] = turned
-        for pair in range(PAIRS):
-            out[LANES + 16 * pair : LANES + 16 * pair + 16, :] = matrix[:, pair * UNIT : pair * UNIT + UNIT]
-        out[LANES + 16 * PAIRS : BASE, :] = listed
+        for at in range(PAIRS // 2):
+            halves = [matrix[0:FIELDS, pair * UNIT : pair * UNIT + UNIT] for pair in (2 * at, 2 * at + 1)]
+            out[LANES + 16 * at : LANES + 16 * at + 16, :] = jnp.concatenate(halves, axis=0).astype(BF16)
+        out[LANES + 8 * PAIRS : BASE, :] = listed
 
     def piece(chunk):
         return h_piece(h_ref, hm_ref, chunk)
@@ -159,8 +173,8 @@
             pltpu.SMEM(h_mask.shape, h_mask.dtype),
             *[pltpu.VMEM(x.shape, x.dtype) for x in gauss],
             pltpu.VMEM(p.shape, F32),
-            pltpu.VMEM((16 * 8, LANES), F32),
-            pltpu.VMEM((16, 2 * PAIRS * LANES), BF16),
+            pltpu.VMEM((FIELDS * 8, LANES), F32),
+            pltpu.VMEM((2 * FIELDS, 2 * PAIRS * LANES), F32),
             pltpu.VMEM((UNIT, 2 * PAIRS * LANES), BF16),
             pltpu.SemaphoreType.DMA((9,)),
         ],
@@ -190,8 +204,8 @@
         index = layer * self.num_col + piece
         return self.refs[0][index, 0:LANES, :]
 
-    def tile(self, which, side, pair):
-        rows = pl.ds(LANES + 16 * pair, 16)
+    def tile(self, which, side, at):
+        rows = pl.ds(LANES + 16 * at, 16)
         if self.paired:
             return self.refs[which * 4 + side][rows, :].astype(F32)
         shift_l = 0 if side == 0 else (1 if side == 1 else -1)
@@ -214,13 +228,16 @@
     def listed(self, which):
         halves = []
         for side in self.sides():
-            both = self.tile(which, side, PAIRS)
+            both = self.tile(which, side, PAIRS // 2)[0:FIELDS, :]
             upward = self.side_shift(side) > 0
             halves.append(jnp.where(upward, both[:, 0:LANES], both[:, LANES:UNIT]))
         return jnp.concatenate(halves, axis=1)
 
     def unit(self, which, pair):
-        return self.tile(which, 0, pair) if pair < PAIRS else self.listed(which)
+        if pair == PAIRS:
+            return Gaussians(self.listed(which))
+        half = (pair % 2) * FIELDS
+        return Gaussians(self.tile(which, 0, pair // 2)[half : half + FIELDS, :])
 
     def lifts(self, pair):
         if pair < PAIRS:
@@ -231,7 +248,7 @@
 
     def over(self):
         flags = [
-            self.tile(which, side, PAIRS)[FLAG : FLAG + 1, :]
+            self.tile(which, side, PAIRS // 2)[FLAG : FLAG + 1, :]
             for which in range(len(self.col_shifts))
             for side in self.sides()
         ]
@@ -243,14 +260,14 @@
 
 def weigh(blocks, whole, tile):
     band = whole.shape[1]
-    onehot = jnp.where(iota((band, UNIT), 0) == tile[0:1, :], 1.0, 0.0).astype(BF16)
+    onehot = jnp.where(iota((band, UNIT), 0) == tile.row, 1.0, 0.0).astype(BF16)
     found = jnp.dot(whole[...], onehot, preferred_element_type=F32)
     picked = jnp.zeros((LANES, UNIT), F32)
     for index in range(blocks.total):
-        mine = tile[1:2, :] == jnp.asarray(blocks.ident(index)).astype(F32)
+        mine = tile.block == jnp.asarray(blocks.ident(index)).astype(F32)
         picked = jnp.where(mine, found[index * LANES : index * LANES + LANES, :], picked)
-    value = jnp.sum(jnp.where(iota((LANES, UNIT), 0) == tile[2:3, :], picked, 0.0), axis=0, keepdims=True)
-    return (tile[9:10, :] + tile[10:11, :] + tile[11:12, :]) * value
+    value = jnp.sum(jnp.where(iota((LANES, UNIT), 0) == tile.lane, picked, 0.0), axis=0, keepdims=True)
+    return tile.pref * value
 
 
 def bell(dist, expo):
@@ -263,23 +280,19 @@
 ALL_X = tuple(range(GX + 2 * R))
 
 
-def decay(tile):
-    return tile[6:7, :] + tile[7:8, :] + tile[8:9, :]
-
-
 def shapes_x(tile):
-    return bell(iota((GX + 2 * R, UNIT), 0) - float(R) - tile[3:4, :], decay(tile))
+    return bell(iota((GX + 2 * R, UNIT), 0) - float(R) - tile.x, tile.expo)
 
 
 def shapes_y(tile, shift, wraps):
-    dy = iota((GY, UNIT), 0) - tile[4:5, :] - float(shift * GY)
+    dy = iota((GY, UNIT), 0) - tile.y - float(shift * GY)
     if wraps:
         dy = jnp.where(dy < -float(GY), dy + 2.0 * GY, dy)
-    return bell(dy, decay(tile))
+    return bell(dy, tile.expo)
 
 
 def shapes_z(tile, lift):
-    return bell(iota((GZ, UNIT), 0) - tile[5:6, :] - lift, decay(tile))
+    return bell(iota((GZ, UNIT), 0) - tile.z - lift, tile.expo)
 
 
 def fill_planes(ex, ey, places, at, planeh, planel):
@@ -332,15 +345,17 @@
         acc[...] = jnp.zeros_like(acc)
         for which, side in blocks.long_steps():
 
-            def step(pair, carry):
-                tile = blocks.tile(which, side, pair)
+            def step(at, carry):
+                both = blocks.tile(which, side, at)
                 lift = blocks.side_shift(side) * float(GZ)
-                set_planes(blocks, tile, which, ALL_X, 0, longh, longl)
-                fill_depth(shapes_z(tile, lift), weigh(blocks, whole, tile), 0, long_depth)
-                acc[...] += summed(longh[...], longl[...], long_depth[...])
+                for half in range(2):
+                    tile = Gaussians(both[half * FIELDS : half * FIELDS + FIELDS, :])
+                    set_planes(blocks, tile, which, ALL_X, 0, longh, longl)
+                    fill_depth(shapes_z(tile, lift), weigh(blocks, whole, tile), 0, long_depth)
+                    acc[...] += summed(longh[...], longl[...], long_depth[...])
                 return carry
 
-            lax.fori_loop(0, PAIRS, step, 0)
+            lax.fori_loop(0, PAIRS // 2, step, 0)
         low_ref[...] += acc[0:HALO, :]
         extra[...] = acc[HALO : HALO + CORE, :]
         high_ref[...] += acc[HALO + CORE : FULL, :]

time: 26.9 us -> 26.8 us (level)
  no operation moved by 1% of the time
where the time goes in v7:
time: 26.8 us; the launch traced here: 26.6 us
  starting transfers between devices  13 us (49%)
  Pallas kernels  7.3 us (27%)
  waiting for transfers between devices  4.73 us (18%)
  local copies, waits for them, and re-layouts  0.9 us (3%)
  between operations  0.71 us (3%)
    ppermute x7, starting transfers between devices, crossed(): return lax.ppermute(value, ('col', 'layer'), pairs)  4.65 us
    ppermute x7, waiting for transfers between devices, crossed(): return lax.ppermute(value, ('col', 'layer'), pairs)  4.6 us
    ppermute x3, starting transfers between devices, on_device(): lax.ppermute(mine, 'row', [(i, i ^ step) for i in range(num_row)])  4.45 us
    ppermute x2, starting transfers between devices, shifted(): lax.ppermute(value, axis, [(i, (i + step) % count) for i in range(count)])  3.88 us
    pallas_call x1, Pallas kernels, rims(): pl.pallas_call(functools.partial(rims_kernel, num_col, num_layer, len(arr...  2.45 us
    pallas_call x1, Pallas kernels, prepare(): pl.pallas_call(functools.partial(prepare_kernel, paired), out_shape=outs,...  2.28 us
    pallas_call x1, Pallas kernels, multiply(): pl.pallas_call(functools.partial(product_kernel, num_row, num_col, num_la...  0.98 us
    unnamed x2, local copies, waits for them, and re-layouts  0.9 us
  transfers between devices with their start and end apart: 12, of which 4 were waited for; matrix products, arithmetic and copies ran while one was open for 0% of the time, Pallas kernels for 16%

profile of v7, /device:TPU:0, one launch (start us, length us, event | category | flops | bytes accessed | tf_op | source)
XLA Modules:
  0.0 26.6 jit_solution(7135693260190415939)
XLA Ops:
  0.6 2.3 %prepare.1 = (bf16[176,256]{1,0:T(8,128)(2,1)}, bf16[240,256]{1,0:T(8,128)(2,1)}, bf16[240,256]{1,0:T(8,128)(2,1)}) custom-call(bf16[256,128]{1,0:T(8,128)(2,1)} %bitcast.13, s32[4,8]{1,0:T(4,128)} %bitcast.20, bf16[64,512]{1,0:T(8,128)(2,1)} %bitcast.14, s32[2,16]{1,0:T(2,128)} %bitcast.21, s32[8,128]{1,0:T(8,128)} %bitcast.15, s32[8,128]{1,0:T(8,128)} %bitcast.16, ...), custom_call_target="tpu_custom_call" | custom-call | tf_op jit(solution)/shard_map/prepare/pallas_call | solution.py:164
  2.9 3.0 %collective-permute-start.1 = (bf16[240,256]{1,0:T(8,128)(2,1)}, bf16[240,256]{1,0:T(8,128)(2,1)S(1)}, u32[]{:S(2)}, u32[]{:S(2)}) collective-permute-start(bf16[240,256]{1,0:T(8,128)(2,1)} %get-tuple-element.12), channel_id=1, source_target_pairs={{0,2},{1,3},{2,0},{3,1},{4,6},{5,7},{6,4},{7,5},{8,10},{9,11},{10,... | collective-permute-start | bytes 368648 | tf_op jit(solution)/shard_map/ppermute | solution.py:517
  6.0 1.5 %collective-permute-start.3 = (bf16[176,256]{1,0:T(8,128)(2,1)}, bf16[176,256]{1,0:T(8,128)(2,1)S(1)}, u32[]{:S(2)}, u32[]{:S(2)}) collective-permute-start(bf16[176,256]{1,0:T(8,128)(2,1)} %get-tuple-element.13), channel_id=1, source_target_pairs={{0,4},{1,5},{2,6},{3,7},{4,0},{5,1},{6,2},{7,3},{8,12},{9,13},{10,... | collective-permute-start | bytes 270344 | tf_op jit(solution)/shard_map/ppermute | solution.py:517
  7.4 0.0 collective-permute-start.5
  7.5 0.9 %copy-done = bf16[240,256]{1,0:T(8,128)(2,1)S(1)} copy-done((bf16[240,256]{1,0:T(8,128)(2,1)S(1)}, bf16[240,256]{1,0:T(8,128)(2,1)}, u32[]{:S(2)}) %copy-start) | copy-done | bytes 122904
  8.4 0.1 collective-permute-start
  8.5 1.0 %collective-permute-done.1.far_ref.refs_2_ = bf16[240,256]{1,0:T(8,128)(2,1)S(1)} collective-permute-done((bf16[240,256]{1,0:T(8,128)(2,1)}, bf16[240,256]{1,0:T(8,128)(2,1)S(1)}, u32[]{:S(2)}, u32[]{:S(2)}) %collective-permute-start.1) | collective-permute-done | bytes 122912 | tf_op jit(solution)/shard_map/ppermute | solution.py:517
  9.5 0.0 collective-permute-start.2
  9.5 1.9 %collective-permute-done.3.refs_4_ = bf16[176,256]{1,0:T(8,128)(2,1)S(1)} collective-permute-done((bf16[176,256]{1,0:T(8,128)(2,1)}, bf16[176,256]{1,0:T(8,128)(2,1)S(1)}, u32[]{:S(2)}, u32[]{:S(2)}) %collective-permute-start.3) | collective-permute-done | bytes 90144 | tf_op jit(solution)/shard_map/ppermute | solution.py:517
  11.4 0.0 collective-permute-start.4
  11.4 1.7 %collective-permute-done.5.refs_6_ = bf16[176,256]{1,0:T(8,128)(2,1)S(1)} collective-permute-done((bf16[176,256]{1,0:T(8,128)(2,1)}, bf16[176,256]{1,0:T(8,128)(2,1)S(1)}, u32[]{:S(2)}, u32[]{:S(2)}) %collective-permute-start.5) | collective-permute-done | bytes 90144 | tf_op jit(solution)/shard_map/ppermute | solution.py:517
  13.1 0.0 collective-permute-start.6
  13.1 0.0 collective-permute-done.near_ref.refs_1_
  13.1 0.0 collective-permute-done.2.both_ref.refs_3_
  13.1 1.6 %collective-permute-start.7 = (bf16[4,64,128]{2,1,0:T(8,128)(2,1)S(1)}, bf16[4,64,128]{2,1,0:T(8,128)(2,1)S(1)}, u32[]{:S(2)}, u32[]{:S(2)}) collective-permute-start(bf16[4,64,128]{2,1,0:T(8,128)(2,1)S(1)} %stack.1.refs_8_), channel_id=1, source_target_pairs={{0,8},{8,0},{16,24},{24,16},{1,9},{9,1},{17,25},{25,17},{2,10},{10... | collective-permute-start | bytes 196616 | tf_op jit(solution)/shard_map/ppermute | solution.py:546
  14.8 2.6 %collective-permute-start.8 = (bf16[4,64,128]{2,1,0:T(8,128)(2,1)S(1)}, bf16[4,64,128]{2,1,0:T(8,128)(2,1)S(1)}, u32[]{:S(2)}, u32[]{:S(2)}) collective-permute-start(bf16[4,64,128]{2,1,0:T(8,128)(2,1)S(1)} %stack.1.refs_8_), channel_id=1, source_target_pairs={{0,16},{8,24},{16,0},{24,8},{1,17},{9,25},{17,1},{25,9},{2,18},{10... | collective-permute-start | bytes 196616 | tf_op jit(solution)/shard_map/ppermute | solution.py:546
  17.4 0.2 collective-permute-start.9
  17.6 2.5 %rims.1 = (f32[64,128]{1,0:T(8,128)S(1)}, f32[64,128]{1,0:T(8,128)S(1)}, bf16[256,2560]{1,0:T(8,128)(2,1)S(1)}, f32[256,128]{1,0:T(8,128)S(1)}) custom-call(bf16[240,256]{1,0:T(8,128)(2,1)S(1)} %settle.1.own_ref.refs_0_, bf16[240,256]{1,0:T(8,128)(2,1)S(1)} %collective-permute-done.near_ref.refs_1_, ...), custom_call_target="tpu_custom_call" | custom-call | flops 3000000000 | bytes 1000000 | tf_op jit(solution)/shard_map/rims/pallas_call | solution.py:366
  20.0 0.7 %collective-permute-start.10 = (f32[64,128]{1,0:T(8,128)S(1)}, f32[64,128]{1,0:T(8,128)S(1)}, u32[]{:S(2)}, u32[]{:S(2)}) collective-permute-start(f32[64,128]{1,0:T(8,128)S(1)} %get-tuple-element.17), channel_id=1, source_target_pairs={{0,8},{8,16},{16,24},{24,0},{1,9},{9,17},{17,25},{25,1},{2,10},{10... | collective-permute-start | bytes 98312 | tf_op jit(solution)/shard_map/ppermute | solution.py:512
  20.8 3.1 %collective-permute-start.11 = (f32[64,128]{1,0:T(8,128)S(1)}, f32[64,128]{1,0:T(8,128)S(1)}, u32[]{:S(2)}, u32[]{:S(2)}) collective-permute-start(f32[64,128]{1,0:T(8,128)S(1)} %get-tuple-element.18), channel_id=1, source_target_pairs={{0,24},{8,0},{16,8},{24,16},{1,25},{9,1},{17,9},{25,17},{2,26},{10... | collective-permute-start | bytes 98312 | tf_op jit(solution)/shard_map/ppermute | solution.py:512
  23.9 0.9 %core.1.core_ref = f32[256,128]{1,0:T(8,128)S(1)} custom-call(bf16[240,256]{1,0:T(8,128)(2,1)S(1)} %settle.1.own_ref.refs_0_, bf16[240,256]{1,0:T(8,128)(2,1)S(1)} %collective-permute-done.near_ref.refs_1_, bf16[240,256]{1,0:T(8,128)(2,1)S(1)} %collective-permute-done.1.far_ref.refs_2_, bf16[240,256]{1,0:T(8,128)(2,1)S(1)} %collective-permute-done.2.both_ref.refs_3_, ...), custom_call_target="tpu_custom_call" | custom-call | flops 1500000000 | bytes 1000000 | tf_op jit(solution)/shard_map/core/pallas_call | solution.py:405
  24.8 1.0 %multiply.1 = (bf16[256,128]{1,0:T(8,128)(2,1)}, f32[8,128]{1,0:T(8,128)S(1)}) custom-call(bf16[240,256]{1,0:T(8,128)(2,1)S(1)} %settle.1.own_ref.refs_0_, bf16[240,256]{1,0:T(8,128)(2,1)S(1)} %collective-permute-done.near_ref.refs_1_, bf16[240,256]{1,0:T(8,128)(2,1)S(1)} %collective-permute-done.1.far_ref.refs_2_, ...), custom_call_target="tpu_custom_call" | custom-call | flops 500000000 | bytes 1000000 | tf_op jit(solution)/shard_map/multiply/pallas_call | solution.py:444
  25.8 0.1 collective-permute-done.10.below_ref
  25.9 0.7 %fold.1 = f32[256,128]{1,0:T(8,128)} custom-call(f32[256,128]{1,0:T(8,128)S(1)} %core.1.core_ref, f32[64,128]{1,0:T(8,128)S(1)} %collective-permute-done.10.below_ref, f32[64,128]{1,0:T(8,128)S(1)} %collective-permute-done.11.above_ref, f32[8,128]{1,0:T(8,128)S(1)} %get-tuple-element.19.after_ref), custom_call_target="tpu_custom_call" | custom-call | flops 1000000 | bytes 400000 | tf_op jit(solution)/shard_map/fold/pallas_call | solution.py:500
  (9 shorter events, 0.0 us)
Async XLA Ops:
  2.9 6.6 %collective-permute-start.1 = (bf16[240,256]{1,0:T(8,128)(2,1)}, bf16[240,256]{1,0:T(8,128)(2,1)S(1)}, u32[]{:S(2)}, u32[]{:S(2)}) collective-permute-start(bf16[240,256]{1,0:T(8,128)(2,1)} %get-tuple-element.12), channel_id=1, source_target_pairs={{0,2},{1,3},{2,0},{3,1},{4,6},{5,7},{6,4},{7,5},{8,10},{9,11},{10,... | collective-permute-start | bytes 368648 | tf_op jit(solution)/shard_map/ppermute | solution.py:517
  6.0 5.4 %collective-permute-start.3 = (bf16[176,256]{1,0:T(8,128)(2,1)}, bf16[176,256]{1,0:T(8,128)(2,1)S(1)}, u32[]{:S(2)}, u32[]{:S(2)}) collective-permute-start(bf16[176,256]{1,0:T(8,128)(2,1)} %get-tuple-element.13), channel_id=1, source_target_pairs={{0,4},{1,5},{2,6},{3,7},{4,0},{5,1},{6,2},{7,3},{8,12},{9,13},{10,... | collective-permute-start | bytes 270344 | tf_op jit(solution)/shard_map/ppermute | solution.py:517
  7.4 5.6 %collective-permute-start.5 = (bf16[176,256]{1,0:T(8,128)(2,1)}, bf16[176,256]{1,0:T(8,128)(2,1)S(1)}, u32[]{:S(2)}, u32[]{:S(2)}) collective-permute-start(bf16[176,256]{1,0:T(8,128)(2,1)} %get-tuple-element.13), channel_id=1, source_target_pairs={{0,6},{1,7},{2,4},{3,5},{4,2},{5,3},{6,0},{7,1},{8,14},{9,15},{10,... | collective-permute-start | bytes 270344 | tf_op jit(solution)/shard_map/ppermute | solution.py:517
  7.5 0.9 %copy-start = (bf16[240,256]{1,0:T(8,128)(2,1)S(1)}, bf16[240,256]{1,0:T(8,128)(2,1)}, u32[]{:S(2)}) copy-start(bf16[240,256]{1,0:T(8,128)(2,1)} %get-tuple-element.11.block_ref) | copy-start | bytes 368644
  8.4 4.7 %collective-permute-start = (bf16[240,256]{1,0:T(8,128)(2,1)S(1)}, bf16[240,256]{1,0:T(8,128)(2,1)S(1)}, u32[]{:S(2)}, u32[]{:S(2)}) collective-permute-start(bf16[240,256]{1,0:T(8,128)(2,1)S(1)} %settle.1.own_ref.refs_0_), channel_id=1, source_target_pairs={{0,1},{1,0},{2,3},{3,2},{4,5},{5,4},{6,7},{7,6},{8,9},{9,8},{10,11... | collective-permute-start | bytes 368648 | tf_op jit(solution)/shard_map/ppermute | solution.py:517
  9.5 3.6 %collective-permute-start.2 = (bf16[240,256]{1,0:T(8,128)(2,1)S(1)}, bf16[240,256]{1,0:T(8,128)(2,1)S(1)}, u32[]{:S(2)}, u32[]{:S(2)}) collective-permute-start(bf16[240,256]{1,0:T(8,128)(2,1)S(1)} %collective-permute-done.1.far_ref.refs_2_), channel_id=1, source_target_pairs={{0,1},{1,0},{2,3},{3,2},{4,5},{5,4},{6,7},{7,6},{8,9},{9,8},{10,11... | collective-permute-start | bytes 368648 | tf_op jit(solution)/shard_map/ppermute | solution.py:517
  11.4 6.2 %collective-permute-start.4 = (bf16[176,256]{1,0:T(8,128)(2,1)S(1)}, bf16[176,256]{1,0:T(8,128)(2,1)S(1)}, u32[]{:S(2)}, u32[]{:S(2)}) collective-permute-start(bf16[176,256]{1,0:T(8,128)(2,1)S(1)} %collective-permute-done.3.refs_4_), channel_id=1, source_target_pairs={{0,1},{1,0},{2,3},{3,2},{4,5},{5,4},{6,7},{7,6},{8,9},{9,8},{10,11... | collective-permute-start | bytes 270344 | tf_op jit(solution)/shard_map/ppermute | solution.py:517
  13.1 4.5 %collective-permute-start.6 = (bf16[176,256]{1,0:T(8,128)(2,1)S(1)}, bf16[176,256]{1,0:T(8,128)(2,1)S(1)}, u32[]{:S(2)}, u32[]{:S(2)}) collective-permute-start(bf16[176,256]{1,0:T(8,128)(2,1)S(1)} %collective-permute-done.5.refs_6_), channel_id=1, source_target_pairs={{0,1},{1,0},{2,3},{3,2},{4,5},{5,4},{6,7},{7,6},{8,9},{9,8},{10,11... | collective-permute-start | bytes 270344 | tf_op jit(solution)/shard_map/ppermute | solution.py:517
  13.1 11.7 %collective-permute-start.7 = (bf16[4,64,128]{2,1,0:T(8,128)(2,1)S(1)}, bf16[4,64,128]{2,1,0:T(8,128)(2,1)S(1)}, u32[]{:S(2)}, u32[]{:S(2)}) collective-permute-start(bf16[4,64,128]{2,1,0:T(8,128)(2,1)S(1)} %stack.1.refs_8_), channel_id=1, source_target_pairs={{0,8},{8,0},{16,24},{24,16},{1,9},{9,1},{17,25},{25,17},{2,10},{10... | collective-permute-start | bytes 196616 | tf_op jit(solution)/shard_map/ppermute | solution.py:546
  14.8 10.1 %collective-permute-start.8 = (bf16[4,64,128]{2,1,0:T(8,128)(2,1)S(1)}, bf16[4,64,128]{2,1,0:T(8,128)(2,1)S(1)}, u32[]{:S(2)}, u32[]{:S(2)}) collective-permute-start(bf16[4,64,128]{2,1,0:T(8,128)(2,1)S(1)} %stack.1.refs_8_), channel_id=1, source_target_pairs={{0,16},{8,24},{16,0},{24,8},{1,17},{9,25},{17,1},{25,9},{2,18},{10... | collective-permute-start | bytes 196616 | tf_op jit(solution)/shard_map/ppermute | solution.py:546
  17.4 7.5 %collective-permute-start.9 = (bf16[4,64,128]{2,1,0:T(8,128)(2,1)S(1)}, bf16[4,64,128]{2,1,0:T(8,128)(2,1)S(1)}, u32[]{:S(2)}, u32[]{:S(2)}) collective-permute-start(bf16[4,64,128]{2,1,0:T(8,128)(2,1)S(1)} %stack.1.refs_8_), channel_id=1, source_target_pairs={{0,24},{8,16},{16,8},{24,0},{1,25},{9,17},{17,9},{25,1},{2,26},{10... | collective-permute-start | bytes 196616 | tf_op jit(solution)/shard_map/ppermute | solution.py:546
  20.0 5.9 %collective-permute-start.10 = (f32[64,128]{1,0:T(8,128)S(1)}, f32[64,128]{1,0:T(8,128)S(1)}, u32[]{:S(2)}, u32[]{:S(2)}) collective-permute-start(f32[64,128]{1,0:T(8,128)S(1)} %get-tuple-element.17), channel_id=1, source_target_pairs={{0,8},{8,16},{16,24},{24,0},{1,9},{9,17},{17,25},{25,1},{2,10},{10... | collective-permute-start | bytes 98312 | tf_op jit(solution)/shard_map/ppermute | solution.py:512
  20.8 5.2 %collective-permute-start.11 = (f32[64,128]{1,0:T(8,128)S(1)}, f32[64,128]{1,0:T(8,128)S(1)}, u32[]{:S(2)}, u32[]{:S(2)}) collective-permute-start(f32[64,128]{1,0:T(8,128)S(1)} %get-tuple-element.18), channel_id=1, source_target_pairs={{0,24},{8,0},{16,8},{24,16},{1,25},{9,1},{17,9},{25,17},{2,26},{10... | collective-permute-start | bytes 98312 | tf_op jit(solution)/shard_map/ppermute | solution.py:512

commit v8 on v7

--- a/solution.py
+++ b/solution.py
@@ -337,8 +337,13 @@
         set_planes(blocks, tile, which, RIM_X, at, planeh, planel)
         fill_depth(shapes_z(tile, blocks.lifts(pair)), coef, at, depth)
     total = summed(planeh[...], planel[...], depth[...])
-    low_ref[...] = total[0:HALO, :]
-    high_ref[...] = total[HALO:, :]
+    swap = lax.rem(lax.axis_index("row"), 2) * int(lax.axis_size("row") == 4)
+
+    def put(low, high, base_low, base_high):
+        low_ref[...] = jnp.where(swap > 0, high, low) + base_low
+        high_ref[...] = jnp.where(swap > 0, low, high) + base_high
+
+    put(total[0:HALO, :], total[HALO:, :], 0.0, 0.0)
 
     @pl.when(jnp.max(over) > 0)
     def _():
@@ -356,9 +361,8 @@
                 return carry
 
             lax.fori_loop(0, PAIRS // 2, step, 0)
-        low_ref[...] += acc[0:HALO, :]
+        put(acc[0:HALO, :], acc[HALO + CORE : FULL, :], low_ref[...], high_ref[...])
         extra[...] = acc[HALO : HALO + CORE, :]
-        high_ref[...] += acc[HALO + CORE : FULL, :]
 
 
 def rims(arrays, num_col, num_layer):
@@ -414,6 +418,10 @@
     )(*arrays, depth, extra)
 
 
+def row_steps(num_row):
+    return [0, 1, num_row - 1] + list(range(2, num_row - 1))
+
+
 def product_kernel(num_row, num_col, num_layer, refs_in, *refs):
     blocks = Blocks(refs[:refs_in], num_col, num_layer)
     h_refs = refs[refs_in : refs_in + num_row]
@@ -422,9 +430,9 @@
     row = lax.axis_index("row")
     rows = h_refs[0].shape[1]
     for back in range(num_layer):
-        for step in range(num_row):
-            start = pl.multiple_of((row ^ step) * rows, rows)
-            slab[back, pl.ds(start, rows), :] = h_refs[step][back]
+        for spot, step in enumerate(row_steps(num_row)):
+            start = pl.multiple_of(lax.rem(row - step + num_row, num_row) * rows, rows)
+            slab[back, pl.ds(start, rows), :] = h_refs[spot][back]
     total = jnp.zeros(out_ref.shape, F32)
     for back in range(num_layer):
         for piece in range(num_col):
@@ -491,9 +499,11 @@
 
 
 def fold_kernel(core_ref, below_ref, above_ref, after_ref, out_ref):
-    out_ref[0:HALO, :] = core_ref[0:HALO, :] + below_ref[...]
+    swap = lax.rem(lax.axis_index("row"), 2) * int(lax.axis_size("row") == 4)
+    below, above = below_ref[...], above_ref[...]
+    out_ref[0:HALO, :] = core_ref[0:HALO, :] + jnp.where(swap > 0, above, below)
     out_ref[HALO : CORE - HALO, :] = core_ref[HALO : CORE - HALO, :]
-    out_ref[CORE - HALO : CORE, :] = core_ref[CORE - HALO : CORE, :] + above_ref[...]
+    out_ref[CORE - HALO : CORE, :] = core_ref[CORE - HALO : CORE, :] + jnp.where(swap > 0, below, above)
 
 
 def fold(core, below, above, after):
@@ -542,11 +552,13 @@
         mine = [pieces[0]] + [shifted(pieces[step], "layer", num_layer, step) for step in range(1, num_layer)]
         mine = jnp.stack(mine)
     low, high, depth, extra = rims(arrays, num_col, num_layer)
-    parts = [mine] + [
-        lax.ppermute(mine, "row", [(i, i ^ step) for i in range(num_row)]) for step in range(1, num_row)
-    ]
-    below = shifted(high, "row", num_row, 1)
-    above = shifted(low, "row", num_row, num_row - 1)
+    parts = [mine] + [shifted(mine, "row", num_row, step) for step in row_steps(num_row)[1:]]
+    if num_row == 4:
+        below = lax.ppermute(low, "row", [(i, i ^ 3) for i in range(4)])
+        above = lax.ppermute(high, "row", [(i, i ^ 1) for i in range(4)])
+    else:
+        below = shifted(high, "row", num_row, 1)
+        above = shifted(low, "row", num_row, num_row - 1)
     core = core_part(arrays, depth, extra, num_col, num_layer)
     product, token = multiply(arrays, parts, num_row, num_col, num_layer)
     density = fold(core, below, above, token).reshape(GX, GY, GZ)

time: 26.8 us -> 26.9 us (level)
  waiting for transfers between devices: 4.73 us -> 5.71 us
  starting transfers between devices: 13 us -> 12.1 us
    ppermute x3 -> x2, starting transfers between devices: 4.45 us -> 2.77 us  [the longest x1 1.41 us: on_device(): below = lax.ppermute(low, 'row', [(i, i ^ 3) for i in range(4)])]
    ppermute x3 -> x2, waiting for transfers between devices: 0.01 us -> 1.1 us  [the longest x1 1.1 us: on_device(): below = lax.ppermute(low, 'row', [(i, i ^ 3) for i in range(4)])]
    ppermute x2 -> x3, starting transfers between devices: 3.88 us -> 4.67 us  [shifted(): lax.ppermute(value, axis, [(i, (i + step) % count) for i in range(count)])]
where the time goes in v8:
time: 26.9 us; the launch traced here: 26.7 us
  starting transfers between devices  12.1 us (45%)
  Pallas kernels  7.3 us (27%)
  waiting for transfers between devices  5.71 us (21%)
  local copies, waits for them, and re-layouts  0.9 us (3%)
  between operations  0.71 us (3%)
    ppermute x3, starting transfers between devices, shifted(): lax.ppermute(value, axis, [(i, (i + step) % count) for i in range(count)])  4.67 us
    ppermute x7, starting transfers between devices, crossed(): return lax.ppermute(value, ('col', 'layer'), pairs)  4.65 us
    ppermute x7, waiting for transfers between devices, crossed(): return lax.ppermute(value, ('col', 'layer'), pairs)  4.6 us
    pallas_call x1, Pallas kernels, rims(): pl.pallas_call(functools.partial(rims_kernel, num_col, num_layer, len(arr...  2.45 us
    pallas_call x1, Pallas kernels, prepare(): pl.pallas_call(functools.partial(prepare_kernel, paired), out_shape=outs,...  2.28 us
    ppermute x1, starting transfers between devices, on_device(): below = lax.ppermute(low, 'row', [(i, i ^ 3) for i in range(4)])  1.41 us
    ppermute x1, starting transfers between devices, on_device(): above = lax.ppermute(high, 'row', [(i, i ^ 1) for i in range(4)])  1.35 us
    ppermute x1, waiting for transfers between devices, on_device(): below = lax.ppermute(low, 'row', [(i, i ^ 3) for i in range(4)])  1.1 us
  transfers between devices with their start and end apart: 12, of which 4 were waited for; matrix products, arithmetic and copies ran while one was open for 0% of the time, Pallas kernels for 16%

profile of v8, /device:TPU:0, one launch (start us, length us, event | category | flops | bytes accessed | tf_op | source)
XLA Modules:
  0.0 26.7 jit_solution(15879288234408020237)
XLA Ops:
  0.6 2.3 %prepare.1 = (bf16[176,256]{1,0:T(8,128)(2,1)}, bf16[240,256]{1,0:T(8,128)(2,1)}, bf16[240,256]{1,0:T(8,128)(2,1)}) custom-call(bf16[256,128]{1,0:T(8,128)(2,1)} %bitcast.13, s32[4,8]{1,0:T(4,128)} %bitcast.20, bf16[64,512]{1,0:T(8,128)(2,1)} %bitcast.14, s32[2,16]{1,0:T(2,128)} %bitcast.21, s32[8,128]{1,0:T(8,128)} %bitcast.15, s32[8,128]{1,0:T(8,128)} %bitcast.16, ...), custom_call_target="tpu_custom_call" | custom-call | tf_op jit(solution)/shard_map/prepare/pallas_call | solution.py:164
  2.9 3.0 %collective-permute-start.1 = (bf16[240,256]{1,0:T(8,128)(2,1)}, bf16[240,256]{1,0:T(8,128)(2,1)S(1)}, u32[]{:S(2)}, u32[]{:S(2)}) collective-permute-start(bf16[240,256]{1,0:T(8,128)(2,1)} %get-tuple-element.12), channel_id=1, source_target_pairs={{0,2},{1,3},{2,0},{3,1},{4,6},{5,7},{6,4},{7,5},{8,10},{9,11},{10,... | collective-permute-start | bytes 368648 | tf_op jit(solution)/shard_map/ppermute | solution.py:527
  6.0 1.5 %collective-permute-start.3 = (bf16[176,256]{1,0:T(8,128)(2,1)}, bf16[176,256]{1,0:T(8,128)(2,1)S(1)}, u32[]{:S(2)}, u32[]{:S(2)}) collective-permute-start(bf16[176,256]{1,0:T(8,128)(2,1)} %get-tuple-element.13), channel_id=1, source_target_pairs={{0,4},{1,5},{2,6},{3,7},{4,0},{5,1},{6,2},{7,3},{8,12},{9,13},{10,... | collective-permute-start | bytes 270344 | tf_op jit(solution)/shard_map/ppermute | solution.py:527
  7.4 0.0 collective-permute-start.5
  7.5 0.9 %copy-done = bf16[240,256]{1,0:T(8,128)(2,1)S(1)} copy-done((bf16[240,256]{1,0:T(8,128)(2,1)S(1)}, bf16[240,256]{1,0:T(8,128)(2,1)}, u32[]{:S(2)}) %copy-start) | copy-done | bytes 122904
  8.4 0.1 collective-permute-start
  8.5 1.0 %collective-permute-done.1.far_ref.refs_2_ = bf16[240,256]{1,0:T(8,128)(2,1)S(1)} collective-permute-done((bf16[240,256]{1,0:T(8,128)(2,1)}, bf16[240,256]{1,0:T(8,128)(2,1)S(1)}, u32[]{:S(2)}, u32[]{:S(2)}) %collective-permute-start.1) | collective-permute-done | bytes 122912 | tf_op jit(solution)/shard_map/ppermute | solution.py:527
  9.5 0.0 collective-permute-start.2
  9.5 1.9 %collective-permute-done.3.refs_4_ = bf16[176,256]{1,0:T(8,128)(2,1)S(1)} collective-permute-done((bf16[176,256]{1,0:T(8,128)(2,1)}, bf16[176,256]{1,0:T(8,128)(2,1)S(1)}, u32[]{:S(2)}, u32[]{:S(2)}) %collective-permute-start.3) | collective-permute-done | bytes 90144 | tf_op jit(solution)/shard_map/ppermute | solution.py:527
  11.4 1.7 %collective-permute-done.5.refs_6_ = bf16[176,256]{1,0:T(8,128)(2,1)S(1)} collective-permute-done((bf16[176,256]{1,0:T(8,128)(2,1)}, bf16[176,256]{1,0:T(8,128)(2,1)S(1)}, u32[]{:S(2)}, u32[]{:S(2)}) %collective-permute-start.5) | collective-permute-done | bytes 90144 | tf_op jit(solution)/shard_map/ppermute | solution.py:527
  13.1 0.0 collective-permute-start.6
  13.1 1.6 %collective-permute-start.7 = (bf16[4,64,128]{2,1,0:T(8,128)(2,1)S(1)}, bf16[4,64,128]{2,1,0:T(8,128)(2,1)S(1)}, u32[]{:S(2)}, u32[]{:S(2)}) collective-permute-start(bf16[4,64,128]{2,1,0:T(8,128)(2,1)S(1)} %stack.1.refs_8_), channel_id=1, source_target_pairs={{0,8},{8,16},{16,24},{24,0},{1,9},{9,17},{17,25},{25,1},{2,10},{10... | collective-permute-start | bytes 196616 | tf_op jit(solution)/shard_map/ppermute | solution.py:522
  14.7 2.2 %collective-permute-start.8 = (bf16[4,64,128]{2,1,0:T(8,128)(2,1)S(1)}, bf16[4,64,128]{2,1,0:T(8,128)(2,1)S(1)}, u32[]{:S(2)}, u32[]{:S(2)}) collective-permute-start(bf16[4,64,128]{2,1,0:T(8,128)(2,1)S(1)} %stack.1.refs_8_), channel_id=1, source_target_pairs={{0,24},{8,0},{16,8},{24,16},{1,25},{9,1},{17,9},{25,17},{2,26},{10... | collective-permute-start | bytes 196616 | tf_op jit(solution)/shard_map/ppermute | solution.py:522
  17.0 0.8 %collective-permute-start.9 = (bf16[4,64,128]{2,1,0:T(8,128)(2,1)S(1)}, bf16[4,64,128]{2,1,0:T(8,128)(2,1)S(1)}, u32[]{:S(2)}, u32[]{:S(2)}) collective-permute-start(bf16[4,64,128]{2,1,0:T(8,128)(2,1)S(1)} %stack.1.refs_8_), channel_id=1, source_target_pairs={{0,16},{8,24},{16,0},{24,8},{1,17},{9,25},{17,1},{25,9},{2,18},{10... | collective-permute-start | bytes 196616 | tf_op jit(solution)/shard_map/ppermute | solution.py:522
  17.8 0.0 collective-permute-done.4.refs_5_
  17.8 0.0 collective-permute-done.6.refs_7_
  17.8 2.5 %rims.1 = (f32[64,128]{1,0:T(8,128)S(1)}, f32[64,128]{1,0:T(8,128)S(1)}, bf16[256,2560]{1,0:T(8,128)(2,1)S(1)}, f32[256,128]{1,0:T(8,128)S(1)}) custom-call(bf16[240,256]{1,0:T(8,128)(2,1)S(1)} %settle.1.own_ref.refs_0_, bf16[240,256]{1,0:T(8,128)(2,1)S(1)} %collective-permute-done.near_ref.refs_1_, ...), custom_call_target="tpu_custom_call" | custom-call | flops 3000000000 | bytes 1000000 | tf_op jit(solution)/shard_map/rims/pallas_call | solution.py:370
  20.3 1.4 %collective-permute-start.10 = (f32[64,128]{1,0:T(8,128)S(1)}, f32[64,128]{1,0:T(8,128)S(1)}, u32[]{:S(2)}, u32[]{:S(2)}) collective-permute-start(f32[64,128]{1,0:T(8,128)S(1)} %get-tuple-element.17), channel_id=1, source_target_pairs={{0,24},{8,16},{16,8},{24,0},{1,25},{9,17},{17,9},{25,1},{2,26},{10... | collective-permute-start | bytes 98312 | tf_op jit(solution)/shard_map/ppermute | solution.py:557
  21.7 1.4 %collective-permute-start.11 = (f32[64,128]{1,0:T(8,128)S(1)}, f32[64,128]{1,0:T(8,128)S(1)}, u32[]{:S(2)}, u32[]{:S(2)}) collective-permute-start(f32[64,128]{1,0:T(8,128)S(1)} %get-tuple-element.18), channel_id=1, source_target_pairs={{0,8},{8,0},{16,24},{24,16},{1,9},{9,1},{17,25},{25,17},{2,10},{10... | collective-permute-start | bytes 98312 | tf_op jit(solution)/shard_map/ppermute | solution.py:558
  23.0 0.9 %core.1.core_ref = f32[256,128]{1,0:T(8,128)S(1)} custom-call(bf16[240,256]{1,0:T(8,128)(2,1)S(1)} %settle.1.own_ref.refs_0_, bf16[240,256]{1,0:T(8,128)(2,1)S(1)} %collective-permute-done.near_ref.refs_1_, bf16[240,256]{1,0:T(8,128)(2,1)S(1)} %collective-permute-done.1.far_ref.refs_2_, bf16[240,256]{1,0:T(8,128)(2,1)S(1)} %collective-permute-done.2.both_ref.refs_3_, ...), custom_call_target="tpu_custom_call" | custom-call | flops 1500000000 | bytes 1000000 | tf_op jit(solution)/shard_map/core/pallas_call | solution.py:409
  23.9 0.0 collective-permute-done.7.refs_9_
  23.9 1.0 %multiply.1 = (bf16[256,128]{1,0:T(8,128)(2,1)}, f32[8,128]{1,0:T(8,128)S(1)}) custom-call(bf16[240,256]{1,0:T(8,128)(2,1)S(1)} %settle.1.own_ref.refs_0_, bf16[240,256]{1,0:T(8,128)(2,1)S(1)} %collective-permute-done.near_ref.refs_1_, bf16[240,256]{1,0:T(8,128)(2,1)S(1)} %collective-permute-done.1.far_ref.refs_2_, ...), custom_call_target="tpu_custom_call" | custom-call | flops 500000000 | bytes 1000000 | tf_op jit(solution)/shard_map/multiply/pallas_call | solution.py:452
  24.9 1.1 %collective-permute-done.10.below_ref = f32[64,128]{1,0:T(8,128)S(1)} collective-permute-done((f32[64,128]{1,0:T(8,128)S(1)}, f32[64,128]{1,0:T(8,128)S(1)}, u32[]{:S(2)}, u32[]{:S(2)}) %collective-permute-start.10) | collective-permute-done | bytes 32800 | tf_op jit(solution)/shard_map/ppermute | solution.py:557
  26.0 0.7 %fold.1 = f32[256,128]{1,0:T(8,128)} custom-call(f32[256,128]{1,0:T(8,128)S(1)} %core.1.core_ref, f32[64,128]{1,0:T(8,128)S(1)} %collective-permute-done.10.below_ref, f32[64,128]{1,0:T(8,128)S(1)} %collective-permute-done.11.above_ref, f32[8,128]{1,0:T(8,128)S(1)} %get-tuple-element.19.after_ref), custom_call_target="tpu_custom_call" | custom-call | flops 1000000 | bytes 400000 | tf_op jit(solution)/shard_map/fold/pallas_call | solution.py:510
  (9 shorter events, 0.0 us)
Async XLA Ops:
  2.9 6.6 %collective-permute-start.1 = (bf16[240,256]{1,0:T(8,128)(2,1)}, bf16[240,256]{1,0:T(8,128)(2,1)S(1)}, u32[]{:S(2)}, u32[]{:S(2)}) collective-permute-start(bf16[240,256]{1,0:T(8,128)(2,1)} %get-tuple-element.12), channel_id=1, source_target_pairs={{0,2},{1,3},{2,0},{3,1},{4,6},{5,7},{6,4},{7,5},{8,10},{9,11},{10,... | collective-permute-start | bytes 368648 | tf_op jit(solution)/shard_map/ppermute | solution.py:527
  6.0 5.4 %collective-permute-start.3 = (bf16[176,256]{1,0:T(8,128)(2,1)}, bf16[176,256]{1,0:T(8,128)(2,1)S(1)}, u32[]{:S(2)}, u32[]{:S(2)}) collective-permute-start(bf16[176,256]{1,0:T(8,128)(2,1)} %get-tuple-element.13), channel_id=1, source_target_pairs={{0,4},{1,5},{2,6},{3,7},{4,0},{5,1},{6,2},{7,3},{8,12},{9,13},{10,... | collective-permute-start | bytes 270344 | tf_op jit(solution)/shard_map/ppermute | solution.py:527
  7.4 5.6 %collective-permute-start.5 = (bf16[176,256]{1,0:T(8,128)(2,1)}, bf16[176,256]{1,0:T(8,128)(2,1)S(1)}, u32[]{:S(2)}, u32[]{:S(2)}) collective-permute-start(bf16[176,256]{1,0:T(8,128)(2,1)} %get-tuple-element.13), channel_id=1, source_target_pairs={{0,6},{1,7},{2,4},{3,5},{4,2},{5,3},{6,0},{7,1},{8,14},{9,15},{10,... | collective-permute-start | bytes 270344 | tf_op jit(solution)/shard_map/ppermute | solution.py:527
  7.5 0.9 %copy-start = (bf16[240,256]{1,0:T(8,128)(2,1)S(1)}, bf16[240,256]{1,0:T(8,128)(2,1)}, u32[]{:S(2)}) copy-start(bf16[240,256]{1,0:T(8,128)(2,1)} %get-tuple-element.11.block_ref) | copy-start | bytes 368644
  8.4 4.7 %collective-permute-start = (bf16[240,256]{1,0:T(8,128)(2,1)S(1)}, bf16[240,256]{1,0:T(8,128)(2,1)S(1)}, u32[]{:S(2)}, u32[]{:S(2)}) collective-permute-start(bf16[240,256]{1,0:T(8,128)(2,1)S(1)} %settle.1.own_ref.refs_0_), channel_id=1, source_target_pairs={{0,1},{1,0},{2,3},{3,2},{4,5},{5,4},{6,7},{7,6},{8,9},{9,8},{10,11... | collective-permute-start | bytes 368648 | tf_op jit(solution)/shard_map/ppermute | solution.py:527
  9.5 3.6 %collective-permute-start.2 = (bf16[240,256]{1,0:T(8,128)(2,1)S(1)}, bf16[240,256]{1,0:T(8,128)(2,1)S(1)}, u32[]{:S(2)}, u32[]{:S(2)}) collective-permute-start(bf16[240,256]{1,0:T(8,128)(2,1)S(1)} %collective-permute-done.1.far_ref.refs_2_), channel_id=1, source_target_pairs={{0,1},{1,0},{2,3},{3,2},{4,5},{5,4},{6,7},{7,6},{8,9},{9,8},{10,11... | collective-permute-start | bytes 368648 | tf_op jit(solution)/shard_map/ppermute | solution.py:527
  11.4 6.4 %collective-permute-start.4 = (bf16[176,256]{1,0:T(8,128)(2,1)S(1)}, bf16[176,256]{1,0:T(8,128)(2,1)S(1)}, u32[]{:S(2)}, u32[]{:S(2)}) collective-permute-start(bf16[176,256]{1,0:T(8,128)(2,1)S(1)} %collective-permute-done.3.refs_4_), channel_id=1, source_target_pairs={{0,1},{1,0},{2,3},{3,2},{4,5},{5,4},{6,7},{7,6},{8,9},{9,8},{10,11... | collective-permute-start | bytes 270344 | tf_op jit(solution)/shard_map/ppermute | solution.py:527
  13.1 4.7 %collective-permute-start.6 = (bf16[176,256]{1,0:T(8,128)(2,1)S(1)}, bf16[176,256]{1,0:T(8,128)(2,1)S(1)}, u32[]{:S(2)}, u32[]{:S(2)}) collective-permute-start(bf16[176,256]{1,0:T(8,128)(2,1)S(1)} %collective-permute-done.5.refs_6_), channel_id=1, source_target_pairs={{0,1},{1,0},{2,3},{3,2},{4,5},{5,4},{6,7},{7,6},{8,9},{9,8},{10,11... | collective-permute-start | bytes 270344 | tf_op jit(solution)/shard_map/ppermute | solution.py:527
  13.1 10.8 %collective-permute-start.7 = (bf16[4,64,128]{2,1,0:T(8,128)(2,1)S(1)}, bf16[4,64,128]{2,1,0:T(8,128)(2,1)S(1)}, u32[]{:S(2)}, u32[]{:S(2)}) collective-permute-start(bf16[4,64,128]{2,1,0:T(8,128)(2,1)S(1)} %stack.1.refs_8_), channel_id=1, source_target_pairs={{0,8},{8,16},{16,24},{24,0},{1,9},{9,17},{17,25},{25,1},{2,10},{10... | collective-permute-start | bytes 196616 | tf_op jit(solution)/shard_map/ppermute | solution.py:522
  14.7 9.2 %collective-permute-start.8 = (bf16[4,64,128]{2,1,0:T(8,128)(2,1)S(1)}, bf16[4,64,128]{2,1,0:T(8,128)(2,1)S(1)}, u32[]{:S(2)}, u32[]{:S(2)}) collective-permute-start(bf16[4,64,128]{2,1,0:T(8,128)(2,1)S(1)} %stack.1.refs_8_), channel_id=1, source_target_pairs={{0,24},{8,0},{16,8},{24,16},{1,25},{9,1},{17,9},{25,17},{2,26},{10... | collective-permute-start | bytes 196616 | tf_op jit(solution)/shard_map/ppermute | solution.py:522
  17.0 6.9 %collective-permute-start.9 = (bf16[4,64,128]{2,1,0:T(8,128)(2,1)S(1)}, bf16[4,64,128]{2,1,0:T(8,128)(2,1)S(1)}, u32[]{:S(2)}, u32[]{:S(2)}) collective-permute-start(bf16[4,64,128]{2,1,0:T(8,128)(2,1)S(1)} %stack.1.refs_8_), channel_id=1, source_target_pairs={{0,16},{8,24},{16,0},{24,8},{1,17},{9,25},{17,1},{25,9},{2,18},{10... | collective-permute-start | bytes 196616 | tf_op jit(solution)/shard_map/ppermute | solution.py:522
  20.3 5.8 %collective-permute-start.10 = (f32[64,128]{1,0:T(8,128)S(1)}, f32[64,128]{1,0:T(8,128)S(1)}, u32[]{:S(2)}, u32[]{:S(2)}) collective-permute-start(f32[64,128]{1,0:T(8,128)S(1)} %get-tuple-element.17), channel_id=1, source_target_pairs={{0,24},{8,16},{16,8},{24,0},{1,25},{9,17},{17,9},{25,1},{2,26},{10... | collective-permute-start | bytes 98312 | tf_op jit(solution)/shard_map/ppermute | solution.py:557
  21.7 4.4 %collective-permute-start.11 = (f32[64,128]{1,0:T(8,128)S(1)}, f32[64,128]{1,0:T(8,128)S(1)}, u32[]{:S(2)}, u32[]{:S(2)}) collective-permute-start(f32[64,128]{1,0:T(8,128)S(1)} %get-tuple-element.18), channel_id=1, source_target_pairs={{0,8},{8,0},{16,24},{24,16},{1,9},{9,1},{17,25},{25,17},{2,10},{10... | collective-permute-start | bytes 98312 | tf_op jit(solution)/shard_map/ppermute | solution.py:558

commit v9 on v8

--- a/solution.py
+++ b/solution.py
@@ -418,10 +418,6 @@
     )(*arrays, depth, extra)
 
 
-def row_steps(num_row):
-    return [0, 1, num_row - 1] + list(range(2, num_row - 1))
-
-
 def product_kernel(num_row, num_col, num_layer, refs_in, *refs):
     blocks = Blocks(refs[:refs_in], num_col, num_layer)
     h_refs = refs[refs_in : refs_in + num_row]
@@ -430,9 +426,10 @@
     row = lax.axis_index("row")
     rows = h_refs[0].shape[1]
     for back in range(num_layer):
-        for spot, step in enumerate(row_steps(num_row)):
-            start = pl.multiple_of(lax.rem(row - step + num_row, num_row) * rows, rows)
-            slab[back, pl.ds(start, rows), :] = h_refs[spot][back]
+        for step in range(num_row):
+            source = (row ^ step) if num_row == 4 else lax.rem(row - step + num_row, num_row)
+            start = pl.multiple_of(source * rows, rows)
+            slab[back, pl.ds(start, rows), :] = h_refs[step][back]
     total = jnp.zeros(out_ref.shape, F32)
     for back in range(num_layer):
         for piece in range(num_col):
@@ -552,7 +549,11 @@
         mine = [pieces[0]] + [shifted(pieces[step], "layer", num_layer, step) for step in range(1, num_layer)]
         mine = jnp.stack(mine)
     low, high, depth, extra = rims(arrays, num_col, num_layer)
-    parts = [mine] + [shifted(mine, "row", num_row, step) for step in row_steps(num_row)[1:]]
+    if num_row == 4:
+        near, far = (lax.ppermute(mine, "row", [(i, i ^ step) for i in range(4)]) for step in (1, 2))
+        parts = [mine, near, far, lax.ppermute(far, "row", [(i, i ^ 1) for i in range(4)])]
+    else:
+        parts = [mine] + [shifted(mine, "row", num_row, step) for step in range(1, num_row)]
     if num_row == 4:
         below = lax.ppermute(low, "row", [(i, i ^ 3) for i in range(4)])
         above = lax.ppermute(high, "row", [(i, i ^ 1) for i in range(4)])

time: 26.9 us -> 27.7 us (1.030)
  waiting for transfers between devices: 5.71 us -> 6.99 us
  starting transfers between devices: 12.1 us -> 11.6 us
    ppermute x3, waiting for transfers between devices: 0.01 us -> 2.39 us  [the longest x1 2.38 us: on_device(): lax.ppermute(far, 'row', [(i, i ^ 1) for i in range(4)])]
    ppermute x3, starting transfers between devices: 4.67 us -> 5.98 us  [the longest x2 4.23 us: on_device(): lax.ppermute(mine, 'row', [(i, i ^ step) for i in range(4)])]
    ppermute x1, waiting for transfers between devices: 1.1 us -> 0.01 us  [on_device(): below = lax.ppermute(low, 'row', [(i, i ^ 3) for i in range(4)])]
    ppermute x1, starting transfers between devices: 1.35 us -> 0.28 us  [on_device(): above = lax.ppermute(high, 'row', [(i, i ^ 1) for i in range(4)])]
    ppermute x1, starting transfers between devices: 1.41 us -> 0.69 us  [on_device(): below = lax.ppermute(low, 'row', [(i, i ^ 3) for i in range(4)])]
where the time goes in v9:
time: 27.7 us; the launch traced here: 27.5 us
  starting transfers between devices  11.6 us (42%)
  Pallas kernels  7.3 us (26%)
  waiting for transfers between devices  6.99 us (25%)
  local copies, waits for them, and re-layouts  0.9 us (3%)
  between operations  0.69 us (2%)
    ppermute x7, starting transfers between devices, crossed(): return lax.ppermute(value, ('col', 'layer'), pairs)  4.65 us
    ppermute x7, waiting for transfers between devices, crossed(): return lax.ppermute(value, ('col', 'layer'), pairs)  4.6 us
    ppermute x2, starting transfers between devices, on_device(): lax.ppermute(mine, 'row', [(i, i ^ step) for i in range(4)])  4.23 us
    pallas_call x1, Pallas kernels, rims(): pl.pallas_call(functools.partial(rims_kernel, num_col, num_layer, len(arr...  2.45 us
    ppermute x1, waiting for transfers between devices, on_device(): lax.ppermute(far, 'row', [(i, i ^ 1) for i in range(4)])  2.38 us
    pallas_call x1, Pallas kernels, prepare(): pl.pallas_call(functools.partial(prepare_kernel, paired), out_shape=outs,...  2.28 us
    ppermute x1, starting transfers between devices, on_device(): lax.ppermute(far, 'row', [(i, i ^ 1) for i in range(4)])  1.74 us
    pallas_call x1, Pallas kernels, multiply(): pl.pallas_call(functools.partial(product_kernel, num_row, num_col, num_la...  0.98 us
  transfers between devices with their start and end apart: 12, of which 4 were waited for; matrix products, arithmetic and copies ran while one was open for 0% of the time, Pallas kernels for 16%

profile of v9, /device:TPU:0, one launch (start us, length us, event | category | flops | bytes accessed | tf_op | source)
XLA Modules:
  0.0 27.5 jit_solution(2387489458268882568)
XLA Ops:
  0.6 2.3 %prepare.1 = (bf16[176,256]{1,0:T(8,128)(2,1)}, bf16[240,256]{1,0:T(8,128)(2,1)}, bf16[240,256]{1,0:T(8,128)(2,1)}) custom-call(bf16[256,128]{1,0:T(8,128)(2,1)} %bitcast.13, s32[4,8]{1,0:T(4,128)} %bitcast.20, bf16[64,512]{1,0:T(8,128)(2,1)} %bitcast.14, s32[2,16]{1,0:T(2,128)} %bitcast.21, s32[8,128]{1,0:T(8,128)} %bitcast.15, s32[8,128]{1,0:T(8,128)} %bitcast.16, ...), custom_call_target="tpu_custom_call" | custom-call | tf_op jit(solution)/shard_map/prepare/pallas_call | solution.py:164
  2.9 3.0 %collective-permute-start.1 = (bf16[240,256]{1,0:T(8,128)(2,1)}, bf16[240,256]{1,0:T(8,128)(2,1)S(1)}, u32[]{:S(2)}, u32[]{:S(2)}) collective-permute-start(bf16[240,256]{1,0:T(8,128)(2,1)} %get-tuple-element.12), channel_id=1, source_target_pairs={{0,2},{1,3},{2,0},{3,1},{4,6},{5,7},{6,4},{7,5},{8,10},{9,11},{10,... | collective-permute-start | bytes 368648 | tf_op jit(solution)/shard_map/ppermute | solution.py:524
  6.0 1.5 %collective-permute-start.3 = (bf16[176,256]{1,0:T(8,128)(2,1)}, bf16[176,256]{1,0:T(8,128)(2,1)S(1)}, u32[]{:S(2)}, u32[]{:S(2)}) collective-permute-start(bf16[176,256]{1,0:T(8,128)(2,1)} %get-tuple-element.13), channel_id=1, source_target_pairs={{0,4},{1,5},{2,6},{3,7},{4,0},{5,1},{6,2},{7,3},{8,12},{9,13},{10,... | collective-permute-start | bytes 270344 | tf_op jit(solution)/shard_map/ppermute | solution.py:524
  7.4 0.0 collective-permute-start.5
  7.5 0.9 %copy-done = bf16[240,256]{1,0:T(8,128)(2,1)S(1)} copy-done((bf16[240,256]{1,0:T(8,128)(2,1)S(1)}, bf16[240,256]{1,0:T(8,128)(2,1)}, u32[]{:S(2)}) %copy-start) | copy-done | bytes 122904
  8.4 0.1 collective-permute-start
  8.5 1.0 %collective-permute-done.1.far_ref.refs_2_ = bf16[240,256]{1,0:T(8,128)(2,1)S(1)} collective-permute-done((bf16[240,256]{1,0:T(8,128)(2,1)}, bf16[240,256]{1,0:T(8,128)(2,1)S(1)}, u32[]{:S(2)}, u32[]{:S(2)}) %collective-permute-start.1) | collective-permute-done | bytes 122912 | tf_op jit(solution)/shard_map/ppermute | solution.py:524
  9.5 0.0 collective-permute-start.2
  9.5 1.9 %collective-permute-done.3.refs_4_ = bf16[176,256]{1,0:T(8,128)(2,1)S(1)} collective-permute-done((bf16[176,256]{1,0:T(8,128)(2,1)}, bf16[176,256]{1,0:T(8,128)(2,1)S(1)}, u32[]{:S(2)}, u32[]{:S(2)}) %collective-permute-start.3) | collective-permute-done | bytes 90144 | tf_op jit(solution)/shard_map/ppermute | solution.py:524
  11.4 0.0 collective-permute-start.4
  11.4 1.7 %collective-permute-done.5.refs_6_ = bf16[176,256]{1,0:T(8,128)(2,1)S(1)} collective-permute-done((bf16[176,256]{1,0:T(8,128)(2,1)}, bf16[176,256]{1,0:T(8,128)(2,1)S(1)}, u32[]{:S(2)}, u32[]{:S(2)}) %collective-permute-start.5) | collective-permute-done | bytes 90144 | tf_op jit(solution)/shard_map/ppermute | solution.py:524
  13.1 0.0 collective-permute-start.6
  13.1 0.0 collective-permute-done.near_ref.refs_1_
  13.1 0.0 collective-permute-done.2.both_ref.refs_3_
  13.1 2.7 %collective-permute-start.8 = (bf16[4,64,128]{2,1,0:T(8,128)(2,1)S(1)}, bf16[4,64,128]{2,1,0:T(8,128)(2,1)S(1)}, u32[]{:S(2)}, u32[]{:S(2)}) collective-permute-start(bf16[4,64,128]{2,1,0:T(8,128)(2,1)S(1)} %stack.1.refs_8_), channel_id=1, source_target_pairs={{0,16},{8,24},{16,0},{24,8},{1,17},{9,25},{17,1},{25,9},{2,18},{10... | collective-permute-start | bytes 196616 | tf_op jit(solution)/shard_map/ppermute | solution.py:553
  15.8 1.6 %collective-permute-start.7 = (bf16[4,64,128]{2,1,0:T(8,128)(2,1)S(1)}, bf16[4,64,128]{2,1,0:T(8,128)(2,1)S(1)}, u32[]{:S(2)}, u32[]{:S(2)}) collective-permute-start(bf16[4,64,128]{2,1,0:T(8,128)(2,1)S(1)} %stack.1.refs_8_), channel_id=1, source_target_pairs={{0,8},{8,0},{16,24},{24,16},{1,9},{9,1},{17,25},{25,17},{2,10},{10... | collective-permute-start | bytes 196616 | tf_op jit(solution)/shard_map/ppermute | solution.py:553
  17.4 2.5 %rims.1 = (f32[64,128]{1,0:T(8,128)S(1)}, f32[64,128]{1,0:T(8,128)S(1)}, bf16[256,2560]{1,0:T(8,128)(2,1)S(1)}, f32[256,128]{1,0:T(8,128)S(1)}) custom-call(bf16[240,256]{1,0:T(8,128)(2,1)S(1)} %settle.1.own_ref.refs_0_, bf16[240,256]{1,0:T(8,128)(2,1)S(1)} %collective-permute-done.near_ref.refs_1_, ...), custom_call_target="tpu_custom_call" | custom-call | flops 3000000000 | bytes 1000000 | tf_op jit(solution)/shard_map/rims/pallas_call | solution.py:370
  19.8 0.7 %collective-permute-start.10 = (f32[64,128]{1,0:T(8,128)S(1)}, f32[64,128]{1,0:T(8,128)S(1)}, u32[]{:S(2)}, u32[]{:S(2)}) collective-permute-start(f32[64,128]{1,0:T(8,128)S(1)} %get-tuple-element.17), channel_id=1, source_target_pairs={{0,24},{8,16},{16,8},{24,0},{1,25},{9,17},{17,9},{25,1},{2,26},{10... | collective-permute-start | bytes 98312 | tf_op jit(solution)/shard_map/ppermute | solution.py:558
  20.5 0.3 %collective-permute-start.11 = (f32[64,128]{1,0:T(8,128)S(1)}, f32[64,128]{1,0:T(8,128)S(1)}, u32[]{:S(2)}, u32[]{:S(2)}) collective-permute-start(f32[64,128]{1,0:T(8,128)S(1)} %get-tuple-element.18), channel_id=1, source_target_pairs={{0,8},{8,0},{16,24},{24,16},{1,9},{9,1},{17,25},{25,17},{2,10},{10... | collective-permute-start | bytes 98312 | tf_op jit(solution)/shard_map/ppermute | solution.py:559
  20.8 1.7 %collective-permute-start.9 = (bf16[4,64,128]{2,1,0:T(8,128)(2,1)S(1)}, bf16[4,64,128]{2,1,0:T(8,128)(2,1)S(1)}, u32[]{:S(2)}, u32[]{:S(2)}) collective-permute-start(bf16[4,64,128]{2,1,0:T(8,128)(2,1)S(1)} %collective-permute-done.8.refs_10_), channel_id=1, source_target_pairs={{0,8},{8,0},{16,24},{24,16},{1,9},{9,1},{17,25},{25,17},{2,10},{10... | collective-permute-start | bytes 196616 | tf_op jit(solution)/shard_map/ppermute | solution.py:554
  22.5 0.9 %core.1.core_ref = f32[256,128]{1,0:T(8,128)S(1)} custom-call(bf16[240,256]{1,0:T(8,128)(2,1)S(1)} %settle.1.own_ref.refs_0_, bf16[240,256]{1,0:T(8,128)(2,1)S(1)} %collective-permute-done.near_ref.refs_1_, bf16[240,256]{1,0:T(8,128)(2,1)S(1)} %collective-permute-done.1.far_ref.refs_2_, bf16[240,256]{1,0:T(8,128)(2,1)S(1)} %collective-permute-done.2.both_ref.refs_3_, ...), custom_call_target="tpu_custom_call" | custom-call | flops 1500000000 | bytes 1000000 | tf_op jit(solution)/shard_map/core/pallas_call | solution.py:409
  23.4 2.4 %collective-permute-done.9.refs_11_ = bf16[4,64,128]{2,1,0:T(8,128)(2,1)S(1)} collective-permute-done((bf16[4,64,128]{2,1,0:T(8,128)(2,1)S(1)}, bf16[4,64,128]{2,1,0:T(8,128)(2,1)S(1)}, u32[]{:S(2)}, u32[]{:S(2)}) %collective-permute-start.9) | collective-permute-done | bytes 65568 | tf_op jit(solution)/shard_map/ppermute | solution.py:554
  25.8 1.0 %multiply.1 = (bf16[256,128]{1,0:T(8,128)(2,1)}, f32[8,128]{1,0:T(8,128)S(1)}) custom-call(bf16[240,256]{1,0:T(8,128)(2,1)S(1)} %settle.1.own_ref.refs_0_, bf16[240,256]{1,0:T(8,128)(2,1)S(1)} %collective-permute-done.near_ref.refs_1_, bf16[240,256]{1,0:T(8,128)(2,1)S(1)} %collective-permute-done.1.far_ref.refs_2_, ...), custom_call_target="tpu_custom_call" | custom-call | flops 500000000 | bytes 1000000 | tf_op jit(solution)/shard_map/multiply/pallas_call | solution.py:449
  26.8 0.7 %fold.1 = f32[256,128]{1,0:T(8,128)} custom-call(f32[256,128]{1,0:T(8,128)S(1)} %core.1.core_ref, f32[64,128]{1,0:T(8,128)S(1)} %collective-permute-done.10.below_ref, f32[64,128]{1,0:T(8,128)S(1)} %collective-permute-done.11.above_ref, f32[8,128]{1,0:T(8,128)S(1)} %get-tuple-element.19.after_ref), custom_call_target="tpu_custom_call" | custom-call | flops 1000000 | bytes 400000 | tf_op jit(solution)/shard_map/fold/pallas_call | solution.py:507
  (9 shorter events, 0.0 us)
Async XLA Ops:
  2.9 6.6 %collective-permute-start.1 = (bf16[240,256]{1,0:T(8,128)(2,1)}, bf16[240,256]{1,0:T(8,128)(2,1)S(1)}, u32[]{:S(2)}, u32[]{:S(2)}) collective-permute-start(bf16[240,256]{1,0:T(8,128)(2,1)} %get-tuple-element.12), channel_id=1, source_target_pairs={{0,2},{1,3},{2,0},{3,1},{4,6},{5,7},{6,4},{7,5},{8,10},{9,11},{10,... | collective-permute-start | bytes 368648 | tf_op jit(solution)/shard_map/ppermute | solution.py:524
  6.0 5.4 %collective-permute-start.3 = (bf16[176,256]{1,0:T(8,128)(2,1)}, bf16[176,256]{1,0:T(8,128)(2,1)S(1)}, u32[]{:S(2)}, u32[]{:S(2)}) collective-permute-start(bf16[176,256]{1,0:T(8,128)(2,1)} %get-tuple-element.13), channel_id=1, source_target_pairs={{0,4},{1,5},{2,6},{3,7},{4,0},{5,1},{6,2},{7,3},{8,12},{9,13},{10,... | collective-permute-start | bytes 270344 | tf_op jit(solution)/shard_map/ppermute | solution.py:524
  7.4 5.6 %collective-permute-start.5 = (bf16[176,256]{1,0:T(8,128)(2,1)}, bf16[176,256]{1,0:T(8,128)(2,1)S(1)}, u32[]{:S(2)}, u32[]{:S(2)}) collective-permute-start(bf16[176,256]{1,0:T(8,128)(2,1)} %get-tuple-element.13), channel_id=1, source_target_pairs={{0,6},{1,7},{2,4},{3,5},{4,2},{5,3},{6,0},{7,1},{8,14},{9,15},{10,... | collective-permute-start | bytes 270344 | tf_op jit(solution)/shard_map/ppermute | solution.py:524
  7.5 0.9 %copy-start = (bf16[240,256]{1,0:T(8,128)(2,1)S(1)}, bf16[240,256]{1,0:T(8,128)(2,1)}, u32[]{:S(2)}) copy-start(bf16[240,256]{1,0:T(8,128)(2,1)} %get-tuple-element.11.block_ref) | copy-start | bytes 368644
  8.4 4.7 %collective-permute-start = (bf16[240,256]{1,0:T(8,128)(2,1)S(1)}, bf16[240,256]{1,0:T(8,128)(2,1)S(1)}, u32[]{:S(2)}, u32[]{:S(2)}) collective-permute-start(bf16[240,256]{1,0:T(8,128)(2,1)S(1)} %settle.1.own_ref.refs_0_), channel_id=1, source_target_pairs={{0,1},{1,0},{2,3},{3,2},{4,5},{5,4},{6,7},{7,6},{8,9},{9,8},{10,11... | collective-permute-start | bytes 368648 | tf_op jit(solution)/shard_map/ppermute | solution.py:524
  9.5 3.6 %collective-permute-start.2 = (bf16[240,256]{1,0:T(8,128)(2,1)S(1)}, bf16[240,256]{1,0:T(8,128)(2,1)S(1)}, u32[]{:S(2)}, u32[]{:S(2)}) collective-permute-start(bf16[240,256]{1,0:T(8,128)(2,1)S(1)} %collective-permute-done.1.far_ref.refs_2_), channel_id=1, source_target_pairs={{0,1},{1,0},{2,3},{3,2},{4,5},{5,4},{6,7},{7,6},{8,9},{9,8},{10,11... | collective-permute-start | bytes 368648 | tf_op jit(solution)/shard_map/ppermute | solution.py:524
  11.4 6.0 %collective-permute-start.4 = (bf16[176,256]{1,0:T(8,128)(2,1)S(1)}, bf16[176,256]{1,0:T(8,128)(2,1)S(1)}, u32[]{:S(2)}, u32[]{:S(2)}) collective-permute-start(bf16[176,256]{1,0:T(8,128)(2,1)S(1)} %collective-permute-done.3.refs_4_), channel_id=1, source_target_pairs={{0,1},{1,0},{2,3},{3,2},{4,5},{5,4},{6,7},{7,6},{8,9},{9,8},{10,11... | collective-permute-start | bytes 270344 | tf_op jit(solution)/shard_map/ppermute | solution.py:524
  13.1 4.3 %collective-permute-start.6 = (bf16[176,256]{1,0:T(8,128)(2,1)S(1)}, bf16[176,256]{1,0:T(8,128)(2,1)S(1)}, u32[]{:S(2)}, u32[]{:S(2)}) collective-permute-start(bf16[176,256]{1,0:T(8,128)(2,1)S(1)} %collective-permute-done.5.refs_6_), channel_id=1, source_target_pairs={{0,1},{1,0},{2,3},{3,2},{4,5},{5,4},{6,7},{7,6},{8,9},{9,8},{10,11... | collective-permute-start | bytes 270344 | tf_op jit(solution)/shard_map/ppermute | solution.py:524
  13.1 7.7 %collective-permute-start.8 = (bf16[4,64,128]{2,1,0:T(8,128)(2,1)S(1)}, bf16[4,64,128]{2,1,0:T(8,128)(2,1)S(1)}, u32[]{:S(2)}, u32[]{:S(2)}) collective-permute-start(bf16[4,64,128]{2,1,0:T(8,128)(2,1)S(1)} %stack.1.refs_8_), channel_id=1, source_target_pairs={{0,16},{8,24},{16,0},{24,8},{1,17},{9,25},{17,1},{25,9},{2,18},{10... | collective-permute-start | bytes 196616 | tf_op jit(solution)/shard_map/ppermute | solution.py:553
  15.8 7.7 %collective-permute-start.7 = (bf16[4,64,128]{2,1,0:T(8,128)(2,1)S(1)}, bf16[4,64,128]{2,1,0:T(8,128)(2,1)S(1)}, u32[]{:S(2)}, u32[]{:S(2)}) collective-permute-start(bf16[4,64,128]{2,1,0:T(8,128)(2,1)S(1)} %stack.1.refs_8_), channel_id=1, source_target_pairs={{0,8},{8,0},{16,24},{24,16},{1,9},{9,1},{17,25},{25,17},{2,10},{10... | collective-permute-start | bytes 196616 | tf_op jit(solution)/shard_map/ppermute | solution.py:553
  19.8 7.0 %collective-permute-start.10 = (f32[64,128]{1,0:T(8,128)S(1)}, f32[64,128]{1,0:T(8,128)S(1)}, u32[]{:S(2)}, u32[]{:S(2)}) collective-permute-start(f32[64,128]{1,0:T(8,128)S(1)} %get-tuple-element.17), channel_id=1, source_target_pairs={{0,24},{8,16},{16,8},{24,0},{1,25},{9,17},{17,9},{25,1},{2,26},{10... | collective-permute-start | bytes 98312 | tf_op jit(solution)/shard_map/ppermute | solution.py:558
  20.5 6.3 %collective-permute-start.11 = (f32[64,128]{1,0:T(8,128)S(1)}, f32[64,128]{1,0:T(8,128)S(1)}, u32[]{:S(2)}, u32[]{:S(2)}) collective-permute-start(f32[64,128]{1,0:T(8,128)S(1)} %get-tuple-element.18), channel_id=1, source_target_pairs={{0,8},{8,0},{16,24},{24,16},{1,9},{9,1},{17,25},{25,17},{2,10},{10... | collective-permute-start | bytes 98312 | tf_op jit(solution)/shard_map/ppermute | solution.py:559
  20.8 5.0 %collective-permute-start.9 = (bf16[4,64,128]{2,1,0:T(8,128)(2,1)S(1)}, bf16[4,64,128]{2,1,0:T(8,128)(2,1)S(1)}, u32[]{:S(2)}, u32[]{:S(2)}) collective-permute-start(bf16[4,64,128]{2,1,0:T(8,128)(2,1)S(1)} %collective-permute-done.8.refs_10_), channel_id=1, source_target_pairs={{0,8},{8,0},{16,24},{24,16},{1,9},{9,1},{17,25},{25,17},{2,10},{10... | collective-permute-start | bytes 196616 | tf_op jit(solution)/shard_map/ppermute | solution.py:554

commit v10 on v8

--- a/solution.py
+++ b/solution.py
@@ -431,7 +431,7 @@
     rows = h_refs[0].shape[1]
     for back in range(num_layer):
         for spot, step in enumerate(row_steps(num_row)):
-            start = pl.multiple_of(lax.rem(row - step + num_row, num_row) * rows, rows)
+            start = pl.multiple_of((row ^ step) * rows, rows)
             slab[back, pl.ds(start, rows), :] = h_refs[spot][back]
     total = jnp.zeros(out_ref.shape, F32)
     for back in range(num_layer):
@@ -552,7 +552,9 @@
         mine = [pieces[0]] + [shifted(pieces[step], "layer", num_layer, step) for step in range(1, num_layer)]
         mine = jnp.stack(mine)
     low, high, depth, extra = rims(arrays, num_col, num_layer)
-    parts = [mine] + [shifted(mine, "row", num_row, step) for step in row_steps(num_row)[1:]]
+    parts = [mine] + [
+        lax.ppermute(mine, "row", [(i, i ^ step) for i in range(num_row)]) for step in row_steps(num_row)[1:]
+    ]
     if num_row == 4:
         below = lax.ppermute(low, "row", [(i, i ^ 3) for i in range(4)])
         above = lax.ppermute(high, "row", [(i, i ^ 1) for i in range(4)])

time: 26.9 us -> 27.6 us (1.026)
  waiting for transfers between devices: 5.71 us -> 6.16 us
    ppermute x1, starting transfers between devices: 1.41 us -> 2.99 us  [on_device(): below = lax.ppermute(low, 'row', [(i, i ^ 3) for i in range(4)])]
    ppermute x1, waiting for transfers between devices: 0.01 us -> 1.12 us  [on_device(): above = lax.ppermute(high, 'row', [(i, i ^ 1) for i in range(4)])]
    ppermute x1, starting transfers between devices: 1.35 us -> 0.45 us  [on_device(): above = lax.ppermute(high, 'row', [(i, i ^ 1) for i in range(4)])]
    ppermute x1, waiting for transfers between devices: 1.1 us -> 0.43 us  [on_device(): below = lax.ppermute(low, 'row', [(i, i ^ 3) for i in range(4)])]
    ppermute x3, starting transfers between devices: 4.67 us -> 4.23 us  [on_device(): lax.ppermute(mine, 'row', [(i, i ^ step) for i in range(num_row)])]
  transfers between devices with their start and end apart: 12 -> 12, of which waited for: 4 -> 5; matrix products, arithmetic and copies ran while one was open for 0% -> 0% of each run, Pallas kernels for 16% -> 16%
where the time goes in v10:
time: 27.6 us; the launch traced here: 27.4 us
  starting transfers between devices  12.3 us (45%)
  Pallas kernels  7.3 us (26%)
  waiting for transfers between devices  6.16 us (22%)
  local copies, waits for them, and re-layouts  0.9 us (3%)
  between operations  0.71 us (3%)
    ppermute x7, starting transfers between devices, crossed(): return lax.ppermute(value, ('col', 'layer'), pairs)  4.65 us
    ppermute x7, waiting for transfers between devices, crossed(): return lax.ppermute(value, ('col', 'layer'), pairs)  4.6 us
    ppermute x3, starting transfers between devices, on_device(): lax.ppermute(mine, 'row', [(i, i ^ step) for i in range(num_row)])  4.23 us
    ppermute x1, starting transfers between devices, on_device(): below = lax.ppermute(low, 'row', [(i, i ^ 3) for i in range(4)])  2.99 us
    pallas_call x1, Pallas kernels, rims(): pl.pallas_call(functools.partial(rims_kernel, num_col, num_layer, len(arr...  2.45 us
    pallas_call x1, Pallas kernels, prepare(): pl.pallas_call(functools.partial(prepare_kernel, paired), out_shape=outs,...  2.28 us
    ppermute x1, waiting for transfers between devices, on_device(): above = lax.ppermute(high, 'row', [(i, i ^ 1) for i in range(4)])  1.12 us
    pallas_call x1, Pallas kernels, multiply(): pl.pallas_call(functools.partial(product_kernel, num_row, num_col, num_la...  0.98 us
  transfers between devices with their start and end apart: 12, of which 5 were waited for; matrix products, arithmetic and copies ran while one was open for 0% of the time, Pallas kernels for 16%

profile of v10, /device:TPU:0, one launch (start us, length us, event | category | flops | bytes accessed | tf_op | source)
XLA Modules:
  0.0 27.4 jit_solution(216674885996998962)
XLA Ops:
  0.6 2.3 %prepare.1 = (bf16[176,256]{1,0:T(8,128)(2,1)}, bf16[240,256]{1,0:T(8,128)(2,1)}, bf16[240,256]{1,0:T(8,128)(2,1)}) custom-call(bf16[256,128]{1,0:T(8,128)(2,1)} %bitcast.13, s32[4,8]{1,0:T(4,128)} %bitcast.20, bf16[64,512]{1,0:T(8,128)(2,1)} %bitcast.14, s32[2,16]{1,0:T(2,128)} %bitcast.21, s32[8,128]{1,0:T(8,128)} %bitcast.15, s32[8,128]{1,0:T(8,128)} %bitcast.16, ...), custom_call_target="tpu_custom_call" | custom-call | tf_op jit(solution)/shard_map/prepare/pallas_call | solution.py:164
  2.9 3.0 %collective-permute-start.1 = (bf16[240,256]{1,0:T(8,128)(2,1)}, bf16[240,256]{1,0:T(8,128)(2,1)S(1)}, u32[]{:S(2)}, u32[]{:S(2)}) collective-permute-start(bf16[240,256]{1,0:T(8,128)(2,1)} %get-tuple-element.12), channel_id=1, source_target_pairs={{0,2},{1,3},{2,0},{3,1},{4,6},{5,7},{6,4},{7,5},{8,10},{9,11},{10,... | collective-permute-start | bytes 368648 | tf_op jit(solution)/shard_map/ppermute | solution.py:527
  6.0 1.5 %collective-permute-start.3 = (bf16[176,256]{1,0:T(8,128)(2,1)}, bf16[176,256]{1,0:T(8,128)(2,1)S(1)}, u32[]{:S(2)}, u32[]{:S(2)}) collective-permute-start(bf16[176,256]{1,0:T(8,128)(2,1)} %get-tuple-element.13), channel_id=1, source_target_pairs={{0,4},{1,5},{2,6},{3,7},{4,0},{5,1},{6,2},{7,3},{8,12},{9,13},{10,... | collective-permute-start | bytes 270344 | tf_op jit(solution)/shard_map/ppermute | solution.py:527
  7.4 0.0 collective-permute-start.5
  7.5 0.9 %copy-done = bf16[240,256]{1,0:T(8,128)(2,1)S(1)} copy-done((bf16[240,256]{1,0:T(8,128)(2,1)S(1)}, bf16[240,256]{1,0:T(8,128)(2,1)}, u32[]{:S(2)}) %copy-start) | copy-done | bytes 122904
  8.4 0.1 collective-permute-start
  8.5 1.0 %collective-permute-done.1.far_ref.refs_2_ = bf16[240,256]{1,0:T(8,128)(2,1)S(1)} collective-permute-done((bf16[240,256]{1,0:T(8,128)(2,1)}, bf16[240,256]{1,0:T(8,128)(2,1)S(1)}, u32[]{:S(2)}, u32[]{:S(2)}) %collective-permute-start.1) | collective-permute-done | bytes 122912 | tf_op jit(solution)/shard_map/ppermute | solution.py:527
  9.5 0.0 collective-permute-start.2
  9.5 1.9 %collective-permute-done.3.refs_4_ = bf16[176,256]{1,0:T(8,128)(2,1)S(1)} collective-permute-done((bf16[176,256]{1,0:T(8,128)(2,1)}, bf16[176,256]{1,0:T(8,128)(2,1)S(1)}, u32[]{:S(2)}, u32[]{:S(2)}) %collective-permute-start.3) | collective-permute-done | bytes 90144 | tf_op jit(solution)/shard_map/ppermute | solution.py:527
  11.4 1.7 %collective-permute-done.5.refs_6_ = bf16[176,256]{1,0:T(8,128)(2,1)S(1)} collective-permute-done((bf16[176,256]{1,0:T(8,128)(2,1)}, bf16[176,256]{1,0:T(8,128)(2,1)S(1)}, u32[]{:S(2)}, u32[]{:S(2)}) %collective-permute-start.5) | collective-permute-done | bytes 90144 | tf_op jit(solution)/shard_map/ppermute | solution.py:527
  13.1 0.0 collective-permute-start.6
  13.1 0.0 collective-permute-done.near_ref.refs_1_
  13.1 1.6 %collective-permute-start.7 = (bf16[4,64,128]{2,1,0:T(8,128)(2,1)S(1)}, bf16[4,64,128]{2,1,0:T(8,128)(2,1)S(1)}, u32[]{:S(2)}, u32[]{:S(2)}) collective-permute-start(bf16[4,64,128]{2,1,0:T(8,128)(2,1)S(1)} %stack.1.refs_8_), channel_id=1, source_target_pairs={{0,8},{8,0},{16,24},{24,16},{1,9},{9,1},{17,25},{25,17},{2,10},{10... | collective-permute-start | bytes 196616 | tf_op jit(solution)/shard_map/ppermute | solution.py:556
  14.8 2.5 %collective-permute-start.8 = (bf16[4,64,128]{2,1,0:T(8,128)(2,1)S(1)}, bf16[4,64,128]{2,1,0:T(8,128)(2,1)S(1)}, u32[]{:S(2)}, u32[]{:S(2)}) collective-permute-start(bf16[4,64,128]{2,1,0:T(8,128)(2,1)S(1)} %stack.1.refs_8_), channel_id=1, source_target_pairs={{0,24},{8,16},{16,8},{24,0},{1,25},{9,17},{17,9},{25,1},{2,26},{10... | collective-permute-start | bytes 196616 | tf_op jit(solution)/shard_map/ppermute | solution.py:556
  17.2 0.1 collective-permute-start.9
  17.4 2.5 %rims.1 = (f32[64,128]{1,0:T(8,128)S(1)}, f32[64,128]{1,0:T(8,128)S(1)}, bf16[256,2560]{1,0:T(8,128)(2,1)S(1)}, f32[256,128]{1,0:T(8,128)S(1)}) custom-call(bf16[240,256]{1,0:T(8,128)(2,1)S(1)} %settle.1.own_ref.refs_0_, bf16[240,256]{1,0:T(8,128)(2,1)S(1)} %collective-permute-done.near_ref.refs_1_, ...), custom_call_target="tpu_custom_call" | custom-call | flops 3000000000 | bytes 1000000 | tf_op jit(solution)/shard_map/rims/pallas_call | solution.py:370
  19.8 3.0 %collective-permute-start.10 = (f32[64,128]{1,0:T(8,128)S(1)}, f32[64,128]{1,0:T(8,128)S(1)}, u32[]{:S(2)}, u32[]{:S(2)}) collective-permute-start(f32[64,128]{1,0:T(8,128)S(1)} %get-tuple-element.17), channel_id=1, source_target_pairs={{0,24},{8,16},{16,8},{24,0},{1,25},{9,17},{17,9},{25,1},{2,26},{10... | collective-permute-start | bytes 98312 | tf_op jit(solution)/shard_map/ppermute | solution.py:559
  22.8 0.5 %collective-permute-start.11 = (f32[64,128]{1,0:T(8,128)S(1)}, f32[64,128]{1,0:T(8,128)S(1)}, u32[]{:S(2)}, u32[]{:S(2)}) collective-permute-start(f32[64,128]{1,0:T(8,128)S(1)} %get-tuple-element.18), channel_id=1, source_target_pairs={{0,8},{8,0},{16,24},{24,16},{1,9},{9,1},{17,25},{25,17},{2,10},{10... | collective-permute-start | bytes 98312 | tf_op jit(solution)/shard_map/ppermute | solution.py:560
  23.3 0.9 %core.1.core_ref = f32[256,128]{1,0:T(8,128)S(1)} custom-call(bf16[240,256]{1,0:T(8,128)(2,1)S(1)} %settle.1.own_ref.refs_0_, bf16[240,256]{1,0:T(8,128)(2,1)S(1)} %collective-permute-done.near_ref.refs_1_, bf16[240,256]{1,0:T(8,128)(2,1)S(1)} %collective-permute-done.1.far_ref.refs_2_, bf16[240,256]{1,0:T(8,128)(2,1)S(1)} %collective-permute-done.2.both_ref.refs_3_, ...), custom_call_target="tpu_custom_call" | custom-call | flops 1500000000 | bytes 1000000 | tf_op jit(solution)/shard_map/core/pallas_call | solution.py:409
  24.2 0.0 collective-permute-done.7.refs_9_
  24.2 1.0 %multiply.1 = (bf16[256,128]{1,0:T(8,128)(2,1)}, f32[8,128]{1,0:T(8,128)S(1)}) custom-call(bf16[240,256]{1,0:T(8,128)(2,1)S(1)} %settle.1.own_ref.refs_0_, bf16[240,256]{1,0:T(8,128)(2,1)S(1)} %collective-permute-done.near_ref.refs_1_, bf16[240,256]{1,0:T(8,128)(2,1)S(1)} %collective-permute-done.1.far_ref.refs_2_, ...), custom_call_target="tpu_custom_call" | custom-call | flops 500000000 | bytes 1000000 | tf_op jit(solution)/shard_map/multiply/pallas_call | solution.py:452
  25.2 0.4 %collective-permute-done.10.below_ref = f32[64,128]{1,0:T(8,128)S(1)} collective-permute-done((f32[64,128]{1,0:T(8,128)S(1)}, f32[64,128]{1,0:T(8,128)S(1)}, u32[]{:S(2)}, u32[]{:S(2)}) %collective-permute-start.10) | collective-permute-done | bytes 32800 | tf_op jit(solution)/shard_map/ppermute | solution.py:559
  25.6 1.1 %collective-permute-done.11.above_ref = f32[64,128]{1,0:T(8,128)S(1)} collective-permute-done((f32[64,128]{1,0:T(8,128)S(1)}, f32[64,128]{1,0:T(8,128)S(1)}, u32[]{:S(2)}, u32[]{:S(2)}) %collective-permute-start.11) | collective-permute-done | bytes 32800 | tf_op jit(solution)/shard_map/ppermute | solution.py:560
  26.7 0.7 %fold.1 = f32[256,128]{1,0:T(8,128)} custom-call(f32[256,128]{1,0:T(8,128)S(1)} %core.1.core_ref, f32[64,128]{1,0:T(8,128)S(1)} %collective-permute-done.10.below_ref, f32[64,128]{1,0:T(8,128)S(1)} %collective-permute-done.11.above_ref, f32[8,128]{1,0:T(8,128)S(1)} %get-tuple-element.19.after_ref), custom_call_target="tpu_custom_call" | custom-call | flops 1000000 | bytes 400000 | tf_op jit(solution)/shard_map/fold/pallas_call | solution.py:510
  (9 shorter events, 0.0 us)
Async XLA Ops:
  2.9 6.6 %collective-permute-start.1 = (bf16[240,256]{1,0:T(8,128)(2,1)}, bf16[240,256]{1,0:T(8,128)(2,1)S(1)}, u32[]{:S(2)}, u32[]{:S(2)}) collective-permute-start(bf16[240,256]{1,0:T(8,128)(2,1)} %get-tuple-element.12), channel_id=1, source_target_pairs={{0,2},{1,3},{2,0},{3,1},{4,6},{5,7},{6,4},{7,5},{8,10},{9,11},{10,... | collective-permute-start | bytes 368648 | tf_op jit(solution)/shard_map/ppermute | solution.py:527
  6.0 5.4 %collective-permute-start.3 = (bf16[176,256]{1,0:T(8,128)(2,1)}, bf16[176,256]{1,0:T(8,128)(2,1)S(1)}, u32[]{:S(2)}, u32[]{:S(2)}) collective-permute-start(bf16[176,256]{1,0:T(8,128)(2,1)} %get-tuple-element.13), channel_id=1, source_target_pairs={{0,4},{1,5},{2,6},{3,7},{4,0},{5,1},{6,2},{7,3},{8,12},{9,13},{10,... | collective-permute-start | bytes 270344 | tf_op jit(solution)/shard_map/ppermute | solution.py:527
  7.4 5.6 %collective-permute-start.5 = (bf16[176,256]{1,0:T(8,128)(2,1)}, bf16[176,256]{1,0:T(8,128)(2,1)S(1)}, u32[]{:S(2)}, u32[]{:S(2)}) collective-permute-start(bf16[176,256]{1,0:T(8,128)(2,1)} %get-tuple-element.13), channel_id=1, source_target_pairs={{0,6},{1,7},{2,4},{3,5},{4,2},{5,3},{6,0},{7,1},{8,14},{9,15},{10,... | collective-permute-start | bytes 270344 | tf_op jit(solution)/shard_map/ppermute | solution.py:527
  7.5 0.9 %copy-start = (bf16[240,256]{1,0:T(8,128)(2,1)S(1)}, bf16[240,256]{1,0:T(8,128)(2,1)}, u32[]{:S(2)}) copy-start(bf16[240,256]{1,0:T(8,128)(2,1)} %get-tuple-element.11.block_ref) | copy-start | bytes 368644
  8.4 4.7 %collective-permute-start = (bf16[240,256]{1,0:T(8,128)(2,1)S(1)}, bf16[240,256]{1,0:T(8,128)(2,1)S(1)}, u32[]{:S(2)}, u32[]{:S(2)}) collective-permute-start(bf16[240,256]{1,0:T(8,128)(2,1)S(1)} %settle.1.own_ref.refs_0_), channel_id=1, source_target_pairs={{0,1},{1,0},{2,3},{3,2},{4,5},{5,4},{6,7},{7,6},{8,9},{9,8},{10,11... | collective-permute-start | bytes 368648 | tf_op jit(solution)/shard_map/ppermute | solution.py:527
  9.5 3.6 %collective-permute-start.2 = (bf16[240,256]{1,0:T(8,128)(2,1)S(1)}, bf16[240,256]{1,0:T(8,128)(2,1)S(1)}, u32[]{:S(2)}, u32[]{:S(2)}) collective-permute-start(bf16[240,256]{1,0:T(8,128)(2,1)S(1)} %collective-permute-done.1.far_ref.refs_2_), channel_id=1, source_target_pairs={{0,1},{1,0},{2,3},{3,2},{4,5},{5,4},{6,7},{7,6},{8,9},{9,8},{10,11... | collective-permute-start | bytes 368648 | tf_op jit(solution)/shard_map/ppermute | solution.py:527
  11.4 6.0 %collective-permute-start.4 = (bf16[176,256]{1,0:T(8,128)(2,1)S(1)}, bf16[176,256]{1,0:T(8,128)(2,1)S(1)}, u32[]{:S(2)}, u32[]{:S(2)}) collective-permute-start(bf16[176,256]{1,0:T(8,128)(2,1)S(1)} %collective-permute-done.3.refs_4_), channel_id=1, source_target_pairs={{0,1},{1,0},{2,3},{3,2},{4,5},{5,4},{6,7},{7,6},{8,9},{9,8},{10,11... | collective-permute-start | bytes 270344 | tf_op jit(solution)/shard_map/ppermute | solution.py:527
  13.1 4.3 %collective-permute-start.6 = (bf16[176,256]{1,0:T(8,128)(2,1)S(1)}, bf16[176,256]{1,0:T(8,128)(2,1)S(1)}, u32[]{:S(2)}, u32[]{:S(2)}) collective-permute-start(bf16[176,256]{1,0:T(8,128)(2,1)S(1)} %collective-permute-done.5.refs_6_), channel_id=1, source_target_pairs={{0,1},{1,0},{2,3},{3,2},{4,5},{5,4},{6,7},{7,6},{8,9},{9,8},{10,11... | collective-permute-start | bytes 270344 | tf_op jit(solution)/shard_map/ppermute | solution.py:527
  13.1 11.0 %collective-permute-start.7 = (bf16[4,64,128]{2,1,0:T(8,128)(2,1)S(1)}, bf16[4,64,128]{2,1,0:T(8,128)(2,1)S(1)}, u32[]{:S(2)}, u32[]{:S(2)}) collective-permute-start(bf16[4,64,128]{2,1,0:T(8,128)(2,1)S(1)} %stack.1.refs_8_), channel_id=1, source_target_pairs={{0,8},{8,0},{16,24},{24,16},{1,9},{9,1},{17,25},{25,17},{2,10},{10... | collective-permute-start | bytes 196616 | tf_op jit(solution)/shard_map/ppermute | solution.py:556
  14.8 9.4 %collective-permute-start.8 = (bf16[4,64,128]{2,1,0:T(8,128)(2,1)S(1)}, bf16[4,64,128]{2,1,0:T(8,128)(2,1)S(1)}, u32[]{:S(2)}, u32[]{:S(2)}) collective-permute-start(bf16[4,64,128]{2,1,0:T(8,128)(2,1)S(1)} %stack.1.refs_8_), channel_id=1, source_target_pairs={{0,24},{8,16},{16,8},{24,0},{1,25},{9,17},{17,9},{25,1},{2,26},{10... | collective-permute-start | bytes 196616 | tf_op jit(solution)/shard_map/ppermute | solution.py:556
  17.2 6.9 %collective-permute-start.9 = (bf16[4,64,128]{2,1,0:T(8,128)(2,1)S(1)}, bf16[4,64,128]{2,1,0:T(8,128)(2,1)S(1)}, u32[]{:S(2)}, u32[]{:S(2)}) collective-permute-start(bf16[4,64,128]{2,1,0:T(8,128)(2,1)S(1)} %stack.1.refs_8_), channel_id=1, source_target_pairs={{0,16},{8,24},{16,0},{24,8},{1,17},{9,25},{17,1},{25,9},{2,18},{10... | collective-permute-start | bytes 196616 | tf_op jit(solution)/shard_map/ppermute | solution.py:556
  19.8 5.8 %collective-permute-start.10 = (f32[64,128]{1,0:T(8,128)S(1)}, f32[64,128]{1,0:T(8,128)S(1)}, u32[]{:S(2)}, u32[]{:S(2)}) collective-permute-start(f32[64,128]{1,0:T(8,128)S(1)} %get-tuple-element.17), channel_id=1, source_target_pairs={{0,24},{8,16},{16,8},{24,0},{1,25},{9,17},{17,9},{25,1},{2,26},{10... | collective-permute-start | bytes 98312 | tf_op jit(solution)/shard_map/ppermute | solution.py:559
  22.8 3.9 %collective-permute-start.11 = (f32[64,128]{1,0:T(8,128)S(1)}, f32[64,128]{1,0:T(8,128)S(1)}, u32[]{:S(2)}, u32[]{:S(2)}) collective-permute-start(f32[64,128]{1,0:T(8,128)S(1)} %get-tuple-element.18), channel_id=1, source_target_pairs={{0,8},{8,0},{16,24},{24,16},{1,9},{9,1},{17,25},{25,17},{2,10},{10... | collective-permute-start | bytes 98312 | tf_op jit(solution)/shard_map/ppermute | solution.py:560

commit v11 on v7

--- a/solution.py
+++ b/solution.py
@@ -414,6 +414,10 @@
     )(*arrays, depth, extra)
 
 
+def row_steps(num_row):
+    return [0, 1, num_row - 1] + list(range(2, num_row - 1))
+
+
 def product_kernel(num_row, num_col, num_layer, refs_in, *refs):
     blocks = Blocks(refs[:refs_in], num_col, num_layer)
     h_refs = refs[refs_in : refs_in + num_row]
@@ -422,9 +426,9 @@
     row = lax.axis_index("row")
     rows = h_refs[0].shape[1]
     for back in range(num_layer):
-        for step in range(num_row):
-            start = pl.multiple_of((row ^ step) * rows, rows)
-            slab[back, pl.ds(start, rows), :] = h_refs[step][back]
+        for spot, step in enumerate(row_steps(num_row)):
+            start = pl.multiple_of(lax.rem(row - step + num_row, num_row) * rows, rows)
+            slab[back, pl.ds(start, rows), :] = h_refs[spot][back]
     total = jnp.zeros(out_ref.shape, F32)
     for back in range(num_layer):
         for piece in range(num_col):
@@ -542,9 +546,7 @@
         mine = [pieces[0]] + [shifted(pieces[step], "layer", num_layer, step) for step in range(1, num_layer)]
         mine = jnp.stack(mine)
     low, high, depth, extra = rims(arrays, num_col, num_layer)
-    parts = [mine] + [
-        lax.ppermute(mine, "row", [(i, i ^ step) for i in range(num_row)]) for step in range(1, num_row)
-    ]
+    parts = [mine] + [shifted(mine, "row", num_row, step) for step in row_steps(num_row)[1:]]
     below = shifted(high, "row", num_row, 1)
     above = shifted(low, "row", num_row, num_row - 1)
     core = core_part(arrays, depth, extra, num_col, num_layer)

time: 26.8 us -> 27 us (level)
    ppermute x2 -> x5, starting transfers between devices: 3.88 us -> 8.54 us  [shifted(): lax.ppermute(value, axis, [(i, (i + step) % count) for i in range(count)])]
    ppermute x3 -> x0, starting transfers between devices: 4.45 us -> none  [on_device(): lax.ppermute(mine, 'row', [(i, i ^ step) for i in range(num_row)])]
where the time goes in v11:
time: 27 us; the launch traced here: 26.8 us
  starting transfers between devices  13.2 us (49%)
  Pallas kernels  7.3 us (27%)
  waiting for transfers between devices  4.72 us (17%)
  local copies, waits for them, and re-layouts  0.9 us (3%)
  between operations  0.71 us (3%)
    ppermute x5, starting transfers between devices, shifted(): lax.ppermute(value, axis, [(i, (i + step) % count) for i in range(count)])  8.54 us
    ppermute x7, starting transfers between devices, crossed(): return lax.ppermute(value, ('col', 'layer'), pairs)  4.65 us
    ppermute x7, waiting for transfers between devices, crossed(): return lax.ppermute(value, ('col', 'layer'), pairs)  4.6 us
    pallas_call x1, Pallas kernels, rims(): pl.pallas_call(functools.partial(rims_kernel, num_col, num_layer, len(arr...  2.45 us
    pallas_call x1, Pallas kernels, prepare(): pl.pallas_call(functools.partial(prepare_kernel, paired), out_shape=outs,...  2.28 us
    pallas_call x1, Pallas kernels, multiply(): pl.pallas_call(functools.partial(product_kernel, num_row, num_col, num_la...  0.98 us
    unnamed x2, local copies, waits for them, and re-layouts  0.9 us
    pallas_call x1, Pallas kernels, core_part(): pl.pallas_call(functools.partial(core_kernel, num_col, num_layer, len(arr...  0.89 us
  transfers between devices with their start and end apart: 12, of which 4 were waited for; matrix products, arithmetic and copies ran while one was open for 0% of the time, Pallas kernels for 16%

profile of v11, /device:TPU:0, one launch (start us, length us, event | category | flops | bytes accessed | tf_op | source)
XLA Modules:
  0.0 26.8 jit_solution(2290019553147971052)
XLA Ops:
  0.6 2.3 %prepare.1 = (bf16[176,256]{1,0:T(8,128)(2,1)}, bf16[240,256]{1,0:T(8,128)(2,1)}, bf16[240,256]{1,0:T(8,128)(2,1)}) custom-call(bf16[256,128]{1,0:T(8,128)(2,1)} %bitcast.13, s32[4,8]{1,0:T(4,128)} %bitcast.20, bf16[64,512]{1,0:T(8,128)(2,1)} %bitcast.14, s32[2,16]{1,0:T(2,128)} %bitcast.21, s32[8,128]{1,0:T(8,128)} %bitcast.15, s32[8,128]{1,0:T(8,128)} %bitcast.16, ...), custom_call_target="tpu_custom_call" | custom-call | tf_op jit(solution)/shard_map/prepare/pallas_call | solution.py:164
  2.9 3.0 %collective-permute-start.1 = (bf16[240,256]{1,0:T(8,128)(2,1)}, bf16[240,256]{1,0:T(8,128)(2,1)S(1)}, u32[]{:S(2)}, u32[]{:S(2)}) collective-permute-start(bf16[240,256]{1,0:T(8,128)(2,1)} %get-tuple-element.12), channel_id=1, source_target_pairs={{0,2},{1,3},{2,0},{3,1},{4,6},{5,7},{6,4},{7,5},{8,10},{9,11},{10,... | collective-permute-start | bytes 368648 | tf_op jit(solution)/shard_map/ppermute | solution.py:521
  6.0 1.5 %collective-permute-start.3 = (bf16[176,256]{1,0:T(8,128)(2,1)}, bf16[176,256]{1,0:T(8,128)(2,1)S(1)}, u32[]{:S(2)}, u32[]{:S(2)}) collective-permute-start(bf16[176,256]{1,0:T(8,128)(2,1)} %get-tuple-element.13), channel_id=1, source_target_pairs={{0,4},{1,5},{2,6},{3,7},{4,0},{5,1},{6,2},{7,3},{8,12},{9,13},{10,... | collective-permute-start | bytes 270344 | tf_op jit(solution)/shard_map/ppermute | solution.py:521
  7.4 0.0 collective-permute-start.5
  7.5 0.9 %copy-done = bf16[240,256]{1,0:T(8,128)(2,1)S(1)} copy-done((bf16[240,256]{1,0:T(8,128)(2,1)S(1)}, bf16[240,256]{1,0:T(8,128)(2,1)}, u32[]{:S(2)}) %copy-start) | copy-done | bytes 122904
  8.4 0.1 collective-permute-start
  8.5 1.0 %collective-permute-done.1.far_ref.refs_2_ = bf16[240,256]{1,0:T(8,128)(2,1)S(1)} collective-permute-done((bf16[240,256]{1,0:T(8,128)(2,1)}, bf16[240,256]{1,0:T(8,128)(2,1)S(1)}, u32[]{:S(2)}, u32[]{:S(2)}) %collective-permute-start.1) | collective-permute-done | bytes 122912 | tf_op jit(solution)/shard_map/ppermute | solution.py:521
  9.5 0.0 collective-permute-start.2
  9.5 1.9 %collective-permute-done.3.refs_4_ = bf16[176,256]{1,0:T(8,128)(2,1)S(1)} collective-permute-done((bf16[176,256]{1,0:T(8,128)(2,1)}, bf16[176,256]{1,0:T(8,128)(2,1)S(1)}, u32[]{:S(2)}, u32[]{:S(2)}) %collective-permute-start.3) | collective-permute-done | bytes 90144 | tf_op jit(solution)/shard_map/ppermute | solution.py:521
  11.4 0.0 collective-permute-start.4
  11.4 1.7 %collective-permute-done.5.refs_6_ = bf16[176,256]{1,0:T(8,128)(2,1)S(1)} collective-permute-done((bf16[176,256]{1,0:T(8,128)(2,1)}, bf16[176,256]{1,0:T(8,128)(2,1)S(1)}, u32[]{:S(2)}, u32[]{:S(2)}) %collective-permute-start.5) | collective-permute-done | bytes 90144 | tf_op jit(solution)/shard_map/ppermute | solution.py:521
  13.1 0.0 collective-permute-start.6
  13.1 0.0 collective-permute-done.near_ref.refs_1_
  13.1 1.6 %collective-permute-start.7 = (bf16[4,64,128]{2,1,0:T(8,128)(2,1)S(1)}, bf16[4,64,128]{2,1,0:T(8,128)(2,1)S(1)}, u32[]{:S(2)}, u32[]{:S(2)}) collective-permute-start(bf16[4,64,128]{2,1,0:T(8,128)(2,1)S(1)} %stack.1.refs_8_), channel_id=1, source_target_pairs={{0,8},{8,16},{16,24},{24,0},{1,9},{9,17},{17,25},{25,1},{2,10},{10... | collective-permute-start | bytes 196616 | tf_op jit(solution)/shard_map/ppermute | solution.py:516
  14.7 2.2 %collective-permute-start.8 = (bf16[4,64,128]{2,1,0:T(8,128)(2,1)S(1)}, bf16[4,64,128]{2,1,0:T(8,128)(2,1)S(1)}, u32[]{:S(2)}, u32[]{:S(2)}) collective-permute-start(bf16[4,64,128]{2,1,0:T(8,128)(2,1)S(1)} %stack.1.refs_8_), channel_id=1, source_target_pairs={{0,24},{8,0},{16,8},{24,16},{1,25},{9,1},{17,9},{25,17},{2,26},{10... | collective-permute-start | bytes 196616 | tf_op jit(solution)/shard_map/ppermute | solution.py:516
  17.0 0.8 %collective-permute-start.9 = (bf16[4,64,128]{2,1,0:T(8,128)(2,1)S(1)}, bf16[4,64,128]{2,1,0:T(8,128)(2,1)S(1)}, u32[]{:S(2)}, u32[]{:S(2)}) collective-permute-start(bf16[4,64,128]{2,1,0:T(8,128)(2,1)S(1)} %stack.1.refs_8_), channel_id=1, source_target_pairs={{0,16},{8,24},{16,0},{24,8},{1,17},{9,25},{17,1},{25,9},{2,18},{10... | collective-permute-start | bytes 196616 | tf_op jit(solution)/shard_map/ppermute | solution.py:516
  17.8 2.5 %rims.1 = (f32[64,128]{1,0:T(8,128)S(1)}, f32[64,128]{1,0:T(8,128)S(1)}, bf16[256,2560]{1,0:T(8,128)(2,1)S(1)}, f32[256,128]{1,0:T(8,128)S(1)}) custom-call(bf16[240,256]{1,0:T(8,128)(2,1)S(1)} %settle.1.own_ref.refs_0_, bf16[240,256]{1,0:T(8,128)(2,1)S(1)} %collective-permute-done.near_ref.refs_1_, ...), custom_call_target="tpu_custom_call" | custom-call | flops 3000000000 | bytes 1000000 | tf_op jit(solution)/shard_map/rims/pallas_call | solution.py:366
  20.3 1.6 %collective-permute-start.10 = (f32[64,128]{1,0:T(8,128)S(1)}, f32[64,128]{1,0:T(8,128)S(1)}, u32[]{:S(2)}, u32[]{:S(2)}) collective-permute-start(f32[64,128]{1,0:T(8,128)S(1)} %get-tuple-element.17), channel_id=1, source_target_pairs={{0,8},{8,16},{16,24},{24,0},{1,9},{9,17},{17,25},{25,1},{2,10},{10... | collective-permute-start | bytes 98312 | tf_op jit(solution)/shard_map/ppermute | solution.py:516
  21.9 2.2 %collective-permute-start.11 = (f32[64,128]{1,0:T(8,128)S(1)}, f32[64,128]{1,0:T(8,128)S(1)}, u32[]{:S(2)}, u32[]{:S(2)}) collective-permute-start(f32[64,128]{1,0:T(8,128)S(1)} %get-tuple-element.18), channel_id=1, source_target_pairs={{0,24},{8,0},{16,8},{24,16},{1,25},{9,1},{17,9},{25,17},{2,26},{10... | collective-permute-start | bytes 98312 | tf_op jit(solution)/shard_map/ppermute | solution.py:516
  24.1 0.9 %core.1.core_ref = f32[256,128]{1,0:T(8,128)S(1)} custom-call(bf16[240,256]{1,0:T(8,128)(2,1)S(1)} %settle.1.own_ref.refs_0_, bf16[240,256]{1,0:T(8,128)(2,1)S(1)} %collective-permute-done.near_ref.refs_1_, bf16[240,256]{1,0:T(8,128)(2,1)S(1)} %collective-permute-done.1.far_ref.refs_2_, bf16[240,256]{1,0:T(8,128)(2,1)S(1)} %collective-permute-done.2.both_ref.refs_3_, ...), custom_call_target="tpu_custom_call" | custom-call | flops 1500000000 | bytes 1000000 | tf_op jit(solution)/shard_map/core/pallas_call | solution.py:405
  25.1 1.0 %multiply.1 = (bf16[256,128]{1,0:T(8,128)(2,1)}, f32[8,128]{1,0:T(8,128)S(1)}) custom-call(bf16[240,256]{1,0:T(8,128)(2,1)S(1)} %settle.1.own_ref.refs_0_, bf16[240,256]{1,0:T(8,128)(2,1)S(1)} %collective-permute-done.near_ref.refs_1_, bf16[240,256]{1,0:T(8,128)(2,1)S(1)} %collective-permute-done.1.far_ref.refs_2_, ...), custom_call_target="tpu_custom_call" | custom-call | flops 500000000 | bytes 1000000 | tf_op jit(solution)/shard_map/multiply/pallas_call | solution.py:448
  26.0 0.1 collective-permute-done.10.below_ref
  26.1 0.0 collective-permute-done.11.above_ref
  26.2 0.7 %fold.1 = f32[256,128]{1,0:T(8,128)} custom-call(f32[256,128]{1,0:T(8,128)S(1)} %core.1.core_ref, f32[64,128]{1,0:T(8,128)S(1)} %collective-permute-done.10.below_ref, f32[64,128]{1,0:T(8,128)S(1)} %collective-permute-done.11.above_ref, f32[8,128]{1,0:T(8,128)S(1)} %get-tuple-element.19.after_ref), custom_call_target="tpu_custom_call" | custom-call | flops 1000000 | bytes 400000 | tf_op jit(solution)/shard_map/fold/pallas_call | solution.py:504
  (9 shorter events, 0.0 us)
Async XLA Ops:
  2.9 6.6 %collective-permute-start.1 = (bf16[240,256]{1,0:T(8,128)(2,1)}, bf16[240,256]{1,0:T(8,128)(2,1)S(1)}, u32[]{:S(2)}, u32[]{:S(2)}) collective-permute-start(bf16[240,256]{1,0:T(8,128)(2,1)} %get-tuple-element.12), channel_id=1, source_target_pairs={{0,2},{1,3},{2,0},{3,1},{4,6},{5,7},{6,4},{7,5},{8,10},{9,11},{10,... | collective-permute-start | bytes 368648 | tf_op jit(solution)/shard_map/ppermute | solution.py:521
  6.0 5.4 %collective-permute-start.3 = (bf16[176,256]{1,0:T(8,128)(2,1)}, bf16[176,256]{1,0:T(8,128)(2,1)S(1)}, u32[]{:S(2)}, u32[]{:S(2)}) collective-permute-start(bf16[176,256]{1,0:T(8,128)(2,1)} %get-tuple-element.13), channel_id=1, source_target_pairs={{0,4},{1,5},{2,6},{3,7},{4,0},{5,1},{6,2},{7,3},{8,12},{9,13},{10,... | collective-permute-start | bytes 270344 | tf_op jit(solution)/shard_map/ppermute | solution.py:521
  7.4 5.6 %collective-permute-start.5 = (bf16[176,256]{1,0:T(8,128)(2,1)}, bf16[176,256]{1,0:T(8,128)(2,1)S(1)}, u32[]{:S(2)}, u32[]{:S(2)}) collective-permute-start(bf16[176,256]{1,0:T(8,128)(2,1)} %get-tuple-element.13), channel_id=1, source_target_pairs={{0,6},{1,7},{2,4},{3,5},{4,2},{5,3},{6,0},{7,1},{8,14},{9,15},{10,... | collective-permute-start | bytes 270344 | tf_op jit(solution)/shard_map/ppermute | solution.py:521
  7.5 0.9 %copy-start = (bf16[240,256]{1,0:T(8,128)(2,1)S(1)}, bf16[240,256]{1,0:T(8,128)(2,1)}, u32[]{:S(2)}) copy-start(bf16[240,256]{1,0:T(8,128)(2,1)} %get-tuple-element.11.block_ref) | copy-start | bytes 368644
  8.4 4.7 %collective-permute-start = (bf16[240,256]{1,0:T(8,128)(2,1)S(1)}, bf16[240,256]{1,0:T(8,128)(2,1)S(1)}, u32[]{:S(2)}, u32[]{:S(2)}) collective-permute-start(bf16[240,256]{1,0:T(8,128)(2,1)S(1)} %settle.1.own_ref.refs_0_), channel_id=1, source_target_pairs={{0,1},{1,0},{2,3},{3,2},{4,5},{5,4},{6,7},{7,6},{8,9},{9,8},{10,11... | collective-permute-start | bytes 368648 | tf_op jit(solution)/shard_map/ppermute | solution.py:521
  9.5 3.6 %collective-permute-start.2 = (bf16[240,256]{1,0:T(8,128)(2,1)S(1)}, bf16[240,256]{1,0:T(8,128)(2,1)S(1)}, u32[]{:S(2)}, u32[]{:S(2)}) collective-permute-start(bf16[240,256]{1,0:T(8,128)(2,1)S(1)} %collective-permute-done.1.far_ref.refs_2_), channel_id=1, source_target_pairs={{0,1},{1,0},{2,3},{3,2},{4,5},{5,4},{6,7},{7,6},{8,9},{9,8},{10,11... | collective-permute-start | bytes 368648 | tf_op jit(solution)/shard_map/ppermute | solution.py:521
  11.4 6.4 %collective-permute-start.4 = (bf16[176,256]{1,0:T(8,128)(2,1)S(1)}, bf16[176,256]{1,0:T(8,128)(2,1)S(1)}, u32[]{:S(2)}, u32[]{:S(2)}) collective-permute-start(bf16[176,256]{1,0:T(8,128)(2,1)S(1)} %collective-permute-done.3.refs_4_), channel_id=1, source_target_pairs={{0,1},{1,0},{2,3},{3,2},{4,5},{5,4},{6,7},{7,6},{8,9},{9,8},{10,11... | collective-permute-start | bytes 270344 | tf_op jit(solution)/shard_map/ppermute | solution.py:521
  13.1 4.7 %collective-permute-start.6 = (bf16[176,256]{1,0:T(8,128)(2,1)S(1)}, bf16[176,256]{1,0:T(8,128)(2,1)S(1)}, u32[]{:S(2)}, u32[]{:S(2)}) collective-permute-start(bf16[176,256]{1,0:T(8,128)(2,1)S(1)} %collective-permute-done.5.refs_6_), channel_id=1, source_target_pairs={{0,1},{1,0},{2,3},{3,2},{4,5},{5,4},{6,7},{7,6},{8,9},{9,8},{10,11... | collective-permute-start | bytes 270344 | tf_op jit(solution)/shard_map/ppermute | solution.py:521
  13.1 11.9 %collective-permute-start.7 = (bf16[4,64,128]{2,1,0:T(8,128)(2,1)S(1)}, bf16[4,64,128]{2,1,0:T(8,128)(2,1)S(1)}, u32[]{:S(2)}, u32[]{:S(2)}) collective-permute-start(bf16[4,64,128]{2,1,0:T(8,128)(2,1)S(1)} %stack.1.refs_8_), channel_id=1, source_target_pairs={{0,8},{8,16},{16,24},{24,0},{1,9},{9,17},{17,25},{25,1},{2,10},{10... | collective-permute-start | bytes 196616 | tf_op jit(solution)/shard_map/ppermute | solution.py:516
  14.7 10.3 %collective-permute-start.8 = (bf16[4,64,128]{2,1,0:T(8,128)(2,1)S(1)}, bf16[4,64,128]{2,1,0:T(8,128)(2,1)S(1)}, u32[]{:S(2)}, u32[]{:S(2)}) collective-permute-start(bf16[4,64,128]{2,1,0:T(8,128)(2,1)S(1)} %stack.1.refs_8_), channel_id=1, source_target_pairs={{0,24},{8,0},{16,8},{24,16},{1,25},{9,1},{17,9},{25,17},{2,26},{10... | collective-permute-start | bytes 196616 | tf_op jit(solution)/shard_map/ppermute | solution.py:516
  17.0 8.1 %collective-permute-start.9 = (bf16[4,64,128]{2,1,0:T(8,128)(2,1)S(1)}, bf16[4,64,128]{2,1,0:T(8,128)(2,1)S(1)}, u32[]{:S(2)}, u32[]{:S(2)}) collective-permute-start(bf16[4,64,128]{2,1,0:T(8,128)(2,1)S(1)} %stack.1.refs_8_), channel_id=1, source_target_pairs={{0,16},{8,24},{16,0},{24,8},{1,17},{9,25},{17,1},{25,9},{2,18},{10... | collective-permute-start | bytes 196616 | tf_op jit(solution)/shard_map/ppermute | solution.py:516
  20.3 5.9 %collective-permute-start.10 = (f32[64,128]{1,0:T(8,128)S(1)}, f32[64,128]{1,0:T(8,128)S(1)}, u32[]{:S(2)}, u32[]{:S(2)}) collective-permute-start(f32[64,128]{1,0:T(8,128)S(1)} %get-tuple-element.17), channel_id=1, source_target_pairs={{0,8},{8,16},{16,24},{24,0},{1,9},{9,17},{17,25},{25,1},{2,10},{10... | collective-permute-start | bytes 98312 | tf_op jit(solution)/shard_map/ppermute | solution.py:516
  21.9 4.3 %collective-permute-start.11 = (f32[64,128]{1,0:T(8,128)S(1)}, f32[64,128]{1,0:T(8,128)S(1)}, u32[]{:S(2)}, u32[]{:S(2)}) collective-permute-start(f32[64,128]{1,0:T(8,128)S(1)} %get-tuple-element.18), channel_id=1, source_target_pairs={{0,24},{8,0},{16,8},{24,16},{1,25},{9,1},{17,9},{25,17},{2,26},{10... | collective-permute-start | bytes 98312 | tf_op jit(solution)/shard_map/ppermute | solution.py:516
